TPU v7x, 128 devices: a whole 4x4x4 slice. The times are simulated.
128 devices in a mesh: ctx: 16 (over y_hi, x, core), grp: 8 (over y_lo, z).
Axes of the slice: x: 4, y: 4 (y_hi: 2, y_lo: 2; y = y_hi * 2 + y_lo), z: 4, core: 2. Of those that a mesh axis runs over, the one named last changes fastest.
Arguments:
- residual: bfloat16 [4096, 4096], P('ctx', 'grp'), may hold values from -48 to 48
- queries: bfloat16 [4096, 4096], P('ctx', 'grp'), may hold values from -200 to 200
- keys: bfloat16 [4096, 4096], P('ctx', 'grp'), may hold values from -6 to 6
- values: bfloat16 [4096, 4096], P('ctx', 'grp'), may hold values from -6 to 6
- frame_lengths: int32 [16], replicated, may hold values from 1 to 512, 4096 in all
- routes: int32 [4096, 2], P('ctx'), may hold values from 0 to 31, all different within a row; in each aligned block of 256 rows (0 to 255, 256 to 511, ...) at most 48 rows name the same one
- route_gates: float32 [4096, 2], P('ctx'), may hold values from 0.2 to 1
- w_in: bfloat16 [32, 4096, 1536], P('ctx', 'grp'), may hold values from -0.09375 to 0.09375
- w_out: bfloat16 [32, 1536, 4096], P('ctx', None, 'grp'), may hold values from -0.15625 to 0.15625
- out_grad: bfloat16 [4096, 4096], P('ctx', 'grp'), may hold values from -6 to 6
Outputs:
- layer_out: bfloat16 [4096, 4096], P('ctx', 'grp')
- input_grad: bfloat16 [4096, 4096], P('ctx', 'grp')
- query_grad: bfloat16 [4096, 4096], P('ctx', 'grp')
- key_grad: bfloat16 [4096, 4096], P('ctx', 'grp')
- value_grad: bfloat16 [4096, 4096], P('ctx', 'grp')
- w_in_grad: bfloat16 [32, 4096, 1536], P('ctx', 'grp')
- w_out_grad: bfloat16 [32, 1536, 4096], P('ctx', None, 'grp')
Inputs may be any that keep to these rules, and one draw needn't show every extreme that they name: `routes`: in every aligned block of 256 rows no expert is named more than 48 times, and in every draw some expert is named exactly 48 times in some block. The two experts of a row differ. `frame_lengths`: the 16 lengths sum to 4096 and the longest is exactly 512.
All inputs are finite; a program needn't handle non-finite values.
Results may differ from a plain program's by a relative error of at most 0.035.
Values may be sent and summed in bfloat16 or wider, within the bound.
A program may use at most 192 MiB of HBM per device.

v0:
```python
import jax
import jax.numpy as jnp
from jax import lax
from jax.sharding import PartitionSpec as P

HEAD_DIM = 128


gelu_coef = 0.7978845608028654


def gelu_tanh(field):
    return 0.5 * field * (1.0 + jnp.tanh(gelu_coef * (field + 0.044715 * field * field * field)))


def gelu_slope(field):
    tanh_val = jnp.tanh(gelu_coef * (field + 0.044715 * field * field * field))
    return 0.5 * (1.0 + tanh_val) + 0.5 * field * (1.0 - tanh_val * tanh_val) * gelu_coef * (
        1.0 + 3.0 * 0.044715 * field * field
    )


def frame_index(frame_lengths, positions):
    frame_ends = jnp.cumsum(frame_lengths)
    return jnp.sum((frame_ends[None, :] <= positions[:, None]).astype(jnp.int32), axis=1)


def masked_scores(query_heads, key_heads, key_frames, own_frames, score_scale):
    scores = (
        jnp.einsum("qhd,khd->hqk", query_heads, key_heads, preferred_element_type=jnp.float32)
        * score_scale
    )
    allowed = key_frames[None, :] <= own_frames[:, None]
    return jnp.where(allowed[None, :, :], scores, -jnp.inf)


def shards(
    residual, queries, keys, values, frame_lengths, routes, route_gates, w_in, w_out, out_grad
):
    n_ctx = lax.axis_size("ctx")
    n_grp = lax.axis_size("grp")
    tok_rows, feat_dev = residual.shape
    exp_dev = w_in.shape[0]
    head_dim = HEAD_DIM
    heads_dev = feat_dev // head_dim
    seq_len = tok_rows * n_ctx
    experts_all = exp_dev * n_ctx
    capacity = 6 * tok_rows // experts_all
    width_all = feat_dev * n_grp
    score_scale = head_dim ** (-0.5)
    ctx_index = lax.axis_index("ctx")
    frames = frame_index(frame_lengths, jnp.arange(seq_len, dtype=jnp.int32))
    own_frames = lax.dynamic_slice_in_dim(frames, ctx_index * tok_rows, tok_rows)
    query_heads = queries.reshape(tok_rows, heads_dev, head_dim)
    keys_all, values_all = (
        lax.all_gather(keys, "ctx", axis=0, tiled=True),
        lax.all_gather(values, "ctx", axis=0, tiled=True),
    )
    key_heads_all = keys_all.reshape(seq_len, heads_dev, head_dim)
    value_heads_all = values_all.reshape(seq_len, heads_dev, head_dim)
    scores = masked_scores(query_heads, key_heads_all, frames, own_frames, score_scale)
    row_max = jnp.max(scores, axis=2, keepdims=True)
    log_total = row_max + jnp.log(jnp.sum(jnp.exp(scores - row_max), axis=2, keepdims=True))
    prob = jnp.exp(scores - log_total).astype(jnp.bfloat16)
    attn_heads = jnp.einsum(
        "hqk,khd->qhd", prob, value_heads_all, preferred_element_type=jnp.float32
    ).astype(jnp.bfloat16)
    attn = attn_heads.reshape(tok_rows, feat_dev)
    mixed = (residual.astype(jnp.float32) + attn.astype(jnp.float32)).astype(jnp.bfloat16)
    mixed_f = mixed.astype(jnp.float32)
    square_sum = lax.psum(jnp.sum(mixed_f * mixed_f, axis=1), "grp")
    inv_rms = lax.rsqrt(square_sum / width_all + 1e-06)
    normed = (mixed_f * inv_rms[:, None]).astype(jnp.bfloat16)
    expert_flat = routes.reshape(-1)
    onehot = (expert_flat[:, None] == jnp.arange(experts_all, dtype=jnp.int32)[None, :]).astype(
        jnp.int32
    )
    earlier = jnp.cumsum(onehot, axis=0) - onehot
    ranks = jnp.sum(earlier * onehot, axis=1)
    slot_ids = jnp.arange(experts_all * capacity, dtype=jnp.int32)
    matched = (expert_flat[None, :] == (slot_ids // capacity)[:, None]) & (
        ranks[None, :] == (slot_ids % capacity)[:, None]
    )
    source = jnp.sum(
        jnp.where(matched, jnp.arange(2 * tok_rows, dtype=jnp.int32)[None, :], 0), axis=1
    )
    filled = jnp.any(matched, axis=1)[:, None]
    token_of = source // 2
    picked_rows = normed[token_of]
    rows_buffer = jnp.where(filled, picked_rows, jnp.zeros_like(picked_rows)).reshape(
        n_ctx, exp_dev, capacity, feat_dev
    )
    gate_of = route_gates.reshape(-1)[source]
    grad_rows = (gate_of[:, None] * out_grad[token_of].astype(jnp.float32)).astype(jnp.bfloat16)
    grads_buffer = jnp.where(filled, grad_rows, jnp.zeros_like(grad_rows)).reshape(
        n_ctx, exp_dev, capacity, feat_dev
    )
    row_index = expert_flat * capacity + ranks
    rows_recv = lax.all_to_all(rows_buffer, "ctx", split_axis=0, concat_axis=0, tiled=True)
    partial_value = jnp.einsum(
        "secf,efh->sech", rows_recv, w_in, preferred_element_type=jnp.float32
    )
    pre_act = lax.psum(partial_value.astype(jnp.bfloat16), "grp").astype(jnp.float32)
    activated = gelu_tanh(pre_act).astype(jnp.bfloat16)
    expert_out = jnp.einsum(
        "sech,ehf->secf", activated, w_out, preferred_element_type=jnp.float32
    ).astype(jnp.bfloat16)
    returned = lax.all_to_all(expert_out, "ctx", split_axis=0, concat_axis=0, tiled=True)
    returned_rows = returned.reshape(experts_all * capacity, feat_dev)[row_index].reshape(
        tok_rows, 2, feat_dev
    )
    combined = jnp.sum(route_gates[:, :, None] * returned_rows.astype(jnp.float32), axis=1)
    layer_out = (mixed_f + combined).astype(jnp.bfloat16)
    grads_recv = lax.all_to_all(grads_buffer, "ctx", split_axis=0, concat_axis=0, tiled=True)
    w_out_grad = jnp.einsum(
        "sech,secf->ehf", activated, grads_recv, preferred_element_type=jnp.float32
    ).astype(jnp.bfloat16)
    partial_back = jnp.einsum(
        "secf,ehf->sech", grads_recv, w_out, preferred_element_type=jnp.float32
    )
    act_grad = lax.psum(partial_back.astype(jnp.bfloat16), "grp").astype(jnp.float32)
    pre_grad = (act_grad * gelu_slope(pre_act)).astype(jnp.bfloat16)
    w_in_grad = jnp.einsum(
        "secf,sech->efh", rows_recv, pre_grad, preferred_element_type=jnp.float32
    ).astype(jnp.bfloat16)
    row_grad = jnp.einsum(
        "sech,efh->secf", pre_grad, w_in, preferred_element_type=jnp.float32
    ).astype(jnp.bfloat16)
    row_grad_back = lax.all_to_all(row_grad, "ctx", split_axis=0, concat_axis=0, tiled=True)
    grad_back_rows = row_grad_back.reshape(experts_all * capacity, feat_dev)[row_index].reshape(
        tok_rows, 2, feat_dev
    )
    normed_grad = jnp.sum(grad_back_rows.astype(jnp.float32), axis=1)
    input_grad_f = out_grad.astype(jnp.float32) + inv_rms[:, None] * normed_grad
    input_grad = input_grad_f.astype(jnp.bfloat16)
    grad_heads = input_grad.reshape(tok_rows, heads_dev, head_dim)
    row_dot = jnp.sum(grad_heads.astype(jnp.float32) * attn_heads.astype(jnp.float32), axis=2).T
    prob_f = jnp.exp(scores - log_total)
    prob_all = prob_f.astype(jnp.bfloat16)
    dprob = jnp.einsum(
        "qhd,khd->hqk", grad_heads, value_heads_all, preferred_element_type=jnp.float32
    )
    dscore_all = (prob_f * (dprob - row_dot[:, :, None]) * score_scale).astype(jnp.bfloat16)
    query_sum = jnp.einsum(
        "hqk,khd->qhd", dscore_all, key_heads_all, preferred_element_type=jnp.float32
    )
    key_term = jnp.einsum(
        "hqk,qhd->khd", dscore_all, query_heads, preferred_element_type=jnp.float32
    ).reshape(seq_len, feat_dev)
    value_term = jnp.einsum(
        "hqk,qhd->khd", prob_all, grad_heads, preferred_element_type=jnp.float32
    ).reshape(seq_len, feat_dev)
    both_terms = jnp.concatenate([key_term, value_term], axis=1)
    key_grad_f, value_grad_f = (
        lax.psum_scatter(
            both_terms[:, :feat_dev].astype(jnp.bfloat16), "ctx", scatter_dimension=0, tiled=True
        ).astype(jnp.float32),
        lax.psum_scatter(
            both_terms[:, feat_dev:].astype(jnp.bfloat16), "ctx", scatter_dimension=0, tiled=True
        ).astype(jnp.float32),
    )
    query_grad = query_sum.reshape(tok_rows, feat_dev).astype(jnp.bfloat16)
    return (
        layer_out,
        input_grad,
        query_grad,
        key_grad_f.astype(jnp.bfloat16),
        value_grad_f.astype(jnp.bfloat16),
        w_in_grad,
        w_out_grad,
    )


def solution(mesh):
    in_specs = (
        P("ctx", "grp"),
        P("ctx", "grp"),
        P("ctx", "grp"),
        P("ctx", "grp"),
        P(),
        P("ctx", None),
        P("ctx", None),
        P("ctx", "grp", None),
        P("ctx", None, "grp"),
        P("ctx", "grp"),
    )
    out_specs = (
        P("ctx", "grp"),
        P("ctx", "grp"),
        P("ctx", "grp"),
        P("ctx", "grp"),
        P("ctx", "grp"),
        P("ctx", "grp", None),
        P("ctx", None, "grp"),
    )
    return jax.shard_map(shards, mesh=mesh, in_specs=in_specs, out_specs=out_specs, check_vma=False)
```

profile of v0, /device:TPU:0, one launch (start us, length us, event | category | flops | bytes accessed | tf_op | source)
XLA Modules:
  0.0 694.6 jit_solution(5121470494980655795)
XLA Ops:
  21.1 13.0 %gather_fusion.2 = f32[1536]{0:T(1024)} fusion(f32[512]{0:T(512)S(1)} %reshape.277, s32[2048]{0:T(1024)} %pad_clamp_fusion), kind=kCustom, calls=%fused_computation.2 | custom fusion | bytes 18432 | tf_op jit(solution)/shard_map/gather | solution.py:93
  48.4 24.0 %all-gather.3.cloned.1.call-done = bf16[4096,512]{0,1:T(8,128)(2,1)} async-done(((bf16[256,512]{0,1:T(8,128)(2,1)}), bf16[4096,512]{0,1:T(8,128)(2,1)}) %all-gather.3.cloned.1.call-update) | async-done | bytes 4194320 | tf_op jit(solution)/shard_map/all_gather | solution.py:56
  83.8 45.8 %all-gather.5.cloned.1.call-done = bf16[4096,512]{1,0:T(8,128)(2,1)} async-done(((bf16[256,512]{1,0:T(8,128)(2,1)}), bf16[4096,512]{1,0:T(8,128)(2,1)}) %all-gather.5.cloned.1.call-update) | async-done | bytes 4194320 | tf_op jit(solution)/shard_map/all_gather | solution.py:57
  129.6 6.4 copy.84
  136.0 10.5 %fusion.41 = f32[4,256,128]{1,2,0:T(8,128)} fusion(bf16[4096,4,128]{0,2,1:T(8,128)(2,1)} %bitcast.101, f32[4,256,4096]{2,1,0:T(8,128)} %copy-done.3, f32[4,256]{1,0:T(4,128)S(1)} %log_add_fusion, pred[256,4096]{1,0:T(8,128)(4,1)} %broadcast_compare_fusion), kind=kOutput, calls=%fused_computation.60 | convolution fusion | flops 1090781184 | bytes 22548480 | tf_op jit(solution)/shard_map/hqk,khd->qhd/dot_general | solution.py:65
  150.5 19.6 %psum.21 = f32[256]{0:T(256)} all-reduce(f32[256]{0:T(256)S(1)} %get-tuple-element.39), channel_id=1, replica_groups=mesh['ctx'=16,'grp'=8] {'grp'}, use_global_device_ids=true, to_apply=%region_9.10 | all-reduce | flops 256 | bytes 2048 | tf_op jit(solution)/shard_map/psum | solution.py:71
  172.5 6.5 gather_fusion
  182.2 28.7 %all_to_all.20 = bf16[16,2,48,512]{3,2,1,0:T(8,128)(2,1)} all-to-all(bf16[16,2,48,512]{3,2,1,0:T(8,128)(2,1)S(1)} %get-tuple-element.41), channel_id=1, replica_groups=mesh['ctx'=16,'grp'=8] {'ctx'}, dimensions={0} | all-to-all | bytes 3145728 | tf_op jit(solution)/shard_map/all_to_all | solution.py:114
  215.4 7.1 %convert_bitcast_fusion = bf16[16,2,48,1536]{3,2,0,1:T(8,128)(2,1)} fusion(bf16[2,1536,512]{2,1,0:T(8,128)(2,1)} %param.18, bf16[16,2,48,512]{3,2,1,0:T(8,128)(2,1)} %all_to_all.20), kind=kOutput, calls=%fused_computation.35 | convolution fusion | flops 2418278400 | bytes 9437184 | tf_op jit(solution)/shard_map/secf,ehf->sech/dot_general | solution.py:118
  222.5 16.4 %all-to-all-done = bf16[16,2,48,512]{3,2,1,0:T(8,128)(2,1)} async-done(((bf16[16,2,48,512]{3,2,1,0:T(8,128)(2,1)}), bf16[16,2,48,512]{3,2,1,0:T(8,128)(2,1)}, u32[]{:S(2)}, u32[]{:S(2)}) %all-to-all-start) | async-done | bytes 1572896 | tf_op jit(solution)/shard_map/all_to_all | solution.py:99
  244.6 200.2 %all-reduce.3.cloned.1.call-done = (bf16[16,2,48,1536]{3,2,0,1:T(8,128)(2,1)}, bf16[16,2,48,1536]{3,2,0,1:T(8,128)(2,1)}) async-done(((bf16[16,2,48,1536]{3,2,0,1:T(8,128)(2,1)}, bf16[16,2,48,1536]{3,2,0,1:T(8,128)(2,1)}), (bf16[16,2,48,1536]{3,2,0,1:T(8,128)(2,1)}, bf16[16,2,48,1536]{3,2,0,1:T(8,128)(2,1)})) %all-reduce.3.cloned.1.call-update) | async-done | bytes 9437200 | tf_op jit(solution)/shard_map/psum | solution.py:103
  444.8 8.5 %fusion.9 = bf16[16,2,48,1536]{3,2,0,1:T(8,128)(2,1)S(1)} fusion(bf16[16,2,48,1536]{3,2,0,1:T(8,128)(2,1)} %get-tuple-element.37, bf16[16,2,48,1536]{3,2,0,1:T(8,128)(2,1)} %get-tuple-element.38), kind=kLoop, calls=%fused_computation.25 | loop fusion | flops 49545216 | bytes 14155776 | tf_op jit(solution)/shard_map/convert_element_type | solution.py:122
  457.3 6.5 all-to-all-start.3
  464.4 23.0 %all-to-all-done.3 = bf16[16,2,48,512]{3,2,1,0:T(8,128)(2,1)S(1)} async-done(((bf16[16,2,48,512]{3,2,1,0:T(8,128)(2,1)}), bf16[16,2,48,512]{3,2,1,0:T(8,128)(2,1)S(1)}, u32[]{:S(2)}, u32[]{:S(2)}) %all-to-all-start.3) | async-done | bytes 1572896 | tf_op jit(solution)/shard_map/all_to_all | solution.py:129
  491.6 12.6 %convolution_convert_fusion.1 = bf16[4,128,4096]{2,1,0:T(8,128)(2,1)} fusion(bf16[256,4,128]{0,2,1:T(8,128)(2,1)S(1)} %bitcast.107, f32[4,256,4096]{2,1,0:T(8,128)} %copy-done.3, f32[4,256]{1,0:T(4,128)S(1)} %copy-done.21, pred[256,4096]{1,0:T(8,128)(4,1)S(1)} %copy-done.5), kind=kOutput, calls=%fused_computation.32 | convolution fusion | flops 1092616192 | bytes 22286336 | tf_op jit(solution)/shard_map/hqk,qhd->khd/dot_general | solution.py:150
  504.2 6.5 copy.101
  511.3 12.0 %multiply_convert_fusion = bf16[4,256,4096]{2,1,0:T(8,128)(2,1)S(1)} fusion(f32[4,256,4096]{2,1,0:T(8,128)} %copy-done.3, bf16[256,4,128]{0,2,1:T(8,128)(2,1)S(1)} %bitcast.108, bf16[4096,4,128]{0,2,1:T(8,128)(2,1)} %bitcast.102, f32[4,256]{1,0:T(4,128)S(1)} %bitcast.112, f32[4,256]{1,0:T(4,128)S(1)} %copy-done.21, pred[256,4096]{1,0:T(8,128)(4,1)S(1)} %copy-done.5), kind=kOutput, calls=%fused_computation.12 | convolution fusion | flops 1103101952 | bytes 30679040 | tf_op jit(solution)/shard_map/qhd,khd->hqk/dot_general | solution.py:140
  528.1 6.5 copy.100
  534.6 6.8 fusion.36
  547.4 8.0 %bitcast_convert_fusion = bf16[2,1536,512]{2,1,0:T(8,128)(2,1)} fusion(bf16[16,2,48,512]{3,2,1,0:T(8,128)(2,1)S(1)} %copy-done.12, bf16[16,2,48,1536]{3,2,0,1:T(8,128)(2,1)} %get-tuple-element.37), kind=kOutput, calls=%fused_computation.29 | convolution fusion | flops 2441084928 | bytes 9437184 | tf_op jit(solution)/shard_map/sech,secf->ehf/dot_general | solution.py:115
  555.4 7.3 %bitcast_convert_fusion.1 = bf16[2,512,1536]{2,1,0:T(8,128)(2,1)} fusion(bf16[16,2,48,512]{3,2,1,0:T(8,128)(2,1)} %all-to-all-done, bf16[16,2,48,1536]{3,2,0,1:T(8,128)(2,1)} %copy-done.7), kind=kOutput, calls=%fused_computation.30 | convolution fusion | flops 2417491968 | bytes 9437184 | tf_op jit(solution)/shard_map/secf,sech->efh/dot_general | solution.py:123
  562.7 7.2 %convolution_convert_fusion.2 = bf16[4,256,128]{1,2,0:T(8,128)(2,1)} fusion(bf16[4,256,4096]{2,1,0:T(8,128)(2,1)} %copy-done.6, bf16[4096,4,128]{0,2,1:T(8,128)(2,1)S(1)} %bitcast.100), kind=kOutput, calls=%fused_computation.58 | convolution fusion | flops 1073872896 | bytes 12845056 | tf_op jit(solution)/shard_map/hqk,khd->qhd/dot_general | solution.py:144
  582.8 20.9 %reduce-scatter.5.cloned.1.call-done = bf16[256,512]{1,0:T(8,128)(2,1)} async-done(((bf16[4096,512]{1,0:T(8,128)(2,1)}), bf16[256,512]{1,0:T(8,128)(2,1)}) %reduce-scatter.5.cloned.1.call-update) | async-done | bytes 262160 | tf_op jit(solution)/shard_map/reduce_scatter | solution.py:158
  603.7 84.2 %reduce-scatter.3.cloned.1.call-done = bf16[256,512]{1,0:T(8,128)(2,1)} async-done(((bf16[4096,512]{1,0:T(8,128)(2,1)}), bf16[256,512]{1,0:T(8,128)(2,1)}) %reduce-scatter.3.cloned.1.call-update) | async-done | bytes 262160 | tf_op jit(solution)/shard_map/reduce_scatter | solution.py:155
  (114 shorter events, 91.8 us)
Async XLA Ops:
  7.2 231.8 %copy-start = (bf16[2,512,1536]{2,1,0:T(8,128)(2,1)S(1)}, bf16[2,512,1536]{2,1,0:T(8,128)(2,1)}, u32[]{:S(2)}) copy-start(bf16[2,512,1536]{2,1,0:T(8,128)(2,1)} %param.17) | copy-start | bytes 9437188
  7.2 65.3 %all-gather.3.cloned.1.call-start = ((), (), s32[]{:S(2)}) async-start(), calls=%async_computation.6 | async-start | bytes 4456448 | tf_op jit(solution)/shard_map/all_gather | solution.py:56
  9.2 120.4 %all-gather.5.cloned.1.call-start = ((), (), s32[]{:S(2)}) async-start(), calls=%async_computation.7 | async-start | bytes 4456448 | tf_op jit(solution)/shard_map/all_gather | solution.py:57
  14.3 26.4 %copy-start.2 = (bf16[256,512]{1,0:T(8,128)(2,1)S(1)}, bf16[256,512]{1,0:T(8,128)(2,1)}, u32[]{:S(2)}) copy-start(bf16[256,512]{1,0:T(8,128)(2,1)} %param.19) | copy-start | bytes 786436
  72.4 5.6 copy-start.4
  78.0 5.7 copy-start.3
  83.8 62.7 %copy-start.20 = (f32[4,256]{1,0:T(4,128)}, f32[4,256]{1,0:T(4,128)S(1)}, u32[]{:S(2)}) copy-start(f32[4,256]{1,0:T(4,128)S(1)} %log_add_fusion) | copy-start | bytes 12292
  210.9 28.0 %all-to-all-start = ((bf16[16,2,48,512]{3,2,1,0:T(8,128)(2,1)}), bf16[16,2,48,512]{3,2,1,0:T(8,128)(2,1)}, u32[]{:S(2)}, u32[]{:S(2)}) async-start(bf16[16,2,48,512]{3,2,1,0:T(8,128)(2,1)} %get-tuple-element.42), calls=%async_computation | async-start | bytes 3145728 | tf_op jit(solution)/shard_map/all_to_all | solution.py:99
  215.3 229.5 %all-reduce.3.cloned.1.call-start = ((), (), s32[]{:S(2)}) async-start(), calls=%async_computation.10 | async-start | bytes 18874368 | tf_op jit(solution)/shard_map/psum | solution.py:103
  456.0 8.1 %copy-start.19 = (s32[256,2]{0,1:T(2,128)S(1)}, s32[256,2]{0,1:T(2,128)}, u32[]{:S(2)}) copy-start(s32[256,2]{0,1:T(2,128)} %param.15) | copy-start | bytes 6148
  456.0 8.4 %copy-start.18 = (s32[512]{0:T(512)S(1)}, s32[512]{0:T(512)}, u32[]{:S(2)}) copy-start(s32[512]{0:T(512)} %copy-done.17) | copy-start | bytes 6148
  457.3 30.1 %all-to-all-start.3 = ((bf16[16,2,48,512]{3,2,1,0:T(8,128)(2,1)}), bf16[16,2,48,512]{3,2,1,0:T(8,128)(2,1)S(1)}, u32[]{:S(2)}, u32[]{:S(2)}) async-start(bf16[16,2,48,512]{3,2,1,0:T(8,128)(2,1)} %copy.95), calls=%async_computation.3 | async-start | bytes 3145728 | tf_op jit(solution)/shard_map/all_to_all | solution.py:129
  463.8 139.9 %reduce-scatter.5.cloned.1.call-start = ((), (), s32[]{:S(2)}) async-start(), calls=%async_computation.9 | async-start | bytes 4456448 | tf_op jit(solution)/shard_map/reduce_scatter | solution.py:158
  487.4 4.2 copy-start.21
  491.4 12.7 %copy-start.13 = (bf16[256,512]{1,0:T(8,128)(2,1)}, bf16[256,512]{1,0:T(8,128)(2,1)S(1)}, u32[]{:S(2)}) copy-start(bf16[256,512]{1,0:T(8,128)(2,1)S(1)} %add_convert_fusion) | copy-start | bytes 786436
  504.2 7.0 %copy-start.11 = (f32[4,256,128]{1,2,0:T(8,128)S(1)}, f32[4,256,128]{1,2,0:T(8,128)}, u32[]{:S(2)}) copy-start(f32[4,256,128]{1,2,0:T(8,128)} %fusion.41) | copy-start | bytes 1572868
  510.7 177.2 %reduce-scatter.3.cloned.1.call-start = ((), (), s32[]{:S(2)}) async-start(), calls=%async_computation.8 | async-start | bytes 4456448 | tf_op jit(solution)/shard_map/reduce_scatter | solution.py:155
  511.2 12.1 %copy-start.9 = (bf16[256,512]{0,1:T(8,128)(2,1)S(1)}, bf16[256,512]{0,1:T(8,128)(2,1)}, u32[]{:S(2)}) copy-start(bf16[256,512]{0,1:T(8,128)(2,1)} %copy.111) | copy-start | bytes 786436
  523.3 4.7 copy-start.6
  541.4 5.9 copy-start.12
  542.8 29.5 %all-to-all-start.1 = ((bf16[16,2,48,512]{3,2,1,0:T(8,128)(2,1)}), bf16[16,2,48,512]{3,2,1,0:T(8,128)(2,1)}, u32[]{:S(2)}, u32[]{:S(2)}) async-start(bf16[16,2,48,512]{3,2,1,0:T(8,128)(2,1)} %copy.91), calls=%async_computation.1 | async-start | bytes 3145728 | tf_op jit(solution)/shard_map/all_to_all | solution.py:108
  555.4 7.3 %copy-start.8 = (bf16[4096,512]{0,1:T(8,128)(2,1)S(1)}, bf16[4096,512]{0,1:T(8,128)(2,1)}, u32[]{:S(2)}) copy-start(bf16[4096,512]{0,1:T(8,128)(2,1)} %all-gather.3.cloned.1.call-done) | copy-start | bytes 12582916
  569.9 12.1 %copy-start.10 = (bf16[256,512]{1,0:T(8,128)(2,1)S(1)}, bf16[256,512]{1,0:T(8,128)(2,1)}, u32[]{:S(2)}) copy-start(bf16[256,512]{1,0:T(8,128)(2,1)} %get-tuple-element.40) | copy-start | bytes 786436
  569.9 118.1 %copy-start.1 = (bf16[2,512,1536]{2,1,0:T(8,128)(2,1)S(1)}, bf16[2,512,1536]{2,1,0:T(8,128)(2,1)}, u32[]{:S(2)}) copy-start(bf16[2,512,1536]{2,1,0:T(8,128)(2,1)} %param.17) | copy-start | bytes 9437188
  (6 other events, 10.9 us)
Sparse Core Ops, SparseCore 0:
  10.9 61.5 all-gather.2
  74.9 54.6 all-gather.4
  244.7 200.0 all-reduce.2
  510.8 92.8 reduce-scatter.4
  608.7 79.1 reduce-scatter.2
where the time goes:
time: 704 us; the launch traced here: 695 us
  waiting for transfers between devices  416 us (59%)
  matrix products  89.3 us (13%)
  local copies, waits for them, and re-layouts  73.7 us (10%)
  blocking collectives  48.4 us (7%)
  other arithmetic  36.8 us (5%)
  starting transfers between devices  16.3 us (2%)
  between operations  14.4 us (2%)
    psum x1, waiting for transfers between devices, shards(): lax.psum(partial_value.astype(jnp.bfloat16), 'grp').astype(jnp.float32)  200 us
    reduce_scatter x1, waiting for transfers between devices, shards(): lax.psum_scatter(both_terms[:, :feat_dev].astype(jnp.bfloat16), 'ctx', sc...  84.2 us
    all_gather x1, waiting for transfers between devices, shards(): lax.all_gather(values, 'ctx', axis=0, tiled=True)  45.8 us
    all_to_all x1, blocking collectives, shards(): lax.all_to_all(grads_buffer, 'ctx', split_axis=0, concat_axis=0, tiled=True)  28.7 us
    all_gather x1, waiting for transfers between devices, shards(): lax.all_gather(keys, 'ctx', axis=0, tiled=True)  24 us
    all_to_all x1, waiting for transfers between devices, shards(): lax.all_to_all(row_grad, 'ctx', split_axis=0, concat_axis=0, tiled=True)  23 us
    reduce_scatter x1, waiting for transfers between devices, shards(): lax.psum_scatter(both_terms[:, feat_dev:].astype(jnp.bfloat16), 'ctx', sc...  20.9 us
    psum x1, blocking collectives, shards(): square_sum = lax.psum(jnp.sum(mixed_f * mixed_f, axis=1), 'grp')  19.6 us
  transfers between devices with their start and end apart: 8, of which 8 were waited for; matrix products, arithmetic and copies ran while one was open for 17% of the time, Pallas kernels for 0%

commit v1 on v0

--- a/solution.py
+++ b/solution.py
@@ -48,6 +48,49 @@
     capacity = 6 * tok_rows // experts_all
     width_all = feat_dev * n_grp
     score_scale = head_dim ** (-0.5)
+    expert_flat = routes.reshape(-1)
+    onehot = (expert_flat[:, None] == jnp.arange(experts_all, dtype=jnp.int32)[None, :]).astype(
+        jnp.int32
+    )
+    earlier = jnp.cumsum(onehot, axis=0) - onehot
+    ranks = jnp.sum(earlier * onehot, axis=1)
+    row_index = (expert_flat * capacity + ranks).reshape(tok_rows, 2)
+    slot_ids = jnp.arange(experts_all * capacity, dtype=jnp.int32)
+    pick = [
+        (slot_ids[:, None] == row_index[None, :, a]).astype(jnp.bfloat16) for a in range(2)
+    ]
+    pick_both = pick[0] + pick[1]
+    pick_two = jnp.concatenate(pick, axis=1)
+
+    def to_experts(rows):
+        rows = rows.reshape(n_ctx, exp_dev * capacity, feat_dev)
+        recv = lax.all_to_all(rows, "ctx", split_axis=0, concat_axis=0, tiled=True)
+        recv = recv.reshape(n_ctx, exp_dev, capacity, feat_dev)
+        return recv.transpose(1, 0, 2, 3).reshape(exp_dev, n_ctx * capacity, feat_dev)
+
+    def to_tokens(rows):
+        rows = rows.reshape(exp_dev, n_ctx, capacity, feat_dev).transpose(1, 0, 2, 3)
+        rows = rows.reshape(n_ctx, exp_dev * capacity, feat_dev)
+        back = lax.all_to_all(rows, "ctx", split_axis=0, concat_axis=0, tiled=True)
+        return back.reshape(experts_all * capacity, feat_dev)
+
+    def sum_scatter(partial):
+        flat = partial.astype(jnp.bfloat16).reshape(-1, partial.shape[-1])
+        return lax.psum_scatter(flat, "grp", scatter_dimension=0, tiled=True).astype(jnp.float32)
+
+    def gather(shard):
+        full = lax.all_gather(shard, "grp", axis=0, tiled=True)
+        return full.reshape(exp_dev, n_ctx * capacity, -1)
+
+    out_grad_f = out_grad.astype(jnp.float32)
+    gated = jnp.concatenate(
+        [(route_gates[:, a : a + 1] * out_grad_f).astype(jnp.bfloat16) for a in range(2)], axis=0
+    )
+    grad_rows = jnp.dot(pick_two, gated, preferred_element_type=jnp.float32).astype(jnp.bfloat16)
+    grads_recv = to_experts(grad_rows)
+    act_grad = sum_scatter(
+        jnp.einsum("erf,ehf->erh", grads_recv, w_out, preferred_element_type=jnp.float32)
+    )
     ctx_index = lax.axis_index("ctx")
     frames = frame_index(frame_lengths, jnp.arange(seq_len, dtype=jnp.int32))
     own_frames = lax.dynamic_slice_in_dim(frames, ctx_index * tok_rows, tok_rows)
@@ -71,67 +114,36 @@
     square_sum = lax.psum(jnp.sum(mixed_f * mixed_f, axis=1), "grp")
     inv_rms = lax.rsqrt(square_sum / width_all + 1e-06)
     normed = (mixed_f * inv_rms[:, None]).astype(jnp.bfloat16)
-    expert_flat = routes.reshape(-1)
-    onehot = (expert_flat[:, None] == jnp.arange(experts_all, dtype=jnp.int32)[None, :]).astype(
-        jnp.int32
-    )
-    earlier = jnp.cumsum(onehot, axis=0) - onehot
-    ranks = jnp.sum(earlier * onehot, axis=1)
-    slot_ids = jnp.arange(experts_all * capacity, dtype=jnp.int32)
-    matched = (expert_flat[None, :] == (slot_ids // capacity)[:, None]) & (
-        ranks[None, :] == (slot_ids % capacity)[:, None]
-    )
-    source = jnp.sum(
-        jnp.where(matched, jnp.arange(2 * tok_rows, dtype=jnp.int32)[None, :], 0), axis=1
-    )
-    filled = jnp.any(matched, axis=1)[:, None]
-    token_of = source // 2
-    picked_rows = normed[token_of]
-    rows_buffer = jnp.where(filled, picked_rows, jnp.zeros_like(picked_rows)).reshape(
-        n_ctx, exp_dev, capacity, feat_dev
-    )
-    gate_of = route_gates.reshape(-1)[source]
-    grad_rows = (gate_of[:, None] * out_grad[token_of].astype(jnp.float32)).astype(jnp.bfloat16)
-    grads_buffer = jnp.where(filled, grad_rows, jnp.zeros_like(grad_rows)).reshape(
-        n_ctx, exp_dev, capacity, feat_dev
-    )
-    row_index = expert_flat * capacity + ranks
-    rows_recv = lax.all_to_all(rows_buffer, "ctx", split_axis=0, concat_axis=0, tiled=True)
-    partial_value = jnp.einsum(
-        "secf,efh->sech", rows_recv, w_in, preferred_element_type=jnp.float32
-    )
-    pre_act = lax.psum(partial_value.astype(jnp.bfloat16), "grp").astype(jnp.float32)
-    activated = gelu_tanh(pre_act).astype(jnp.bfloat16)
+    norm_rows = jnp.dot(pick_both, normed, preferred_element_type=jnp.float32).astype(jnp.bfloat16)
+    rows_recv = to_experts(norm_rows)
+    rows_recv, act_grad = lax.optimization_barrier((rows_recv, act_grad))
+    pre_act = sum_scatter(
+        jnp.einsum("erf,efh->erh", rows_recv, w_in, preferred_element_type=jnp.float32)
+    )
+    pre_grad = gather((act_grad * gelu_slope(pre_act)).astype(jnp.bfloat16))
+    act_shard, pre_grad = lax.optimization_barrier(
+        (gelu_tanh(pre_act).astype(jnp.bfloat16), pre_grad)
+    )
+    activated = gather(act_shard)
+    row_grad = jnp.einsum(
+        "erh,efh->erf", pre_grad, w_in, preferred_element_type=jnp.float32
+    ).astype(jnp.bfloat16)
+    normed_grad = jnp.dot(pick_both.T, to_tokens(row_grad), preferred_element_type=jnp.float32)
+    w_in_grad = jnp.einsum(
+        "erf,erh->efh", rows_recv, pre_grad, preferred_element_type=jnp.float32
+    ).astype(jnp.bfloat16)
     expert_out = jnp.einsum(
-        "sech,ehf->secf", activated, w_out, preferred_element_type=jnp.float32
-    ).astype(jnp.bfloat16)
-    returned = lax.all_to_all(expert_out, "ctx", split_axis=0, concat_axis=0, tiled=True)
-    returned_rows = returned.reshape(experts_all * capacity, feat_dev)[row_index].reshape(
-        tok_rows, 2, feat_dev
-    )
-    combined = jnp.sum(route_gates[:, :, None] * returned_rows.astype(jnp.float32), axis=1)
+        "erh,ehf->erf", activated, w_out, preferred_element_type=jnp.float32
+    ).astype(jnp.bfloat16)
+    returned = jnp.dot(pick_two.T, to_tokens(expert_out), preferred_element_type=jnp.float32)
+    combined = (
+        route_gates[:, 0:1] * returned[:tok_rows] + route_gates[:, 1:2] * returned[tok_rows:]
+    )
     layer_out = (mixed_f + combined).astype(jnp.bfloat16)
-    grads_recv = lax.all_to_all(grads_buffer, "ctx", split_axis=0, concat_axis=0, tiled=True)
     w_out_grad = jnp.einsum(
-        "sech,secf->ehf", activated, grads_recv, preferred_element_type=jnp.float32
-    ).astype(jnp.bfloat16)
-    partial_back = jnp.einsum(
-        "secf,ehf->sech", grads_recv, w_out, preferred_element_type=jnp.float32
-    )
-    act_grad = lax.psum(partial_back.astype(jnp.bfloat16), "grp").astype(jnp.float32)
-    pre_grad = (act_grad * gelu_slope(pre_act)).astype(jnp.bfloat16)
-    w_in_grad = jnp.einsum(
-        "secf,sech->efh", rows_recv, pre_grad, preferred_element_type=jnp.float32
-    ).astype(jnp.bfloat16)
-    row_grad = jnp.einsum(
-        "sech,efh->secf", pre_grad, w_in, preferred_element_type=jnp.float32
-    ).astype(jnp.bfloat16)
-    row_grad_back = lax.all_to_all(row_grad, "ctx", split_axis=0, concat_axis=0, tiled=True)
-    grad_back_rows = row_grad_back.reshape(experts_all * capacity, feat_dev)[row_index].reshape(
-        tok_rows, 2, feat_dev
-    )
-    normed_grad = jnp.sum(grad_back_rows.astype(jnp.float32), axis=1)
-    input_grad_f = out_grad.astype(jnp.float32) + inv_rms[:, None] * normed_grad
+        "erh,erf->ehf", activated, grads_recv, preferred_element_type=jnp.float32
+    ).astype(jnp.bfloat16)
+    input_grad_f = out_grad_f + inv_rms[:, None] * normed_grad
     input_grad = input_grad_f.astype(jnp.bfloat16)
     grad_heads = input_grad.reshape(tok_rows, heads_dev, head_dim)
     row_dot = jnp.sum(grad_heads.astype(jnp.float32) * attn_heads.astype(jnp.float32), axis=2).T

time: 704 us -> 578 us (0.82)
  waiting for transfers between devices: 416 us -> 297 us
  blocking collectives: 48.4 us -> 113 us
  local copies, waits for them, and re-layouts: 73.7 us -> 34.6 us
  other arithmetic: 36.8 us -> 17.7 us
  starting transfers between devices: 16.3 us -> 6.21 us
    psum x1 -> x0, waiting for transfers between devices: 200 us -> none  [shards(): lax.psum(partial_value.astype(jnp.bfloat16), 'grp').astype(jnp.float32)]
    all_to_all x1 -> x3, blocking collectives: 28.7 us -> 93.9 us  [the longest x2 62.1 us: to_experts(): recv = lax.all_to_all(rows, 'ctx', split_axis=0, concat_axis=0, tiled=True)]
    all_gather x0 -> x2, waiting for transfers between devices: none -> 56.4 us  [gather(): full = lax.all_gather(shard, 'grp', axis=0, tiled=True)]
    reduce_scatter x0 -> x2, waiting for transfers between devices: none -> 52.4 us  [sum_scatter(): lax.psum_scatter(flat, 'grp', scatter_dimension=0, tiled=True)]
    all_to_all x3 -> x1, waiting for transfers between devices: 39.9 us -> 4.35 us  [to_tokens(): back = lax.all_to_all(rows, 'ctx', split_axis=0, concat_axis=0, tiled=True)]
    gather x5 -> x0, local copies, waits for them, and re-layouts: 31.2 us -> none  [the longest x1 13 us: shards(): gate_of = route_gates.reshape(-1)[source]]
    all_gather x1, waiting for transfers between devices: 24 us -> 54.3 us  [shards(): lax.all_gather(keys, 'ctx', axis=0, tiled=True)]
    all_gather x1, waiting for transfers between devices: 45.8 us -> 16.7 us  [shards(): lax.all_gather(values, 'ctx', axis=0, tiled=True)]
  transfers between devices with their start and end apart: 8 -> 9, of which waited for: 8 -> 7; matrix products, arithmetic and copies ran while one was open for 17% -> 22% of each run, Pallas kernels for 0% -> 0%
where the time goes in v1:
time: 578 us; the launch traced here: 573 us
  waiting for transfers between devices  297 us (51%)
  blocking collectives  113 us (20%)
  matrix products  88 us (15%)
  local copies, waits for them, and re-layouts  34.6 us (6%)
  other arithmetic  17.7 us (3%)
  between operations  16 us (3%)
  starting transfers between devices  6.21 us (1%)
    reduce_scatter x1, waiting for transfers between devices, shards(): lax.psum_scatter(both_terms[:, :feat_dev].astype(jnp.bfloat16), 'ctx', sc...  84.2 us
    all_to_all x2, blocking collectives, to_experts(): recv = lax.all_to_all(rows, 'ctx', split_axis=0, concat_axis=0, tiled=True)  62.1 us
    all_gather x2, waiting for transfers between devices, gather(): full = lax.all_gather(shard, 'grp', axis=0, tiled=True)  56.4 us
    all_gather x1, waiting for transfers between devices, shards(): lax.all_gather(keys, 'ctx', axis=0, tiled=True)  54.3 us
    reduce_scatter x2, waiting for transfers between devices, sum_scatter(): lax.psum_scatter(flat, 'grp', scatter_dimension=0, tiled=True)  52.4 us
    all_to_all x1, blocking collectives, to_tokens(): back = lax.all_to_all(rows, 'ctx', split_axis=0, concat_axis=0, tiled=True)  31.8 us
    reduce_scatter x1, waiting for transfers between devices, shards(): lax.psum_scatter(both_terms[:, feat_dev:].astype(jnp.bfloat16), 'ctx', sc...  27.9 us
    psum x1, blocking collectives, shards(): square_sum = lax.psum(jnp.sum(mixed_f * mixed_f, axis=1), 'grp')  19.5 us
  transfers between devices with their start and end apart: 9, of which 7 were waited for; matrix products, arithmetic and copies ran while one was open for 22% of the time, Pallas kernels for 0%

profile of v1, /device:TPU:0, one launch (start us, length us, event | category | flops | bytes accessed | tf_op | source)
XLA Modules:
  0.0 573.1 jit_solution(17727771724177406112)
XLA Ops:
  17.9 33.6 %all_to_all.20 = bf16[16,96,512]{2,1,0:T(8,128)(2,1)S(1)} all-to-all(bf16[16,96,512]{2,1,0:T(8,128)(2,1)S(1)} %bitcast.112), channel_id=1, replica_groups=mesh['ctx'=16,'grp'=8] {'ctx'}, dimensions={0} | all-to-all | bytes 3145728 | tf_op jit(solution)/shard_map/all_to_all | solution.py:67
  59.5 16.7 %all-gather.7.cloned.1.call-done = bf16[4096,512]{1,0:T(8,128)(2,1)} async-done(((bf16[256,512]{1,0:T(8,128)(2,1)}), bf16[4096,512]{1,0:T(8,128)(2,1)}) %all-gather.7.cloned.1.call-update) | async-done | bytes 4194320 | tf_op jit(solution)/shard_map/all_gather | solution.py:100
  76.2 6.4 %copy.108 = bf16[4096,512]{0,1:T(8,128)(2,1)} copy(bf16[4096,512]{1,0:T(8,128)(2,1)} %all-gather.7.cloned.1.call-done) | data formatting | bytes 8388608 | tf_op jit(solution)/shard_map/all_gather | solution.py:100
  82.6 54.3 %all-gather.5.cloned.1.call-done = bf16[4096,512]{0,1:T(8,128)(2,1)} async-done(((bf16[256,512]{0,1:T(8,128)(2,1)}), bf16[4096,512]{0,1:T(8,128)(2,1)}) %all-gather.5.cloned.1.call-update) | async-done | bytes 4194320 | tf_op jit(solution)/shard_map/all_gather | solution.py:99
  136.9 5.6 fusion.1
  148.3 7.5 %fusion.8 = f32[4,256,128]{1,2,0:T(8,128)} fusion(bf16[4096,4,128]{0,2,1:T(8,128)(2,1)} %bitcast.101, f32[4,256,4096]{2,1,0:T(8,128)S(1)} %get-tuple-element.61, f32[4,256]{1,0:T(4,128)S(1)} %log_add_fusion, pred[256,4096]{1,0:T(8,128)(4,1)S(1)} %copy-done.3), kind=kOutput, calls=%fused_computation.36 | convolution fusion | flops 1090781184 | bytes 22548480 | tf_op jit(solution)/shard_map/hqk,khd->qhd/dot_general | solution.py:108
  159.0 19.5 %psum.7 = f32[256]{0:T(256)S(1)} all-reduce(f32[256]{0:T(256)S(1)} %get-tuple-element.50), channel_id=1, replica_groups=mesh['ctx'=16,'grp'=8] {'grp'}, use_global_device_ids=true, to_apply=%region_8.9 | all-reduce | flops 256 | bytes 2048 | tf_op jit(solution)/shard_map/psum | solution.py:114
  179.2 28.5 %all_to_all.21 = bf16[16,96,512]{2,1,0:T(8,128)(2,1)S(1)} all-to-all(bf16[16,96,512]{2,1,0:T(8,128)(2,1)S(1)} %bitcast.113), channel_id=1, replica_groups=mesh['ctx'=16,'grp'=8] {'ctx'}, dimensions={0} | all-to-all | bytes 3145728 | tf_op jit(solution)/shard_map/all_to_all | solution.py:67
  211.2 5.8 %convolution_convert_fusion.2 = bf16[2,768,1536]{2,1,0:T(8,128)(2,1)} fusion(bf16[2,768,512]{2,1,0:T(8,128)(2,1)} %bitcast.109, bf16[2,512,1536]{2,1,0:T(8,128)(2,1)S(1)} %copy-done), kind=kOutput, calls=%fused_computation.8 | convolution fusion | flops 2418278400 | bytes 9437184 | tf_op jit(solution)/shard_map/erf,efh->erh/dot_general | solution.py:121
  217.0 52.4 %reduce-scatter.7.cloned.1.call-done = bf16[192,1536]{1,0:T(8,128)(2,1)} async-done(((bf16[1536,1536]{1,0:T(8,128)(2,1)}), bf16[192,1536]{1,0:T(8,128)(2,1)}) %reduce-scatter.7.cloned.1.call-update) | async-done | bytes 589840 | tf_op jit(solution)/shard_map/reduce_scatter | solution.py:79
  272.9 56.4 %all-gather.9.cloned.1.call-done = bf16[1536,1536]{1,0:T(8,128)(2,1)} async-done(((bf16[192,1536]{1,0:T(8,128)(2,1)}), bf16[1536,1536]{1,0:T(8,128)(2,1)}) %all-gather.9.cloned.1.call-update) | async-done | bytes 4718608 | tf_op jit(solution)/shard_map/all_gather | solution.py:82
  329.9 5.0 convolution_convert_fusion.8
  335.0 31.8 %all_to_all.22 = bf16[16,96,512]{2,1,0:T(8,128)(2,1)S(1)} all-to-all(bf16[16,96,512]{2,1,0:T(8,128)(2,1)S(1)} %bitcast.96), channel_id=1, replica_groups=mesh['ctx'=16,'grp'=8] {'ctx'}, dimensions={0} | all-to-all | bytes 3145728 | tf_op jit(solution)/shard_map/all_to_all | solution.py:74
  368.1 12.7 %convolution_convert_fusion.1 = bf16[4,128,4096]{2,1,0:T(8,128)(2,1)} fusion(bf16[256,4,128]{0,2,1:T(8,128)(2,1)S(1)} %bitcast.116, f32[4,256,4096]{2,1,0:T(8,128)} %copy-done.2, f32[4,256]{1,0:T(4,128)S(1)} %log_add_fusion, pred[256,4096]{1,0:T(8,128)(4,1)S(1)} %copy-done.4), kind=kOutput, calls=%fused_computation.7 | convolution fusion | flops 1092616192 | bytes 22286336 | tf_op jit(solution)/shard_map/hqk,qhd->khd/dot_general | solution.py:162
  380.8 6.5 %copy.123 = bf16[4096,512]{1,0:T(8,128)(2,1)} copy(bf16[4096,512]{0,1:T(8,128)(2,1)} %bitcast.103) | data formatting | bytes 8388608 | tf_op jit(solution)/shard_map/convert_element_type | solution.py:171
  388.4 12.2 %multiply_convert_fusion = bf16[4,256,4096]{2,1,0:T(8,128)(2,1)S(1)} fusion(f32[4,256,4096]{2,1,0:T(8,128)} %copy-done.2, bf16[256,4,128]{0,2,1:T(8,128)(2,1)S(1)} %bitcast.117, bf16[4096,4,128]{0,2,1:T(8,128)(2,1)} %bitcast.102, f32[4,256]{1,0:T(4,128)S(1)} %bitcast.123, f32[4,256]{1,0:T(4,128)S(1)} %log_add_fusion, pred[256,4096]{1,0:T(8,128)(4,1)S(1)} %copy-done.4), kind=kOutput, calls=%fused_computation | convolution fusion | flops 1103101952 | bytes 30679040 | tf_op jit(solution)/shard_map/qhd,khd->hqk/dot_general | solution.py:152
  405.3 6.5 %copy.122 = bf16[4096,512]{1,0:T(8,128)(2,1)} copy(bf16[4096,512]{0,1:T(8,128)(2,1)} %bitcast.93) | data formatting | bytes 8388608 | tf_op jit(solution)/shard_map/convert_element_type | solution.py:168
  411.9 5.9 %convolution_convert_fusion.9 = bf16[2,768,512]{2,1,0:T(8,128)(2,1)S(1)} fusion(bf16[2,768,1536]{2,1,0:T(8,128)(2,1)} %bitcast.133, bf16[2,1536,512]{2,1,0:T(8,128)(2,1)} %param.18), kind=kOutput, calls=%fused_computation.23 | convolution fusion | flops 2416705536 | bytes 9437184 | tf_op jit(solution)/shard_map/erh,ehf->erf/dot_general | solution.py:135
  419.2 4.9 all-to-all-start.2
  424.1 6.5 %convolution_convert_fusion.5 = bf16[2,512,1536]{2,1,0:T(8,128)(2,1)} fusion(bf16[2,768,512]{2,1,0:T(8,128)(2,1)S(1)} %bitcast.110, bf16[2,768,1536]{2,1,0:T(8,128)(2,1)} %bitcast.132), kind=kOutput, calls=%fused_computation.11 | convolution fusion | flops 2417491968 | bytes 9437184 | tf_op jit(solution)/shard_map/erf,erh->efh/dot_general | solution.py:132
  430.6 6.5 %convolution_convert_fusion.10 = bf16[4,256,128]{1,2,0:T(8,128)(2,1)S(1)} fusion(bf16[4,256,4096]{2,1,0:T(8,128)(2,1)} %copy-done.5, bf16[4096,4,128]{0,2,1:T(8,128)(2,1)S(1)} %bitcast.100), kind=kOutput, calls=%fused_computation.34 | convolution fusion | flops 1073872896 | bytes 12845056 | tf_op jit(solution)/shard_map/hqk,khd->qhd/dot_general | solution.py:156
  438.0 7.3 %convolution_convert_fusion.4 = bf16[2,1536,512]{2,1,0:T(8,128)(2,1)} fusion(bf16[2,768,1536]{2,1,0:T(8,128)(2,1)} %bitcast.134, bf16[2,768,512]{2,1,0:T(8,128)(2,1)} %bitcast.108), kind=kOutput, calls=%fused_computation.10 | convolution fusion | flops 2417491968 | bytes 9437184 | tf_op jit(solution)/shard_map/erh,erf->ehf/dot_general | solution.py:143
  453.4 27.9 %reduce-scatter.11.cloned.1.call-done = bf16[256,512]{1,0:T(8,128)(2,1)} async-done(((bf16[4096,512]{1,0:T(8,128)(2,1)}), bf16[256,512]{1,0:T(8,128)(2,1)}) %reduce-scatter.11.cloned.1.call-update) | async-done | bytes 262160 | tf_op jit(solution)/shard_map/reduce_scatter | solution.py:170
  481.2 84.2 %reduce-scatter.9.cloned.1.call-done = bf16[256,512]{1,0:T(8,128)(2,1)} async-done(((bf16[4096,512]{1,0:T(8,128)(2,1)}), bf16[256,512]{1,0:T(8,128)(2,1)}) %reduce-scatter.9.cloned.1.call-update) | async-done | bytes 262160 | tf_op jit(solution)/shard_map/reduce_scatter | solution.py:167
  (100 shorter events, 52.4 us)
Async XLA Ops:
  8.0 203.2 %copy-start = (bf16[2,512,1536]{2,1,0:T(8,128)(2,1)S(1)}, bf16[2,512,1536]{2,1,0:T(8,128)(2,1)}, u32[]{:S(2)}) copy-start(bf16[2,512,1536]{2,1,0:T(8,128)(2,1)} %param.17) | copy-start | bytes 9437188
  8.0 68.1 %all-gather.7.cloned.1.call-start = ((), (), s32[]{:S(2)}) async-start(), calls=%async_computation.9 | async-start | bytes 4456448 | tf_op jit(solution)/shard_map/all_gather | solution.py:100
  8.7 128.1 %all-gather.5.cloned.1.call-start = ((), (), s32[]{:S(2)}) async-start(), calls=%async_computation.8 | async-start | bytes 4456448 | tf_op jit(solution)/shard_map/all_gather | solution.py:99
  10.8 198.2 %reduce-scatter.5.cloned.1.call-start = ((), (), s32[]{:S(2)}) async-start(), calls=%async_computation.10 | async-start | bytes 5308416 | tf_op jit(solution)/shard_map/reduce_scatter | solution.py:79
  16.8 34.6 %copy-start.11 = (bf16[1536,256]{1,0:T(8,128)(2,1)}, bf16[1536,256]{1,0:T(8,128)(2,1)S(1)}, u32[]{:S(2)}) copy-start(bf16[1536,256]{1,0:T(8,128)(2,1)S(1)} %get-tuple-element.62) | copy-start | bytes 2359300
  16.8 34.6 %copy-start.12 = (bf16[1536,256]{1,0:T(8,128)(2,1)}, bf16[1536,256]{1,0:T(8,128)(2,1)S(1)}, u32[]{:S(2)}) copy-start(bf16[1536,256]{1,0:T(8,128)(2,1)S(1)} %get-tuple-element.63) | copy-start | bytes 2359300
  17.8 33.7 %copy-start.17 = (bf16[2,1536,512]{2,1,0:T(8,128)(2,1)S(1)}, bf16[2,1536,512]{2,1,0:T(8,128)(2,1)}, u32[]{:S(2)}) copy-start(bf16[2,1536,512]{2,1,0:T(8,128)(2,1)} %param.18) | copy-start | bytes 9437188
  51.6 4.3 copy-start.9
  55.9 213.6 %reduce-scatter.7.cloned.1.call-start = ((), (), s32[]{:S(2)}) async-start(), calls=%async_computation.11 | async-start | bytes 5308416 | tf_op jit(solution)/shard_map/reduce_scatter | solution.py:79
  136.9 5.6 copy-start.3
  142.5 5.7 copy-start.2
  217.0 112.3 %all-gather.9.cloned.1.call-start = ((), (), s32[]{:S(2)}) async-start(), calls=%async_computation.12 | async-start | bytes 5308416 | tf_op jit(solution)/shard_map/all_gather | solution.py:82
  272.8 139.1 %all-gather.11.cloned.1.call-start = ((), (), s32[]{:S(2)}) async-start(), calls=%async_computation.13 | async-start | bytes 5308416 | tf_op jit(solution)/shard_map/all_gather | solution.py:82
  329.3 151.9 %reduce-scatter.11.cloned.1.call-start = ((), (), s32[]{:S(2)}) async-start(), calls=%async_computation.15 | async-start | bytes 4456448 | tf_op jit(solution)/shard_map/reduce_scatter | solution.py:170
  334.9 32.0 %copy-start.13 = (bf16[256,512]{1,0:T(8,128)(2,1)S(1)}, bf16[256,512]{1,0:T(8,128)(2,1)}, u32[]{:S(2)}) copy-start(bf16[256,512]{1,0:T(8,128)(2,1)} %param.19) | copy-start | bytes 786436
  366.8 1.2 copy-start.4
  367.5 13.3 %copy-start.15 = (bf16[256,512]{1,0:T(8,128)(2,1)}, bf16[256,512]{1,0:T(8,128)(2,1)S(1)}, u32[]{:S(2)}) copy-start(bf16[256,512]{1,0:T(8,128)(2,1)S(1)} %fusion.7) | copy-start | bytes 786436
  387.3 178.2 %reduce-scatter.9.cloned.1.call-start = ((), (), s32[]{:S(2)}) async-start(), calls=%async_computation.14 | async-start | bytes 4456448 | tf_op jit(solution)/shard_map/reduce_scatter | solution.py:167
  388.4 12.2 %copy-start.7 = (bf16[256,512]{0,1:T(8,128)(2,1)S(1)}, bf16[256,512]{0,1:T(8,128)(2,1)}, u32[]{:S(2)}) copy-start(bf16[256,512]{0,1:T(8,128)(2,1)} %copy.132) | copy-start | bytes 786436
  400.6 4.7 copy-start.5
  417.9 6.2 %copy-start.10 = (bf16[2,16,48,512]{3,2,1,0:T(8,128)(2,1)S(1)}, bf16[2,16,48,512]{3,2,1,0:T(8,128)(2,1)}, u32[]{:S(2)}) copy-start(bf16[2,16,48,512]{3,2,1,0:T(8,128)(2,1)} %copy.114) | copy-start | bytes 4718596
  419.2 30.4 %all-to-all-start.2 = ((bf16[16,96,512]{2,1,0:T(8,128)(2,1)}), bf16[16,96,512]{2,1,0:T(8,128)(2,1)}, u32[]{:S(2)}, u32[]{:S(2)}) async-start(bf16[16,96,512]{2,1,0:T(8,128)(2,1)} %bitcast.24), calls=%async_computation.4 | async-start | bytes 3145728 | tf_op jit(solution)/shard_map/all_to_all | solution.py:74
  424.1 6.6 %copy-start.6 = (bf16[4096,512]{0,1:T(8,128)(2,1)S(1)}, bf16[4096,512]{0,1:T(8,128)(2,1)}, u32[]{:S(2)}) copy-start(bf16[4096,512]{0,1:T(8,128)(2,1)} %all-gather.5.cloned.1.call-done) | copy-start | bytes 12582916
  438.0 127.5 %copy-start.1 = (bf16[2,512,1536]{2,1,0:T(8,128)(2,1)S(1)}, bf16[2,512,1536]{2,1,0:T(8,128)(2,1)}, u32[]{:S(2)}) copy-start(bf16[2,512,1536]{2,1,0:T(8,128)(2,1)} %param.17) | copy-start | bytes 9437188
  (3 other events, 2.7 us)
Sparse Core Ops, SparseCore 0:
  11.3 64.8 all-gather.6
  79.0 57.8 all-gather.4
  387.5 93.7 reduce-scatter.10
  486.3 79.1 reduce-scatter.8
Sparse Core Ops, SparseCore 1:
  56.0 59.1 reduce-scatter.4
  217.1 52.3 reduce-scatter.6
  272.9 56.3 all-gather.8
  330.9 73.1 all-gather.10

commit v2 on v1

--- a/solution.py
+++ b/solution.py
@@ -1,6 +1,8 @@
 import jax
 import jax.numpy as jnp
 from jax import lax
+from jax.experimental import pallas as pl
+from jax.experimental.pallas import tpu as pltpu
 from jax.sharding import PartitionSpec as P
 
 HEAD_DIM = 128
@@ -20,18 +22,349 @@
     )
 
 
-def frame_index(frame_lengths, positions):
-    frame_ends = jnp.cumsum(frame_lengths)
-    return jnp.sum((frame_ends[None, :] <= positions[:, None]).astype(jnp.int32), axis=1)
-
-
-def masked_scores(query_heads, key_heads, key_frames, own_frames, score_scale):
-    scores = (
-        jnp.einsum("qhd,khd->hqk", query_heads, key_heads, preferred_element_type=jnp.float32)
-        * score_scale
-    )
-    allowed = key_frames[None, :] <= own_frames[:, None]
-    return jnp.where(allowed[None, :, :], scores, -jnp.inf)
+MESH_ID = pl.DeviceIdType.MESH
+LOG2E = 1.4426950408889634
+LOW = -1e30
+
+
+def dot_nt(a, b):
+    return lax.dot_general(a, b, (((1,), (1,)), ((), ())), preferred_element_type=jnp.float32)
+
+
+def dot_tn(a, b):
+    return lax.dot_general(a, b, (((0,), (0,)), ((), ())), preferred_element_type=jnp.float32)
+
+
+def dot_nn(a, b):
+    return jnp.dot(a, b, preferred_element_type=jnp.float32)
+
+
+def greet():
+    me = lax.axis_index("ctx")
+    grp = lax.axis_index("grp")
+    barrier = pltpu.get_barrier_semaphore()
+
+    @pl.loop(1, 16)
+    def _(k):
+        pl.semaphore_signal(
+            barrier, inc=1, device_id={"ctx": lax.rem(me + k, 16)}, device_id_type=MESH_ID
+        )
+
+    @pl.loop(1, 8)
+    def _(k):
+        pl.semaphore_signal(
+            barrier, inc=1, device_id={"grp": lax.rem(grp + k, 8)}, device_id_type=MESH_ID
+        )
+
+    pl.semaphore_wait(barrier, 22)
+
+
+def remote(src, dst, send_sem, recv_sem, where):
+    return pltpu.make_async_remote_copy(
+        src_ref=src,
+        dst_ref=dst,
+        send_sem=send_sem,
+        recv_sem=recv_sem,
+        device_id=where,
+        device_id_type=MESH_ID,
+    )
+
+
+def forward_kernel(
+    q_ref, k_ref, v_ref, res_ref, qend_ref, gated_ref, pick_two_ref, pick_both_ref, w_out_ref,
+    attn_ref, lse_ref, mixed_ref, inv_ref, xrecv_ref, grecv_ref, act_grad_ref, kv_out_ref,
+    kv, m_s, l_s, acc_s, gsend, xsend, psend, precv, sq_send, sq_recv,
+    kv_send_sem, kv_recv_sem, out_sem, g_send_sem, g_recv_sem, x_send_sem, x_recv_sem,
+    p_send_sem, p_recv_sem, sq_send_sem, sq_recv_sem,
+):
+    me = lax.axis_index("ctx")
+    grp = lax.axis_index("grp")
+    core = lax.rem(me, 2)
+    chip = me // 2
+    x = lax.rem(chip, 4)
+    yh = chip // 4
+
+    def device(dy, dx, dc):
+        there = lax.rem(yh + dy, 2) * 4 + lax.rem(x + dx, 4)
+        return {"ctx": there * 2 + lax.rem(core + dc, 2)}
+
+    greet()
+
+    copies = {}
+    sent = []
+
+    def move(src, slot, where):
+        copy = remote(src, kv.at[slot], kv_send_sem.at[len(sent)], kv_recv_sem.at[slot], where)
+        copy.start()
+        copies[slot] = copy
+        sent.append(copy)
+
+    def own(which):
+        return k_ref if which == 0 else v_ref
+
+    right, left = device(0, 1, 0), device(0, 3, 0)
+    sibling, partner = device(0, 0, 1), device(1, 0, 0)
+    for which in range(2):
+        move(own(which), (1, 0, 0, which), partner)
+        move(own(which), (0, 3, 0, which), right)
+        move(own(which), (0, 1, 0, which), left)
+        move(own(which), (0, 0, 1, which), sibling)
+    kv[0, 0, 0, 0] = k_ref[...]
+    kv[0, 0, 0, 1] = v_ref[...]
+
+    @pl.loop(0, 16)
+    def _(k):
+        there = lax.rem(me + k, 16)
+        gsend[k] = dot_nn(pick_two_ref[there], gated_ref[...]).astype(jnp.bfloat16)
+
+        @pl.when(k > 0)
+        def _():
+            remote(
+                gsend.at[k], grecv_ref.at[me], g_send_sem.at[k], g_recv_sem.at[k], {"ctx": there}
+            ).start()
+
+    grecv_ref[me] = gsend[0]
+    m_s[...] = jnp.full_like(m_s, LOW)
+    l_s[...] = jnp.zeros_like(l_s)
+    acc_s[...] = jnp.zeros_like(acc_s)
+    outs = []
+
+    def wait_slot(dy, dx, dc, which):
+        copies[(dy, dx, dc, which)].wait_recv()
+
+    def forward(dy, dx, which):
+        wait_slot(dy, dx, 0, which)
+        move(kv.at[dy, dx, 0, which], (dy, dx, 1, which), sibling)
+
+    def relay(dy):
+        forward(dy, 3, 0)
+        move(kv.at[dy, 3, 0, 0], (dy, 2, 0, 0), right)
+        forward(dy, 1, 1)
+        move(kv.at[dy, 1, 0, 1], (dy, 2, 0, 1), left)
+        forward(dy, 3, 1)
+        forward(dy, 1, 0)
+
+    def attend(dy, dx):
+        for which in range(2):
+            wait_slot(dy, dx, 1, which)
+        copy = pltpu.make_async_copy(kv.at[dy, dx], kv_out_ref.at[dy, dx], out_sem.at[dy, dx])
+        copy.start()
+        outs.append(copy)
+        there = lax.rem(yh + dy, 2) * 4 + lax.rem(x + dx, 4)
+        lane = lax.broadcasted_iota(jnp.int32, (256, 256), 1)
+        qend = qend_ref[:, 0:1]
+        limits = [qend - (there * 512 + lax.rem(core + dc, 2) * 256) for dc in range(2)]
+
+        @pl.loop(0, 4)
+        def _(h):
+            cols = pl.ds(pl.multiple_of(h * 128, 128), 128)
+            qh = q_ref[:, cols]
+            scores = []
+            for dc in range(2):
+                s = dot_nt(qh, kv[dy, dx, dc, 0, :, cols]) * (LOG2E * HEAD_DIM**-0.5)
+                scores.append(jnp.where(lane < limits[dc], s, LOW))
+            top = jnp.max(jnp.maximum(scores[0], scores[1]), axis=1, keepdims=True)
+            m_old = m_s[h]
+            m_new = jnp.maximum(m_old, top)
+            alpha = jnp.exp2(m_old - m_new)
+            probs = [jnp.exp2(s - m_new[:, 0:1]) for s in scores]
+            total = jnp.sum(probs[0] + probs[1], axis=1, keepdims=True)
+            m_s[h] = m_new
+            l_s[h] = l_s[h] * alpha + total
+            acc = acc_s[h] * alpha
+            for dc in range(2):
+                acc += dot_nn(probs[dc].astype(jnp.bfloat16), kv[dy, dx, dc, 1, :, cols])
+            acc_s[h] = acc
+
+    attend(0, 0)
+    for which in range(2):
+        wait_slot(1, 0, 0, which)
+        move(kv.at[1, 0, 0, which], (1, 3, 0, which), right)
+        move(kv.at[1, 0, 0, which], (1, 1, 0, which), left)
+        move(kv.at[1, 0, 0, which], (1, 0, 1, which), sibling)
+    relay(0)
+    attend(0, 3)
+    attend(0, 1)
+
+    @pl.loop(1, 16)
+    def _(k):
+        source = lax.rem(me + 16 - k, 16)
+        remote(
+            gsend.at[k], grecv_ref.at[source], g_send_sem.at[k], g_recv_sem.at[k], {"ctx": source}
+        ).wait_recv()
+
+    @pl.loop(0, 8)
+    def _(k):
+        there = lax.rem(grp + k, 8)
+        expert = there // 4
+        first = lax.rem(there, 4) * 4
+        rows = grecv_ref[pl.ds(first, 4), pl.ds(pl.multiple_of(expert * 48, 16), 48), :]
+        rows = rows.reshape(192, 512)
+
+        @pl.loop(0, 3)
+        def _(part):
+            cols = pl.ds(pl.multiple_of(part * 512, 512), 512)
+            psend[k, :, cols] = dot_nt(rows, w_out_ref[expert, cols, :]).astype(jnp.bfloat16)
+
+        @pl.when(k > 0)
+        def _():
+            remote(
+                psend.at[k], precv.at[k], p_send_sem.at[k], p_recv_sem.at[k], {"grp": there}
+            ).start()
+
+    relay(1)
+    attend(1, 0)
+    for which in range(2):
+        forward(0, 2, which)
+    attend(0, 2)
+    attend(1, 3)
+    attend(1, 1)
+    for which in range(2):
+        forward(1, 2, which)
+    attend(1, 2)
+
+    squares = jnp.zeros((256, 1), jnp.float32)
+    for h in range(4):
+        cols = slice(h * 128, h * 128 + 128)
+        out = (acc_s[h] / l_s[h]).astype(jnp.bfloat16)
+        lse_ref[h] = m_s[h] + jnp.log2(l_s[h])
+        attn_ref[:, cols] = out
+        mixed = (res_ref[:, cols].astype(jnp.float32) + out.astype(jnp.float32)).astype(
+            jnp.bfloat16
+        )
+        mixed_ref[:, cols] = mixed
+        mixed_f = mixed.astype(jnp.float32)
+        squares += jnp.sum(mixed_f * mixed_f, axis=1, keepdims=True)
+    turned = jnp.transpose(jnp.broadcast_to(squares, (256, 128)))
+    sq_send[...] = turned[0:8]
+    sq_recv[grp] = turned[0:8]
+
+    @pl.loop(1, 8)
+    def _(k):
+        there = lax.rem(grp + k, 8)
+        remote(
+            sq_send, sq_recv.at[grp], sq_send_sem.at[k], sq_recv_sem.at[k], {"grp": there}
+        ).start()
+
+    @pl.loop(1, 8)
+    def _(k):
+        source = lax.rem(grp + 8 - k, 8)
+        copy = remote(
+            sq_send, sq_recv.at[source], sq_send_sem.at[k], sq_recv_sem.at[k], {"grp": source}
+        )
+        copy.wait_recv()
+        copy.wait_send()
+
+    total = sq_recv[0]
+    for k in range(1, 8):
+        total = total + sq_recv[k]
+    inv = lax.rsqrt(total / 4096 + 1e-06)
+    inv = jnp.transpose(jnp.concatenate([inv] * 16, axis=0))
+    inv_ref[...] = inv
+    normed = jnp.concatenate(
+        [
+            (mixed_ref[:, h * 128 : h * 128 + 128].astype(jnp.float32) * inv).astype(jnp.bfloat16)
+            for h in range(4)
+        ],
+        axis=1,
+    )
+    attn_rows = normed
+
+    @pl.loop(0, 16)
+    def _(k):
+        there = lax.rem(me + k, 16)
+        xsend[k] = dot_nn(pick_both_ref[there], attn_rows).astype(jnp.bfloat16)
+
+        @pl.when(k > 0)
+        def _():
+            remote(
+                xsend.at[k], xrecv_ref.at[me], x_send_sem.at[k], x_recv_sem.at[k], {"ctx": there}
+            ).start()
+
+    xrecv_ref[me] = xsend[0]
+
+    @pl.loop(1, 8)
+    def _(k):
+        source = lax.rem(grp + 8 - k, 8)
+        copy = remote(
+            psend.at[k], precv.at[k], p_send_sem.at[k], p_recv_sem.at[k], {"grp": source}
+        )
+        copy.wait_recv()
+        copy.wait_send()
+
+    @pl.loop(0, 12)
+    def _(part):
+        rows = pl.ds(pl.multiple_of(part * 16, 16), 16)
+        total = psend[0, rows, :].astype(jnp.float32)
+        for k in range(1, 8):
+            total += precv[k, rows, :].astype(jnp.float32)
+        act_grad_ref[rows, :] = total
+
+    @pl.loop(1, 16)
+    def _(k):
+        source = lax.rem(me + 16 - k, 16)
+        copy = remote(
+            gsend.at[k], grecv_ref.at[source], g_send_sem.at[k], g_recv_sem.at[k], {"ctx": source}
+        )
+        copy.wait_send()
+        copy = remote(
+            xsend.at[k], xrecv_ref.at[source], x_send_sem.at[k], x_recv_sem.at[k], {"ctx": source}
+        )
+        copy.wait_recv()
+        copy.wait_send()
+
+    for copy in sent:
+        copy.wait_send()
+    for copy in outs:
+        copy.wait()
+
+
+def forward_call(q, k, v, res, qend, gated, pick_two, pick_both, w_out):
+    bf, f32 = jnp.bfloat16, jnp.float32
+    vmem = pl.BlockSpec(memory_space=pltpu.VMEM)
+    shape = jax.ShapeDtypeStruct
+    return pl.pallas_call(
+        forward_kernel,
+        out_shape=(
+            shape((256, 512), bf),
+            shape((4, 256, 128), f32),
+            shape((256, 512), bf),
+            shape((256, 128), f32),
+            shape((16, 96, 512), bf),
+            shape((16, 96, 512), bf),
+            shape((192, 1536), f32),
+            shape((2, 4, 2, 2, 256, 512), bf),
+        ),
+        in_specs=[vmem] * 9,
+        out_specs=[vmem] * 7 + [pl.BlockSpec(memory_space=pl.ANY)],
+        scratch_shapes=[
+            pltpu.VMEM((2, 4, 2, 2, 256, 512), bf),
+            pltpu.VMEM((4, 256, 128), f32),
+            pltpu.VMEM((4, 256, 128), f32),
+            pltpu.VMEM((4, 256, 128), f32),
+            pltpu.VMEM((16, 96, 512), bf),
+            pltpu.VMEM((16, 96, 512), bf),
+            pltpu.VMEM((8, 192, 1536), bf),
+            pltpu.VMEM((8, 192, 1536), bf),
+            pltpu.VMEM((8, 256), f32),
+            pltpu.VMEM((8, 8, 256), f32),
+            pltpu.SemaphoreType.DMA((30,)),
+            pltpu.SemaphoreType.DMA((2, 4, 2, 2)),
+            pltpu.SemaphoreType.DMA((2, 4)),
+            pltpu.SemaphoreType.DMA((16,)),
+            pltpu.SemaphoreType.DMA((16,)),
+            pltpu.SemaphoreType.DMA((16,)),
+            pltpu.SemaphoreType.DMA((16,)),
+            pltpu.SemaphoreType.DMA((8,)),
+            pltpu.SemaphoreType.DMA((8,)),
+            pltpu.SemaphoreType.DMA((8,)),
+            pltpu.SemaphoreType.DMA((8,)),
+        ],
+        compiler_params=pltpu.CompilerParams(
+            collective_id=0, has_side_effects=True, vmem_limit_bytes=56 * 2**20
+        ),
+        name="forward",
+    )(q, k, v, res, qend, gated, pick_two, pick_both, w_out)
 
 
 def shards(
@@ -86,37 +419,33 @@
     gated = jnp.concatenate(
         [(route_gates[:, a : a + 1] * out_grad_f).astype(jnp.bfloat16) for a in range(2)], axis=0
     )
-    grad_rows = jnp.dot(pick_two, gated, preferred_element_type=jnp.float32).astype(jnp.bfloat16)
-    grads_recv = to_experts(grad_rows)
-    act_grad = sum_scatter(
-        jnp.einsum("erf,ehf->erh", grads_recv, w_out, preferred_element_type=jnp.float32)
-    )
     ctx_index = lax.axis_index("ctx")
-    frames = frame_index(frame_lengths, jnp.arange(seq_len, dtype=jnp.int32))
-    own_frames = lax.dynamic_slice_in_dim(frames, ctx_index * tok_rows, tok_rows)
-    query_heads = queries.reshape(tok_rows, heads_dev, head_dim)
-    keys_all, values_all = (
-        lax.all_gather(keys, "ctx", axis=0, tiled=True),
-        lax.all_gather(values, "ctx", axis=0, tiled=True),
-    )
-    key_heads_all = keys_all.reshape(seq_len, heads_dev, head_dim)
-    value_heads_all = values_all.reshape(seq_len, heads_dev, head_dim)
-    scores = masked_scores(query_heads, key_heads_all, frames, own_frames, score_scale)
-    row_max = jnp.max(scores, axis=2, keepdims=True)
-    log_total = row_max + jnp.log(jnp.sum(jnp.exp(scores - row_max), axis=2, keepdims=True))
-    prob = jnp.exp(scores - log_total).astype(jnp.bfloat16)
-    attn_heads = jnp.einsum(
-        "hqk,khd->qhd", prob, value_heads_all, preferred_element_type=jnp.float32
-    ).astype(jnp.bfloat16)
-    attn = attn_heads.reshape(tok_rows, feat_dev)
-    mixed = (residual.astype(jnp.float32) + attn.astype(jnp.float32)).astype(jnp.bfloat16)
+    frame_ends = jnp.cumsum(frame_lengths)
+    positions = ctx_index * tok_rows + jnp.arange(tok_rows, dtype=jnp.int32)
+    ends = jnp.min(
+        jnp.where(frame_ends[None, :] > positions[:, None], frame_ends[None, :], seq_len), axis=1
+    )
+    qend = jnp.broadcast_to(ends[:, None], (tok_rows, 128)).astype(jnp.int32)
+    attn, lse, mixed, inv_wide, rows_recv, grads_recv, act_grad, kv_all = forward_call(
+        queries,
+        keys,
+        values,
+        residual,
+        qend,
+        gated,
+        pick_two.reshape(n_ctx, exp_dev * capacity, 2 * tok_rows),
+        pick_both.reshape(n_ctx, exp_dev * capacity, tok_rows),
+        w_out,
+    )
     mixed_f = mixed.astype(jnp.float32)
-    square_sum = lax.psum(jnp.sum(mixed_f * mixed_f, axis=1), "grp")
-    inv_rms = lax.rsqrt(square_sum / width_all + 1e-06)
-    normed = (mixed_f * inv_rms[:, None]).astype(jnp.bfloat16)
-    norm_rows = jnp.dot(pick_both, normed, preferred_element_type=jnp.float32).astype(jnp.bfloat16)
-    rows_recv = to_experts(norm_rows)
-    rows_recv, act_grad = lax.optimization_barrier((rows_recv, act_grad))
+    inv_rms = inv_wide[:, 0]
+    attn_heads = attn.reshape(tok_rows, heads_dev, head_dim)
+
+    def by_expert(rows):
+        rows = rows.reshape(n_ctx, exp_dev, capacity, feat_dev)
+        return rows.transpose(1, 0, 2, 3).reshape(exp_dev, n_ctx * capacity, feat_dev)
+
+    rows_recv, grads_recv = by_expert(rows_recv), by_expert(grads_recv)
     pre_act = sum_scatter(
         jnp.einsum("erf,efh->erh", rows_recv, w_in, preferred_element_type=jnp.float32)
     )
@@ -147,6 +476,25 @@
     input_grad = input_grad_f.astype(jnp.bfloat16)
     grad_heads = input_grad.reshape(tok_rows, heads_dev, head_dim)
     row_dot = jnp.sum(grad_heads.astype(jnp.float32) * attn_heads.astype(jnp.float32), axis=2).T
+    core, chip = ctx_index % 2, ctx_index // 2
+    chip_y, chip_x = chip // 4, chip % 4
+    there = [
+        ((chip_y + dy) % 2 * 4 + (chip_x + dx) % 4) * 2 + (core + dc) % 2
+        for dy in range(2)
+        for dx in range(4)
+        for dc in range(2)
+    ]
+    there = jnp.stack(there)
+    key_pos = (there[:, None] * tok_rows + jnp.arange(tok_rows)[None, :]).reshape(-1)
+    key_heads_all = kv_all[:, :, :, 0].reshape(seq_len, heads_dev, head_dim)
+    value_heads_all = kv_all[:, :, :, 1].reshape(seq_len, heads_dev, head_dim)
+    query_heads = queries.reshape(tok_rows, heads_dev, head_dim)
+    scores = (
+        jnp.einsum("qhd,khd->hqk", query_heads, key_heads_all, preferred_element_type=jnp.float32)
+        * score_scale
+    )
+    scores = jnp.where((key_pos[None, :] < ends[:, None])[None], scores, -jnp.inf)
+    log_total = lse[:, :, 0:1] / LOG2E
     prob_f = jnp.exp(scores - log_total)
     prob_all = prob_f.astype(jnp.bfloat16)
     dprob = jnp.einsum(
@@ -163,6 +511,10 @@
         "hqk,qhd->khd", prob_all, grad_heads, preferred_element_type=jnp.float32
     ).reshape(seq_len, feat_dev)
     both_terms = jnp.concatenate([key_term, value_term], axis=1)
+    both_terms = both_terms.reshape(n_ctx, tok_rows, 2 * feat_dev)
+    both_terms = (
+        jnp.zeros_like(both_terms).at[there].set(both_terms).reshape(seq_len, 2 * feat_dev)
+    )
     key_grad_f, value_grad_f = (
         lax.psum_scatter(
             both_terms[:, :feat_dev].astype(jnp.bfloat16), "ctx", scatter_dimension=0, tiled=True

time: 578 us -> 643 us (1.11)
  Pallas kernels: 0 us -> 144 us
  blocking collectives: 113 us -> 0 us
  local copies, waits for them, and re-layouts: 34.6 us -> 130 us
  waiting for transfers between devices: 297 us -> 222 us
  other arithmetic: 17.7 us -> 32.2 us
  matrix products: 88 us -> 79.7 us
    pallas_call x0 -> x1, Pallas kernels: none -> 144 us  [forward_call(): pl.pallas_call(forward_kernel, out_shape=(shape((256, 512), bf), shape((4...]
    all_to_all x3 -> x0, blocking collectives: 93.9 us -> none  [the longest x2 62.1 us: to_experts(): recv = lax.all_to_all(rows, 'ctx', split_axis=0, concat_axis=0, tiled=True)]
    all_gather x2 -> x0, waiting for transfers between devices: 70.9 us -> none  [the longest x1 54.3 us: shards(): lax.all_gather(keys, 'ctx', axis=0, tiled=True)]
    all_gather x2, waiting for transfers between devices: 56.4 us -> 25.8 us  [gather(): full = lax.all_gather(shard, 'grp', axis=0, tiled=True)]
    scatter x0 -> x1, local copies, waits for them, and re-layouts: none -> 30.1 us  [shards(): jnp.zeros_like(both_terms).at[there].set(both_terms)]
    another operation x2 -> x7, local copies, waits for them, and re-layouts: 0.09 us -> 22.4 us  [the longest x2 14.6 us: shards(): key_heads_all = kv_all[:, :, :, 0].reshape(seq_len, heads_dev, head_dim)]
    psum x1 -> x0, blocking collectives: 19.5 us -> none  [shards(): square_sum = lax.psum(jnp.sum(mixed_f * mixed_f, axis=1), 'grp')]
    concatenate x0 -> x1, local copies, waits for them, and re-layouts: none -> 16.6 us  [shards(): both_terms = jnp.concatenate([key_term, value_term], axis=1)]
  transfers between devices with their start and end apart: 9 -> 7, of which waited for: 7 -> 6; matrix products, arithmetic and copies ran while one was open for 22% -> 34% of each run, Pallas kernels for 0% -> 0%
where the time goes in v2:
time: 643 us; the launch traced here: 634 us
  waiting for transfers between devices  222 us (35%)
  Pallas kernels  144 us (22%)
  local copies, waits for them, and re-layouts  130 us (20%)
  matrix products  79.7 us (12%)
  other arithmetic  32.2 us (5%)
  between operations  14.6 us (2%)
  starting transfers between devices  11.9 us (2%)
    pallas_call x1, Pallas kernels, forward_call(): pl.pallas_call(forward_kernel, out_shape=(shape((256, 512), bf), shape((4...  144 us
    reduce_scatter x1, waiting for transfers between devices, shards(): lax.psum_scatter(both_terms[:, :feat_dev].astype(jnp.bfloat16), 'ctx', sc...  84.2 us
    reduce_scatter x1, waiting for transfers between devices, sum_scatter(): lax.psum_scatter(flat, 'grp', scatter_dimension=0, tiled=True)  60.8 us
    reduce_scatter x1, waiting for transfers between devices, shards(): lax.psum_scatter(both_terms[:, feat_dev:].astype(jnp.bfloat16), 'ctx', sc...  32.1 us
    scatter x1, local copies, waits for them, and re-layouts, shards(): jnp.zeros_like(both_terms).at[there].set(both_terms)  30.1 us
    all_gather x2, waiting for transfers between devices, gather(): full = lax.all_gather(shard, 'grp', axis=0, tiled=True)  25.8 us
    unnamed x45, local copies, waits for them, and re-layouts  23.3 us
    all_to_all x2, waiting for transfers between devices, to_tokens(): back = lax.all_to_all(rows, 'ctx', split_axis=0, concat_axis=0, tiled=True)  18.6 us
  transfers between devices with their start and end apart: 7, of which 6 were waited for; matrix products, arithmetic and copies ran while one was open for 34% of the time, Pallas kernels for 0%

profile of v2, /device:TPU:0, one launch (start us, length us, event | category | flops | bytes accessed | tf_op | source)
XLA Modules:
  0.0 634.1 jit_solution(17034256786332673033)
XLA Ops:
  20.8 143.7 %forward.1 = (bf16[256,512]{1,0:T(8,128)(2,1)}, f32[4,256,128]{2,1,0:T(8,128)}, bf16[256,512]{1,0:T(8,128)(2,1)}, f32[256,128]{1,0:T(8,128)}, bf16[16,96,512]{2,...) custom-call(bf16[256,512]{1,0:T(8,128)(2,1)} %q_ref.1, ...), custom_call_target="tpu_custom_call" | custom-call | tf_op jit(solution)/shard_map/forward/pallas_call | solution.py:326
  170.4 60.8 %reduce-scatter.4.cloned.1.call-done = bf16[192,1536]{1,0:T(8,128)(2,1)} async-done(((bf16[1536,1536]{1,0:T(8,128)(2,1)}), bf16[192,1536]{1,0:T(8,128)(2,1)}) %reduce-scatter.4.cloned.1.call-update) | async-done | bytes 589840 | tf_op jit(solution)/shard_map/reduce_scatter | solution.py:412
  236.3 5.9 fusion.52
  242.2 6.9 %reshape_squeeze.7 = bf16[4096,4,128]{2,1,0:T(4,128)(2,1)} reshape(bf16[2,4,2,1,256,512]{5,4,3,2,1,0:T(8,128)(2,1)} %get-tuple-element.71) | data formatting | bytes 8388608 | tf_op jit(solution)/shard_map/reshape;squeeze | solution.py:490
  249.2 7.0 %reshape_squeeze.6 = bf16[4096,4,128]{2,1,0:T(4,128)(2,1)} reshape(bf16[2,4,2,1,256,512]{5,4,3,2,1,0:T(8,128)(2,1)} %get-tuple-element.72) | data formatting | bytes 8388608 | tf_op jit(solution)/shard_map/reshape;squeeze | solution.py:489
  256.1 7.6 %copy.149 = bf16[4096,4,128]{0,2,1:T(8,128)(2,1)} copy(bf16[4096,4,128]{2,1,0:T(4,128)(2,1)} %reshape_squeeze.6) | data formatting | bytes 8388608 | tf_op jit(solution)/shard_map/reshape;squeeze | solution.py:489
  265.2 25.8 %all-gather.3.cloned.1.call-done = bf16[1536,1536]{1,0:T(8,128)(2,1)} async-done(((bf16[192,1536]{1,0:T(8,128)(2,1)}), bf16[1536,1536]{1,0:T(8,128)(2,1)}) %all-gather.3.cloned.1.call-update) | async-done | bytes 4718608 | tf_op jit(solution)/shard_map/all_gather | solution.py:415
  297.4 6.6 %all-to-all-start.1 = ((bf16[16,96,512]{2,1,0:T(8,128)(2,1)}), bf16[16,96,512]{2,1,0:T(8,128)(2,1)}, u32[]{:S(2)}, u32[]{:S(2)}) async-start(bf16[16,96,512]{2,1,0:T(8,128)(2,1)} %bitcast.18), calls=%async_computation.2 | async-start | bytes 3145728 | tf_op jit(solution)/shard_map/all_to_all | solution.py:407
  304.0 10.3 %fusion.36 = f32[4,4096,256]{2,1,0:T(8,128)} fusion(bf16[4096,4,128]{0,2,1:T(8,128)(2,1)} %copy.149, bf16[256,512]{1,0:T(8,128)(2,1)S(1)} %copy-done.4), kind=kOutput, calls=%fused_computation.67 | convolution fusion | flops 1073741824 | bytes 21233664 | tf_op jit(solution)/shard_map/qhd,khd->hqk/dot_general | solution.py:493
  316.2 13.3 %all-to-all-done.1 = bf16[16,96,512]{2,1,0:T(8,128)(2,1)} async-done(((bf16[16,96,512]{2,1,0:T(8,128)(2,1)}), bf16[16,96,512]{2,1,0:T(8,128)(2,1)}, u32[]{:S(2)}, u32[]{:S(2)}) %all-to-all-start.1) | async-done | bytes 1572896 | tf_op jit(solution)/shard_map/all_to_all | solution.py:407
  332.2 11.4 %multiply_convert_fusion = bf16[4,256,4096]{1,2,0:T(8,128)(2,1)S(1)} fusion(f32[4,4096,256]{2,1,0:T(8,128)} %fusion.36, bf16[256,4,128]{0,2,1:T(8,128)(2,1)S(1)} %copy.153, f32[4,256]{1,0:T(4,128)S(1)} %copy.147, f32[4,256]{1,0:T(4,128)S(1)} %multiply_reduce_fusion.1, pred[256,4096]{0,1:T(8,128)(4,1)S(1)} %broadcast_compare_fusion, ...), kind=kOutput, calls=%fused_computation.5 | convolution fusion | flops 1103101952 | bytes 30679040 | tf_op jit(solution)/shard_map/qhd,khd->hqk/dot_general | solution.py:500
  352.5 9.1 %copy.152 = f32[4096,4,128]{0,2,1:T(8,128)} copy(f32[4096,4,128]{2,0,1:T(8,128)} %convolution_bitcast_fusion) | data formatting | bytes 16777216 | tf_op jit(solution)/shard_map/hqk,qhd->khd/transpose | solution.py:507
  361.6 10.5 %copy.168 = f32[64,8,16,256]{3,2,1,0:T(8,128)} copy(f32[64,8,16,256]{3,1,2,0:T(8,128)} %bitcast.148) | data formatting | bytes 16777216
  372.1 13.7 %fusion.3 = f32[4,128,4096]{2,1,0:T(8,128)} fusion(bf16[256,4,128]{0,2,1:T(8,128)(2,1)S(1)} %copy.153, f32[4,4096,256]{2,1,0:T(8,128)} %fusion.36, f32[4,256]{1,0:T(4,128)S(1)} %multiply_reduce_fusion.1, pred[256,4096]{0,1:T(8,128)(4,1)S(1)} %broadcast_compare_fusion), kind=kOutput, calls=%fused_computation.7 | convolution fusion | flops 1090519040 | bytes 26480640 | tf_op jit(solution)/shard_map/hqk,qhd->khd/dot_general | solution.py:510
  385.8 7.7 %copy.169 = f32[64,8,16,256]{3,2,1,0:T(8,128)S(1)} copy(f32[64,8,16,256]{3,1,2,0:T(8,128)} %bitcast.147) | data formatting | bytes 16777216
  393.5 6.7 %pad_maximum_fusion = f32[16,256,1024]{1,0,2:T(8,128)} fusion(f32[16,256,512]{1,0,2:T(8,128)S(1)} %bitcast.152, f32[16,256,512]{1,0,2:T(8,128)S(1)} %bitcast.151), kind=kLoop, calls=%fused_computation.1 | loop fusion | flops 4194304 | bytes 33554432 | tf_op jit(solution)/shard_map/concatenate | solution.py:513
  400.2 16.6 %copy.155 = f32[16,256,1024]{2,1,0:T(8,128)} copy(f32[16,256,1024]{1,0,2:T(8,128)} %pad_maximum_fusion) | data formatting | bytes 33554432 | tf_op jit(solution)/shard_map/concatenate | solution.py:513
  416.8 7.9 %broadcast_in_dim.26 = f32[16,256,1024]{2,1,0:T(8,128)} broadcast(f32[]{:T(128)} %constant.205.clone.1), dimensions={} | broadcast | bytes 16777220 | tf_op jit(solution)/shard_map/broadcast_in_dim | solution.py:516
  424.7 30.1 %scatter_fusion = f32[16,256,1024]{2,1,0:T(8,128)} fusion(f32[16,256,1024]{2,1,0:T(8,128)} %broadcast_in_dim.26, s32[16]{0:T(128)S(1)} %fusion.47, f32[16,256,1024]{2,1,0:T(8,128)} %copy.155), kind=kCustom, calls=%fused_computation | custom fusion | bytes 50331712 | tf_op jit(solution)/shard_map/scatter | solution.py:516
  454.8 6.6 %convert.6 = bf16[16,256,1024]{2,1,0:T(8,128)(2,1)S(1)} convert(f32[16,256,1024]{2,1,0:T(8,128)} %scatter_fusion) | non-fusion elementwise | flops 4194304 | bytes 25165824 | tf_op jit(solution)/shard_map/convert.2
  481.7 6.8 %convolution_convert_fusion.2 = bf16[2,512,1536]{2,1,0:T(8,128)(2,1)} fusion(bf16[2,768,512]{2,1,0:T(8,128)(2,1)S(1)} %bitcast.155, bf16[2,768,1536]{2,1,0:T(8,128)(2,1)} %bitcast.178), kind=kOutput, calls=%fused_computation.16 | convolution fusion | flops 2417491968 | bytes 9437184 | tf_op jit(solution)/shard_map/erf,erh->efh/dot_general | solution.py:461
  494.0 7.8 %convolution_convert_fusion.1 = bf16[2,1536,512]{2,1,0:T(8,128)(2,1)} fusion(bf16[2,768,1536]{2,1,0:T(8,128)(2,1)} %bitcast.180, bf16[2,768,512]{2,1,0:T(8,128)(2,1)} %bitcast.157), kind=kOutput, calls=%fused_computation.15 | convolution fusion | flops 2417491968 | bytes 9437184 | tf_op jit(solution)/shard_map/erh,erf->ehf/dot_general | solution.py:472
  511.0 32.1 %reduce-scatter.8.cloned.1.call-done = bf16[256,512]{1,0:T(8,128)(2,1)} async-done(((bf16[4096,512]{1,0:T(8,128)(2,1)}), bf16[256,512]{1,0:T(8,128)(2,1)}) %reduce-scatter.8.cloned.1.call-update) | async-done | bytes 262160 | tf_op jit(solution)/shard_map/reduce_scatter | solution.py:522
  543.1 84.2 %reduce-scatter.6.cloned.1.call-done = bf16[256,512]{1,0:T(8,128)(2,1)} async-done(((bf16[4096,512]{1,0:T(8,128)(2,1)}), bf16[256,512]{1,0:T(8,128)(2,1)}) %reduce-scatter.6.cloned.1.call-update) | async-done | bytes 262160 | tf_op jit(solution)/shard_map/reduce_scatter | solution.py:519
  (110 shorter events, 80.4 us)
Async XLA Ops:
  7.2 158.8 %copy-start = (bf16[2,512,1536]{2,1,0:T(8,128)(2,1)S(1)}, bf16[2,512,1536]{2,1,0:T(8,128)(2,1)}, u32[]{:S(2)}) copy-start(bf16[2,512,1536]{2,1,0:T(8,128)(2,1)} %param.17) | copy-start | bytes 9437188
  7.2 224.0 %reduce-scatter.4.cloned.1.call-start = ((), (), s32[]{:S(2)}) async-start(), calls=%async_computation.5 | async-start | bytes 5308416 | tf_op jit(solution)/shard_map/reduce_scatter | solution.py:412
  14.5 150.0 %copy-start.14 = (f32[256,1]{0,1:T(1,128)}, f32[256,1]{0,1:T(1,128)S(1)}, u32[]{:S(2)}) copy-start(f32[256,1]{0,1:T(1,128)S(1)} %get-tuple-element.81) | copy-start | bytes 3076
  14.5 150.0 %copy-start.16 = (f32[256,1]{0,1:T(1,128)}, f32[256,1]{0,1:T(1,128)S(1)}, u32[]{:S(2)}) copy-start(f32[256,1]{0,1:T(1,128)S(1)} %get-tuple-element.82) | copy-start | bytes 3076
  170.3 65.1 %copy-start.10 = (bf16[256,512]{1,0:T(8,128)(2,1)S(1)}, bf16[256,512]{1,0:T(8,128)(2,1)}, u32[]{:S(2)}) copy-start(bf16[256,512]{1,0:T(8,128)(2,1)} %get-tuple-element.25) | copy-start | bytes 786436
  170.3 120.8 %all-gather.3.cloned.1.call-start = ((), (), s32[]{:S(2)}) async-start(), calls=%async_computation.6 | async-start | bytes 5308416 | tf_op jit(solution)/shard_map/all_gather | solution.py:415
  234.5 236.0 %all-gather.5.cloned.1.call-start = ((), (), s32[]{:S(2)}) async-start(), calls=%async_computation.7 | async-start | bytes 5308416 | tf_op jit(solution)/shard_map/all_gather | solution.py:415
  256.1 7.7 %copy-start.13 = (f32[256,128]{1,0:T(8,128)S(1)}, f32[256,128]{1,0:T(8,128)}, u32[]{:S(2)}) copy-start(f32[256,128]{1,0:T(8,128)} %get-tuple-element.21) | copy-start | bytes 393220
  296.1 7.9 %copy-start.4 = (bf16[256,512]{1,0:T(8,128)(2,1)S(1)}, bf16[256,512]{1,0:T(8,128)(2,1)}, u32[]{:S(2)}) copy-start(bf16[256,512]{1,0:T(8,128)(2,1)} %q_ref.1) | copy-start | bytes 786436
  297.4 32.1 %all-to-all-start.1 = ((bf16[16,96,512]{2,1,0:T(8,128)(2,1)}), bf16[16,96,512]{2,1,0:T(8,128)(2,1)}, u32[]{:S(2)}, u32[]{:S(2)}) async-start(bf16[16,96,512]{2,1,0:T(8,128)(2,1)} %bitcast.18), calls=%async_computation.2 | async-start | bytes 3145728 | tf_op jit(solution)/shard_map/all_to_all | solution.py:407
  303.9 25.6 %copy-start.9 = (bf16[256,512]{1,0:T(8,128)(2,1)S(1)}, bf16[256,512]{1,0:T(8,128)(2,1)}, u32[]{:S(2)}) copy-start(bf16[256,512]{1,0:T(8,128)(2,1)} %param.19) | copy-start | bytes 786436
  303.9 239.1 %reduce-scatter.8.cloned.1.call-start = ((), (), s32[]{:S(2)}) async-start(), calls=%async_computation.9 | async-start | bytes 4456448 | tf_op jit(solution)/shard_map/reduce_scatter | solution.py:522
  314.3 17.5 %copy-start.6 = (f32[256,4,128]{2,1,0:T(4,128)S(1)}, f32[256,4,128]{2,1,0:T(4,128)}, u32[]{:S(2)}) copy-start(f32[256,4,128]{2,1,0:T(4,128)} %reshape.972) | copy-start | bytes 1572868
  331.5 12.1 %copy-start.11 = (bf16[256,512]{1,0:T(8,128)(2,1)}, bf16[256,512]{1,0:T(8,128)(2,1)S(1)}, u32[]{:S(2)}) copy-start(bf16[256,512]{1,0:T(8,128)(2,1)S(1)} %fusion.19) | copy-start | bytes 786436
  385.8 7.7 %slice-start = ((s8[8388608]{0:T(1024)(128)(4,1)}), s8[4194304]{0:T(1024)(128)(4,1)S(1)}, s32[]{:S(2)}) async-start(s8[8388608]{0:T(1024)(128)(4,1)} %bitcast.149), calls=%async_computation.10 | async-start | bytes 8388608
  385.8 7.7 %slice-start.1 = ((s8[8388608]{0:T(1024)(128)(4,1)}), s8[4194304]{0:T(1024)(128)(4,1)S(1)}, s32[]{:S(2)}) async-start(s8[8388608]{0:T(1024)(128)(4,1)} %bitcast.149), calls=%async_computation.11 | async-start | bytes 8388608
  465.2 162.1 %reduce-scatter.6.cloned.1.call-start = ((), (), s32[]{:S(2)}) async-start(), calls=%async_computation.8 | async-start | bytes 4456448 | tf_op jit(solution)/shard_map/reduce_scatter | solution.py:519
  475.7 6.0 copy-start.8
  477.0 30.2 %all-to-all-start = ((bf16[16,96,512]{2,1,0:T(8,128)(2,1)}), bf16[16,96,512]{2,1,0:T(8,128)(2,1)}, u32[]{:S(2)}, u32[]{:S(2)}) async-start(bf16[16,96,512]{2,1,0:T(8,128)(2,1)} %bitcast.14), calls=%async_computation.1 | async-start | bytes 3145728 | tf_op jit(solution)/shard_map/all_to_all | solution.py:407
  481.7 6.8 %copy-start.2 = (bf16[4096,4,128]{0,2,1:T(8,128)(2,1)S(1)}, bf16[4096,4,128]{0,2,1:T(8,128)(2,1)}, u32[]{:S(2)}) copy-start(bf16[4096,4,128]{0,2,1:T(8,128)(2,1)} %copy.149) | copy-start | bytes 12582916
  494.0 133.3 %copy-start.1 = (bf16[2,512,1536]{2,1,0:T(8,128)(2,1)S(1)}, bf16[2,512,1536]{2,1,0:T(8,128)(2,1)}, u32[]{:S(2)}) copy-start(bf16[2,512,1536]{2,1,0:T(8,128)(2,1)} %param.17) | copy-start | bytes 9437188
  501.8 8.3 %copy-start.12 = (bf16[256,512]{1,0:T(8,128)(2,1)S(1)}, bf16[256,512]{1,0:T(8,128)(2,1)}, u32[]{:S(2)}) copy-start(bf16[256,512]{1,0:T(8,128)(2,1)} %get-tuple-element.17) | copy-start | bytes 786436
  501.8 8.3 %copy-start.15 = (f32[256,1]{0,1:T(1,128)S(1)}, f32[256,1]{0,1:T(1,128)}, u32[]{:S(2)}) copy-start(f32[256,1]{0,1:T(1,128)} %copy-done.14) | copy-start | bytes 3076
  501.9 8.3 %copy-start.17 = (f32[256,1]{0,1:T(1,128)S(1)}, f32[256,1]{0,1:T(1,128)}, u32[]{:S(2)}) copy-start(f32[256,1]{0,1:T(1,128)} %copy-done.16) | copy-start | bytes 3076
  (3 other events, 12.7 us)
Sparse Core Ops, SparseCore 0:
  170.4 60.7 reduce-scatter.3
  234.6 56.4 all-gather.2
  292.7 73.1 all-gather.4
  465.3 77.7 reduce-scatter.7
  548.1 79.1 reduce-scatter.5

commit v3 on v2

--- a/solution.py
+++ b/solution.py
@@ -227,7 +227,7 @@
     for h in range(4):
         cols = slice(h * 128, h * 128 + 128)
         out = (acc_s[h] / l_s[h]).astype(jnp.bfloat16)
-        lse_ref[h] = m_s[h] + jnp.log2(l_s[h])
+        lse_ref[h] = jnp.transpose(m_s[h] + jnp.log2(l_s[h]))[0:8]
         attn_ref[:, cols] = out
         mixed = (res_ref[:, cols].astype(jnp.float32) + out.astype(jnp.float32)).astype(
             jnp.bfloat16
@@ -327,7 +327,7 @@
         forward_kernel,
         out_shape=(
             shape((256, 512), bf),
-            shape((4, 256, 128), f32),
+            shape((4, 8, 256), f32),
             shape((256, 512), bf),
             shape((256, 128), f32),
             shape((16, 96, 512), bf),
@@ -367,6 +367,232 @@
     )(q, k, v, res, qend, gated, pick_two, pick_both, w_out)
 
 
+def backward_kernel(
+    q_ref, kv_ref, lse_ref, attn_ref, qend_ref, og_ref, inv_ref, pick_ref, rg_ref,
+    ig_ref, dq_ref, dk_ref, dv_ref,
+    rg_recv, normed_grad, row_dot, dqt, own_terms, sib_send, sib_recv, ring_send,
+    ring_recv, part_send, part_recv,
+    rg_send_sem, rg_recv_sem, sib_send_sem, sib_recv_sem, ring_send_sem, ring_recv_sem,
+    part_send_sem, part_recv_sem,
+):
+    me = lax.axis_index("ctx")
+    core = lax.rem(me, 2)
+    chip = me // 2
+    x = lax.rem(chip, 4)
+    yh = chip // 4
+    bf, f32 = jnp.bfloat16, jnp.float32
+
+    def device(dy, dx, dc):
+        there = lax.rem(yh + dy, 2) * 4 + lax.rem(x + dx, 4)
+        return {"ctx": there * 2 + lax.rem(core + dc, 2)}
+
+    right, left = device(0, 1, 0), device(0, 3, 0)
+    sibling, partner = device(0, 0, 1), device(1, 0, 0)
+    greet_ctx()
+
+    @pl.loop(1, 16)
+    def _(k):
+        there = lax.rem(me + k, 16)
+        remote(
+            rg_ref.at[there], rg_recv.at[k], rg_send_sem.at[k], rg_recv_sem.at[k], {"ctx": there}
+        ).start()
+
+    dqt[...] = jnp.zeros_like(dqt)
+    normed_grad[...] = dot_tn(pick_ref[me], rg_ref[me])
+
+    @pl.loop(1, 16)
+    def _(k):
+        source = lax.rem(me + 16 - k, 16)
+        remote(
+            rg_ref.at[source], rg_recv.at[k], rg_send_sem.at[k], rg_recv_sem.at[k], {"ctx": source}
+        ).wait_recv()
+        normed_grad[...] += dot_tn(pick_ref[source], rg_recv[k])
+
+    for h in range(4):
+        cols = slice(h * 128, h * 128 + 128)
+        grad = og_ref[:, cols].astype(f32) + inv_ref[...] * normed_grad[:, cols]
+        grad = grad.astype(bf)
+        ig_ref[:, cols] = grad
+        dots = jnp.sum(grad.astype(f32) * attn_ref[:, cols].astype(f32), axis=1, keepdims=True)
+        row_dot[h] = jnp.transpose(jnp.broadcast_to(dots, (256, 128)))[0:8]
+
+    scale = HEAD_DIM**-0.5
+
+    def terms(dy, dx):
+        there = lax.rem(yh + dy, 2) * 4 + lax.rem(x + dx, 4)
+        sub = lax.broadcasted_iota(jnp.int32, (256, 256), 0)
+        qend = qend_ref[0:1, :]
+        limits = [qend - (there * 512 + lax.rem(core + dc, 2) * 256) for dc in range(2)]
+
+        @pl.loop(0, 4)
+        def _(h):
+            cols = pl.ds(pl.multiple_of(h * 128, 128), 128)
+            qh = q_ref[:, cols]
+            gh = ig_ref[:, cols]
+            lse = lse_ref[h][0:1, :]
+            dots = row_dot[h][0:1, :]
+            for dc in range(2):
+                kh = kv_ref[dy, dx, dc, 0, :, cols]
+                vh = kv_ref[dy, dx, dc, 1, :, cols]
+                s = dot_nt(kh, qh) * (LOG2E * scale)
+                p = jnp.exp2(jnp.where(sub < limits[dc], s, LOW) - lse)
+                dp = dot_nt(vh, gh)
+                ds = (p * (dp - dots) * scale).astype(bf)
+                dk = dot_nn(ds, qh).astype(bf)
+                dv = dot_nn(p.astype(bf), gh).astype(bf)
+                dqt[h] += dot_tn(kh, ds)
+                to = own_terms if dc == 0 else sib_send
+                to[dy, dx, 0, :, cols] = dk
+                to[dy, dx, 1, :, cols] = dv
+
+        for which in range(2):
+            sib_copy(dy, dx, which).start()
+
+    def sib_copy(dy, dx, which):
+        return remote(
+            sib_send.at[dy, dx, which],
+            sib_recv.at[dy, dx, which],
+            sib_send_sem.at[dy, dx, which],
+            sib_recv_sem.at[dy, dx, which],
+            sibling,
+        )
+
+    def ring_copy(dy, dx, which):
+        to = (dx + 3) % 4 if which == 0 else (dx + 1) % 4
+        return remote(
+            ring_send.at[dy, dx, which],
+            ring_recv.at[dy, to, which],
+            ring_send_sem.at[dy, dx, which],
+            ring_recv_sem.at[dy, to, which],
+            right if which == 0 else left,
+        )
+
+    def arrival(dy, dx, which):
+        return ring_copy(dy, (dx + 1) % 4 if which == 0 else (dx + 3) % 4, which)
+
+    def total_of(dy, dx, which, ring):
+        sib_copy(dy, dx, which).wait_recv()
+        if ring:
+            arrival(dy, dx, which).wait_recv()
+        sums = own_terms[dy, dx, which].astype(f32) + sib_recv[dy, dx, which].astype(f32)
+        if ring:
+            sums = sums + ring_recv[dy, dx, which].astype(f32)
+        return sums
+
+    def send_ring(dy, dx, which, ring):
+        ring_send[dy, dx, which] = total_of(dy, dx, which, ring).astype(bf)
+        ring_copy(dy, dx, which).start()
+
+    def part_copy(which):
+        return remote(
+            part_send.at[which],
+            part_recv.at[which],
+            part_send_sem.at[which],
+            part_recv_sem.at[which],
+            partner,
+        )
+
+    terms(1, 3)
+    terms(1, 1)
+    send_ring(1, 3, 0, False)
+    send_ring(1, 1, 1, False)
+    terms(1, 2)
+    terms(1, 0)
+    send_ring(1, 2, 0, True)
+    send_ring(1, 2, 1, True)
+    terms(0, 3)
+    terms(0, 1)
+    send_ring(1, 1, 0, True)
+    send_ring(1, 3, 1, True)
+    send_ring(0, 3, 0, False)
+    send_ring(0, 1, 1, False)
+    terms(0, 2)
+    for which in range(2):
+        part_send[which] = total_of(1, 0, which, True).astype(bf)
+        part_copy(which).start()
+    send_ring(0, 2, 0, True)
+    send_ring(0, 2, 1, True)
+    terms(0, 0)
+    for h in range(4):
+        dq_ref[:, h * 128 : h * 128 + 128] = jnp.transpose(dqt[h]).astype(bf)
+    send_ring(0, 1, 0, True)
+    send_ring(0, 3, 1, True)
+    for which in range(2):
+        sums = total_of(0, 0, which, True)
+        part_copy(which).wait_recv()
+        sums = sums + part_recv[which].astype(f32)
+        if which == 0:
+            dk_ref[...] = sums.astype(bf)
+        else:
+            dv_ref[...] = sums.astype(bf)
+
+    for dy in range(2):
+        for dx in range(4):
+            for which in range(2):
+                sib_copy(dy, dx, which).wait_send()
+                if dx > 0:
+                    ring_copy(dy, dx, which).wait_send()
+    for which in range(2):
+        part_copy(which).wait_send()
+
+    @pl.loop(1, 16)
+    def _(k):
+        there = lax.rem(me + k, 16)
+        remote(
+            rg_ref.at[there], rg_recv.at[k], rg_send_sem.at[k], rg_recv_sem.at[k], {"ctx": there}
+        ).wait_send()
+
+
+def greet_ctx():
+    me = lax.axis_index("ctx")
+    barrier = pltpu.get_barrier_semaphore()
+
+    @pl.loop(1, 16)
+    def _(k):
+        pl.semaphore_signal(
+            barrier, inc=1, device_id={"ctx": lax.rem(me + k, 16)}, device_id_type=MESH_ID
+        )
+
+    pl.semaphore_wait(barrier, 15)
+
+
+def backward_call(q, kv, lse, attn, qend, og, inv, pick, rg):
+    bf, f32 = jnp.bfloat16, jnp.float32
+    vmem = pl.BlockSpec(memory_space=pltpu.VMEM)
+    shape = jax.ShapeDtypeStruct
+    return pl.pallas_call(
+        backward_kernel,
+        out_shape=(shape((256, 512), bf),) * 4,
+        in_specs=[vmem] * 9,
+        out_specs=(vmem,) * 4,
+        scratch_shapes=[
+            pltpu.VMEM((16, 96, 512), bf),
+            pltpu.VMEM((256, 512), f32),
+            pltpu.VMEM((4, 8, 256), f32),
+            pltpu.VMEM((4, 128, 256), f32),
+            pltpu.VMEM((2, 4, 2, 256, 512), bf),
+            pltpu.VMEM((2, 4, 2, 256, 512), bf),
+            pltpu.VMEM((2, 4, 2, 256, 512), bf),
+            pltpu.VMEM((2, 4, 2, 256, 512), bf),
+            pltpu.VMEM((2, 4, 2, 256, 512), bf),
+            pltpu.VMEM((2, 256, 512), bf),
+            pltpu.VMEM((2, 256, 512), bf),
+            pltpu.SemaphoreType.DMA((16,)),
+            pltpu.SemaphoreType.DMA((16,)),
+            pltpu.SemaphoreType.DMA((2, 4, 2)),
+            pltpu.SemaphoreType.DMA((2, 4, 2)),
+            pltpu.SemaphoreType.DMA((2, 4, 2)),
+            pltpu.SemaphoreType.DMA((2, 4, 2)),
+            pltpu.SemaphoreType.DMA((2,)),
+            pltpu.SemaphoreType.DMA((2,)),
+        ],
+        compiler_params=pltpu.CompilerParams(
+            collective_id=1, has_side_effects=True, vmem_limit_bytes=56 * 2**20
+        ),
+        name="backward",
+    )(q, kv, lse, attn, qend, og, inv, pick, rg)
+
+
 def shards(
     residual, queries, keys, values, frame_lengths, routes, route_gates, w_in, w_out, out_grad
 ):
@@ -374,13 +600,9 @@
     n_grp = lax.axis_size("grp")
     tok_rows, feat_dev = residual.shape
     exp_dev = w_in.shape[0]
-    head_dim = HEAD_DIM
-    heads_dev = feat_dev // head_dim
     seq_len = tok_rows * n_ctx
     experts_all = exp_dev * n_ctx
     capacity = 6 * tok_rows // experts_all
-    width_all = feat_dev * n_grp
-    score_scale = head_dim ** (-0.5)
     expert_flat = routes.reshape(-1)
     onehot = (expert_flat[:, None] == jnp.arange(experts_all, dtype=jnp.int32)[None, :]).astype(
         jnp.int32
@@ -395,16 +617,12 @@
     pick_both = pick[0] + pick[1]
     pick_two = jnp.concatenate(pick, axis=1)
 
-    def to_experts(rows):
-        rows = rows.reshape(n_ctx, exp_dev * capacity, feat_dev)
-        recv = lax.all_to_all(rows, "ctx", split_axis=0, concat_axis=0, tiled=True)
-        recv = recv.reshape(n_ctx, exp_dev, capacity, feat_dev)
-        return recv.transpose(1, 0, 2, 3).reshape(exp_dev, n_ctx * capacity, feat_dev)
+    def by_source(rows):
+        rows = rows.reshape(exp_dev, n_ctx, capacity, feat_dev).transpose(1, 0, 2, 3)
+        return rows.reshape(n_ctx, exp_dev * capacity, feat_dev)
 
     def to_tokens(rows):
-        rows = rows.reshape(exp_dev, n_ctx, capacity, feat_dev).transpose(1, 0, 2, 3)
-        rows = rows.reshape(n_ctx, exp_dev * capacity, feat_dev)
-        back = lax.all_to_all(rows, "ctx", split_axis=0, concat_axis=0, tiled=True)
+        back = lax.all_to_all(by_source(rows), "ctx", split_axis=0, concat_axis=0, tiled=True)
         return back.reshape(experts_all * capacity, feat_dev)
 
     def sum_scatter(partial):
@@ -438,8 +656,6 @@
         w_out,
     )
     mixed_f = mixed.astype(jnp.float32)
-    inv_rms = inv_wide[:, 0]
-    attn_heads = attn.reshape(tok_rows, heads_dev, head_dim)
 
     def by_expert(rows):
         rows = rows.reshape(n_ctx, exp_dev, capacity, feat_dev)
@@ -457,7 +673,17 @@
     row_grad = jnp.einsum(
         "erh,efh->erf", pre_grad, w_in, preferred_element_type=jnp.float32
     ).astype(jnp.bfloat16)
-    normed_grad = jnp.dot(pick_both.T, to_tokens(row_grad), preferred_element_type=jnp.float32)
+    input_grad, query_grad, key_grad, value_grad = backward_call(
+        queries,
+        kv_all,
+        lse,
+        attn,
+        jnp.broadcast_to(ends[None, :], (8, tok_rows)).astype(jnp.int32),
+        out_grad,
+        inv_wide,
+        pick_both.reshape(n_ctx, exp_dev * capacity, tok_rows),
+        by_source(row_grad),
+    )
     w_in_grad = jnp.einsum(
         "erf,erh->efh", rows_recv, pre_grad, preferred_element_type=jnp.float32
     ).astype(jnp.bfloat16)
@@ -472,64 +698,12 @@
     w_out_grad = jnp.einsum(
         "erh,erf->ehf", activated, grads_recv, preferred_element_type=jnp.float32
     ).astype(jnp.bfloat16)
-    input_grad_f = out_grad_f + inv_rms[:, None] * normed_grad
-    input_grad = input_grad_f.astype(jnp.bfloat16)
-    grad_heads = input_grad.reshape(tok_rows, heads_dev, head_dim)
-    row_dot = jnp.sum(grad_heads.astype(jnp.float32) * attn_heads.astype(jnp.float32), axis=2).T
-    core, chip = ctx_index % 2, ctx_index // 2
-    chip_y, chip_x = chip // 4, chip % 4
-    there = [
-        ((chip_y + dy) % 2 * 4 + (chip_x + dx) % 4) * 2 + (core + dc) % 2
-        for dy in range(2)
-        for dx in range(4)
-        for dc in range(2)
-    ]
-    there = jnp.stack(there)
-    key_pos = (there[:, None] * tok_rows + jnp.arange(tok_rows)[None, :]).reshape(-1)
-    key_heads_all = kv_all[:, :, :, 0].reshape(seq_len, heads_dev, head_dim)
-    value_heads_all = kv_all[:, :, :, 1].reshape(seq_len, heads_dev, head_dim)
-    query_heads = queries.reshape(tok_rows, heads_dev, head_dim)
-    scores = (
-        jnp.einsum("qhd,khd->hqk", query_heads, key_heads_all, preferred_element_type=jnp.float32)
-        * score_scale
-    )
-    scores = jnp.where((key_pos[None, :] < ends[:, None])[None], scores, -jnp.inf)
-    log_total = lse[:, :, 0:1] / LOG2E
-    prob_f = jnp.exp(scores - log_total)
-    prob_all = prob_f.astype(jnp.bfloat16)
-    dprob = jnp.einsum(
-        "qhd,khd->hqk", grad_heads, value_heads_all, preferred_element_type=jnp.float32
-    )
-    dscore_all = (prob_f * (dprob - row_dot[:, :, None]) * score_scale).astype(jnp.bfloat16)
-    query_sum = jnp.einsum(
-        "hqk,khd->qhd", dscore_all, key_heads_all, preferred_element_type=jnp.float32
-    )
-    key_term = jnp.einsum(
-        "hqk,qhd->khd", dscore_all, query_heads, preferred_element_type=jnp.float32
-    ).reshape(seq_len, feat_dev)
-    value_term = jnp.einsum(
-        "hqk,qhd->khd", prob_all, grad_heads, preferred_element_type=jnp.float32
-    ).reshape(seq_len, feat_dev)
-    both_terms = jnp.concatenate([key_term, value_term], axis=1)
-    both_terms = both_terms.reshape(n_ctx, tok_rows, 2 * feat_dev)
-    both_terms = (
-        jnp.zeros_like(both_terms).at[there].set(both_terms).reshape(seq_len, 2 * feat_dev)
-    )
-    key_grad_f, value_grad_f = (
-        lax.psum_scatter(
-            both_terms[:, :feat_dev].astype(jnp.bfloat16), "ctx", scatter_dimension=0, tiled=True
-        ).astype(jnp.float32),
-        lax.psum_scatter(
-            both_terms[:, feat_dev:].astype(jnp.bfloat16), "ctx", scatter_dimension=0, tiled=True
-        ).astype(jnp.float32),
-    )
-    query_grad = query_sum.reshape(tok_rows, feat_dev).astype(jnp.bfloat16)
     return (
         layer_out,
         input_grad,
         query_grad,
-        key_grad_f.astype(jnp.bfloat16),
-        value_grad_f.astype(jnp.bfloat16),
+        key_grad,
+        value_grad,
         w_in_grad,
         w_out_grad,
     )

time: 643 us -> 481 us (0.75); the launches traced: 634 us -> 481 us
  local copies, waits for them, and re-layouts: 130 us -> 14.3 us
  Pallas kernels: 144 us -> 230 us
  waiting for transfers between devices: 222 us -> 171 us
  matrix products: 79.7 us -> 31.6 us
  other arithmetic: 32.2 us -> 12.6 us
    reduce_scatter x2 -> x0, waiting for transfers between devices: 116 us -> none  [the longest x1 84.2 us: shards(): lax.psum_scatter(both_terms[:, :feat_dev].astype(jnp.bfloat16), 'ctx', sc...]
    pallas_call x0 -> x1, Pallas kernels: none -> 86.7 us  [backward_call(): pl.pallas_call(backward_kernel, out_shape=(shape((256, 512), bf),) * 4, i...]
    all_gather x2, waiting for transfers between devices: 25.8 us -> 111 us  [gather(): full = lax.all_gather(shard, 'grp', axis=0, tiled=True)]
    dot_general x6 -> x0, matrix products: 47.8 us -> none  [the longest x1 13.7 us: shards(): jnp.einsum('hqk,qhd->khd', prob_all, grad_heads, preferred_element_type=j...]
    scatter x1 -> x0, local copies, waits for them, and re-layouts: 30.1 us -> none  [shards(): jnp.zeros_like(both_terms).at[there].set(both_terms)]
    another operation x7 -> x2, local copies, waits for them, and re-layouts: 22.4 us -> 0.74 us  [the longest x2 14.6 us: shards(): key_heads_all = kv_all[:, :, :, 0].reshape(seq_len, heads_dev, head_dim)]
    unnamed x45 -> x33, local copies, waits for them, and re-layouts: 23.3 us -> 3.87 us
    all_to_all x2 -> x1, waiting for transfers between devices: 18.6 us -> 0.01 us  [to_tokens(): lax.all_to_all(by_source(rows), 'ctx', split_axis=0, concat_axis=0, tiled...]
  transfers between devices with their start and end apart: 7 -> 4, of which waited for: 6 -> 3; matrix products, arithmetic and copies ran while one was open for 34% -> 5% of each run, Pallas kernels for 0% -> 18%
where the time goes in v3:
time: 481 us
  Pallas kernels  230 us (48%)
  waiting for transfers between devices  171 us (36%)
  matrix products  31.6 us (7%)
  local copies, waits for them, and re-layouts  14.3 us (3%)
  between operations  14 us (3%)
  other arithmetic  12.6 us (3%)
  starting transfers between devices  6.69 us (1%)
    pallas_call x1, Pallas kernels, forward_call(): pl.pallas_call(forward_kernel, out_shape=(shape((256, 512), bf), shape((4...  144 us
    all_gather x2, waiting for transfers between devices, gather(): full = lax.all_gather(shard, 'grp', axis=0, tiled=True)  111 us
    pallas_call x1, Pallas kernels, backward_call(): pl.pallas_call(backward_kernel, out_shape=(shape((256, 512), bf),) * 4, i...  86.7 us
    reduce_scatter x1, waiting for transfers between devices, sum_scatter(): lax.psum_scatter(flat, 'grp', scatter_dimension=0, tiled=True)  60.8 us
  transfers between devices with their start and end apart: 4, of which 3 were waited for; matrix products, arithmetic and copies ran while one was open for 5% of the time, Pallas kernels for 18%

profile of v3, /device:TPU:0, one launch (start us, length us, event | category | flops | bytes accessed | tf_op | source)
XLA Modules:
  0.0 480.9 jit_solution(14662388245366004123)
XLA Ops:
  7.2 1.0 copy.60
  8.5 1.2 reduce-window.19
  11.0 1.5 compare_convert_fusion.1
  12.5 1.2 fusion.20.pick_both_ref.pick_ref
  16.5 1.3 pad_maximum_fusion.pick_two_ref
  18.5 143.5 %forward.1 = (bf16[256,512]{1,0:T(8,128)(2,1)}, f32[4,8,256]{2,1,0:T(8,128)}, bf16[256,512]{1,0:T(8,128)(2,1)}, f32[256,128]{1,0:T(8,128)}, bf16[16,96,512]{2,1,...) custom-call(bf16[256,512]{1,0:T(8,128)(2,1)} %q_ref.3, ...), custom_call_target="tpu_custom_call" | custom-call | tf_op jit(solution)/shard_map/forward/pallas_call | solution.py:326
  162.1 1.5 copy.64
  163.6 4.3 convolution_convert_fusion
  167.9 60.8 %reduce-scatter.2.cloned.1.call-done = bf16[192,1536]{1,0:T(8,128)(2,1)} async-done(((bf16[1536,1536]{1,0:T(8,128)(2,1)}), bf16[192,1536]{1,0:T(8,128)(2,1)}) %reduce-scatter.2.cloned.1.call-update) | async-done | bytes 589840 | tf_op jit(solution)/shard_map/reduce_scatter | solution.py:630
  228.8 3.3 fusion.11
  232.1 56.5 %all-gather.3.cloned.1.call-done = bf16[1536,1536]{1,0:T(8,128)(2,1)} async-done(((bf16[192,1536]{1,0:T(8,128)(2,1)}), bf16[1536,1536]{1,0:T(8,128)(2,1)}) %all-gather.3.cloned.1.call-update) | async-done | bytes 4718608 | tf_op jit(solution)/shard_map/all_gather | solution.py:633
  288.7 2.7 copy.68
  291.3 1.2 iota_compare_fusion
  292.6 54.1 %all-gather.5.cloned.1.call-done = bf16[1536,1536]{1,0:T(8,128)(2,1)} async-done(((bf16[192,1536]{1,0:T(8,128)(2,1)}), bf16[1536,1536]{1,0:T(8,128)(2,1)}) %all-gather.5.cloned.1.call-update) | async-done | bytes 4718608 | tf_op jit(solution)/shard_map/all_gather | solution.py:633
  346.7 5.9 %convolution_convert_fusion.4 = bf16[2,768,512]{2,1,0:T(8,128)(2,1)S(1)} fusion(bf16[2,768,1536]{2,1,0:T(8,128)(2,1)} %bitcast.78, bf16[2,1536,512]{2,1,0:T(8,128)(2,1)} %w_out_ref.1), kind=kOutput, calls=%fused_computation.15 | convolution fusion | flops 2416705536 | bytes 9437184 | tf_op jit(solution)/shard_map/erh,ehf->erf/dot_general | solution.py:690
  352.6 1.3 copy.65
  353.9 6.6 %all-to-all-start = ((bf16[16,96,512]{2,1,0:T(8,128)(2,1)}), bf16[16,96,512]{2,1,0:T(8,128)(2,1)}, u32[]{:S(2)}, u32[]{:S(2)}) async-start(bf16[16,96,512]{2,1,0:T(8,128)(2,1)} %bitcast.55), calls=%async_computation.1 | async-start | bytes 3145728 | tf_op jit(solution)/shard_map/all_to_all | solution.py:625
  360.5 5.0 %convolution_convert_fusion.3 = bf16[2,768,512]{2,1,0:T(8,128)(2,1)S(1)} fusion(bf16[2,768,1536]{2,1,0:T(8,128)(2,1)} %bitcast.76, bf16[2,512,1536]{2,1,0:T(8,128)(2,1)S(1)} %copy-done), kind=kOutput, calls=%fused_computation.14 | convolution fusion | flops 2416705536 | bytes 9437184 | tf_op jit(solution)/shard_map/erh,efh->erf/dot_general | solution.py:673
  365.4 1.3 copy.66
  367.3 86.7 %backward.1 = (bf16[256,512]{1,0:T(8,128)(2,1)}, bf16[256,512]{1,0:T(8,128)(2,1)}, bf16[256,512]{1,0:T(8,128)(2,1)}, bf16[256,512]{1,0:T(8,128)(2,1)}) custom-call(bf16[256,512]{1,0:T(8,128)(2,1)} %q_ref.3, bf16[2,4,2,2,256,512]{5,4,3,2,1,0:T(8,128)(2,1)} %get-tuple-element.25.kv_ref, f32[4,8,256]{2,1,0:T(8,128)} %get-tuple-element.26.lse_ref, ...), custom_call_target="tpu_custom_call" | custom-call | tf_op jit(solution)/shard_map/backward/pallas_call | solution.py:563
  454.0 6.5 %convolution_convert_fusion.2 = bf16[2,512,1536]{2,1,0:T(8,128)(2,1)} fusion(bf16[2,768,512]{2,1,0:T(8,128)(2,1)S(1)} %bitcast.59, bf16[2,768,1536]{2,1,0:T(8,128)(2,1)} %bitcast.77), kind=kOutput, calls=%fused_computation.2 | convolution fusion | flops 2417491968 | bytes 9437184 | tf_op jit(solution)/shard_map/erf,erh->efh/dot_general | solution.py:687
  460.5 7.4 %convolution_convert_fusion.1 = bf16[2,1536,512]{2,1,0:T(8,128)(2,1)} fusion(bf16[2,768,1536]{2,1,0:T(8,128)(2,1)} %bitcast.79, bf16[2,768,512]{2,1,0:T(8,128)(2,1)S(1)} %bitcast.61), kind=kOutput, calls=%fused_computation.1 | convolution fusion | flops 2417491968 | bytes 9437184 | tf_op jit(solution)/shard_map/erh,erf->ehf/dot_general | solution.py:698
  468.0 2.6 fusion
  470.6 0.9 fusion.19
  (61 shorter events, 8.8 us)
Async XLA Ops:
  7.2 156.4 %copy-start = (bf16[2,512,1536]{2,1,0:T(8,128)(2,1)S(1)}, bf16[2,512,1536]{2,1,0:T(8,128)(2,1)}, u32[]{:S(2)}) copy-start(bf16[2,512,1536]{2,1,0:T(8,128)(2,1)} %param.17) | copy-start | bytes 9437188
  7.2 221.6 %reduce-scatter.2.cloned.1.call-start = ((), (), s32[]{:S(2)}) async-start(), calls=%async_computation.2 | async-start | bytes 5308416 | tf_op jit(solution)/shard_map/reduce_scatter | solution.py:630
  8.5 7.0 %copy-start.6 = (bf16[256,512]{1,0:T(8,128)(2,1)S(1)}, bf16[256,512]{1,0:T(8,128)(2,1)}, u32[]{:S(2)}) copy-start(bf16[256,512]{1,0:T(8,128)(2,1)} %og_ref.1) | copy-start | bytes 786436
  14.6 1.9 copy-start.1
  14.6 1.9 copy-start.2
  15.5 2.3 copy-start.12
  163.6 4.3 copy-start.3
  167.9 120.7 %all-gather.3.cloned.1.call-start = ((), (), s32[]{:S(2)}) async-start(), calls=%async_computation.3 | async-start | bytes 5308416 | tf_op jit(solution)/shard_map/all_gather | solution.py:633
  232.1 114.6 %all-gather.5.cloned.1.call-start = ((), (), s32[]{:S(2)}) async-start(), calls=%async_computation.4 | async-start | bytes 5308416 | tf_op jit(solution)/shard_map/all_gather | solution.py:633
  353.9 114.1 %all-to-all-start = ((bf16[16,96,512]{2,1,0:T(8,128)(2,1)}), bf16[16,96,512]{2,1,0:T(8,128)(2,1)}, u32[]{:S(2)}, u32[]{:S(2)}) async-start(bf16[16,96,512]{2,1,0:T(8,128)(2,1)} %bitcast.55), calls=%async_computation.1 | async-start | bytes 3145728 | tf_op jit(solution)/shard_map/all_to_all | solution.py:625
  365.4 1.3 copy-start.13
  367.3 86.7 %copy-start.4 = (bf16[16,2,48,512]{3,2,0,1:T(8,128)(2,1)S(1)}, bf16[16,2,48,512]{3,2,0,1:T(8,128)(2,1)}, u32[]{:S(2)}) copy-start(bf16[16,2,48,512]{3,2,0,1:T(8,128)(2,1)} %copy-done.3) | copy-start | bytes 4718596
  454.0 6.5 %copy-start.5 = (bf16[2,16,48,512]{3,2,1,0:T(8,128)(2,1)S(1)}, bf16[2,16,48,512]{3,2,1,0:T(8,128)(2,1)}, u32[]{:S(2)}) copy-start(bf16[2,16,48,512]{3,2,1,0:T(8,128)(2,1)} %copy.68) | copy-start | bytes 4718596
  468.0 2.6 copy-start.11
  470.6 1.0 copy-start.10
  470.6 1.6 copy-start.9
  470.6 2.3 copy-start.8
  470.6 3.0 copy-start.7
Sparse Core Ops, SparseCore 0:
  168.0 60.7 reduce-scatter.1
  232.2 56.3 all-gather.2
  290.3 56.3 all-gather.4

commit v4 on v3

--- a/solution.py
+++ b/solution.py
@@ -70,10 +70,298 @@
     )
 
 
+def pick_two(rows_ref, there):
+    rows = lax.broadcasted_iota(jnp.int32, (96, 512), 0) + there * 96
+    return jnp.where(rows == rows_ref[0:1, :], 1.0, 0.0).astype(jnp.bfloat16)
+
+
+def pick_both(rows_ref, there):
+    rows = lax.broadcasted_iota(jnp.int32, (96, 256), 0) + there * 96
+    hit = (rows == rows_ref[0:1, 0:256]) | (rows == rows_ref[0:1, 256:512])
+    return jnp.where(hit, 1.0, 0.0).astype(jnp.bfloat16)
+
+
+def grp_device(dy, dz):
+    grp = lax.axis_index("grp")
+    there = lax.rem(grp // 4 + dy, 2) * 4 + lax.rem(lax.rem(grp, 4) + dz, 4)
+    return {"grp": there}
+
+
+class GrpSum:
+    def __init__(self, cut, part, recv, send_sem, recv_sem):
+        self.cut, self.part, self.recv = cut, part, recv
+        self.send_sem, self.recv_sem = send_sem, recv_sem
+        self.head, self.rest = pl.ds(0, cut), pl.ds(cut, 192 - cut)
+
+    def copy(self, number):
+        part, head, rest = self.part, self.head, self.rest
+        if number < 4:
+            src, rows, where = part.at[1, number, head], head, grp_device(1, 0)
+        elif number < 10:
+            dz, dy = (number - 4) // 2 + 1, (number - 4) % 2
+            src, rows, where = part.at[dy, dz, rest], rest, grp_device(0, dz)
+        elif number < 13:
+            dz = number - 9
+            src, rows, where = part.at[0, dz, head], head, grp_device(0, dz)
+        else:
+            src, rows, where = part.at[1, 0, rest], rest, grp_device(1, 0)
+        return remote(
+            src,
+            self.recv.at[number, rows],
+            self.send_sem.at[number],
+            self.recv_sem.at[number],
+            where,
+        )
+
+    def send_first(self, dy, dz):
+        if dy == 1:
+            self.copy(dz).start()
+        if dz > 0:
+            self.copy(4 + (dz - 1) * 2 + dy).start()
+
+    def add(self, target, start, size, slots, out):
+        @pl.loop(0, size // 16)
+        def _(step):
+            rows = pl.ds(pl.multiple_of(start + step * 16, 16), 16)
+            total = self.part[target[0], target[1], rows, :].astype(jnp.float32)
+            for slot in slots:
+                total += self.recv[slot, rows, :].astype(jnp.float32)
+            out(rows, total)
+
+    def second(self, dz):
+        self.copy(dz).wait_recv()
+
+        def out(rows, total):
+            self.part[0, dz, rows, :] = total.astype(jnp.bfloat16)
+
+        self.add((0, dz), 0, self.cut, [dz], out)
+        self.copy(9 + dz).start()
+
+    def second_rest(self):
+        for number in (5, 7, 9):
+            self.copy(number).wait_recv()
+
+        def out(rows, total):
+            self.part[1, 0, rows, :] = total.astype(jnp.bfloat16)
+
+        self.add((1, 0), self.cut, 192 - self.cut, [5, 7, 9], out)
+        self.copy(13).start()
+
+    def finish(self, out):
+        for number in (0, 4, 6, 8, 10, 11, 12, 13):
+            self.copy(number).wait_recv()
+        self.add((0, 0), 0, self.cut, [0, 10, 11, 12], out)
+        self.add((0, 0), self.cut, 192 - self.cut, [4, 6, 8, 13], out)
+
+    def drain(self):
+        for number in range(14):
+            self.copy(number).wait_send()
+
+
+class GrpGather:
+    def __init__(self, cut, full, send_sem, recv_sem):
+        self.full, self.send_sem, self.recv_sem = full, send_sem, recv_sem
+        self.head, self.rest = pl.ds(0, cut), pl.ds(cut, 192 - cut)
+
+    def copy(self, number):
+        head, rest = self.head, self.rest
+        if number < 3:
+            dz = number + 1
+            src, dst, rows, where = (0, 0), (0, 4 - dz), head, grp_device(0, dz)
+        elif number == 3:
+            src, dst, rows, where = (0, 0), (1, 0), rest, grp_device(1, 0)
+        elif number < 8:
+            dz = number - 4
+            src, dst, rows, where = (0, dz), (1, dz), head, grp_device(1, 0)
+        else:
+            dz, dy = (number - 8) // 2 + 1, (number - 8) % 2
+            src, dst, rows, where = (dy, 0), (dy, 4 - dz), rest, grp_device(0, dz)
+        return remote(
+            self.full.at[src[0], src[1], rows],
+            self.full.at[dst[0], dst[1], rows],
+            self.send_sem.at[number],
+            self.recv_sem.at[number],
+            where,
+        )
+
+    def send_own(self):
+        self.copy(3).start()
+        for number in (0, 2, 1):
+            self.copy(number).start()
+        self.copy(4).start()
+        for dz in (1, 3, 2):
+            self.copy(8 + (dz - 1) * 2).start()
+
+    def pass_rest(self):
+        self.copy(3).wait_recv()
+        for dz in (1, 3, 2):
+            self.copy(8 + (dz - 1) * 2 + 1).start()
+
+    def pass_head(self, dz):
+        self.copy(3 - dz).wait_recv()
+        self.copy(4 + dz).start()
+
+    def wait_chunk(self, dy, dz):
+        if dy == 1:
+            self.copy(4 + dz).wait_recv()
+        if dz > 0:
+            self.copy(8 + (3 - dz) * 2 + dy).wait_recv()
+
+    def drain(self):
+        for number in range(14):
+            self.copy(number).wait_send()
+
+
+def chunk_of(dy, dz):
+    grp = lax.axis_index("grp")
+    return lax.rem(grp // 4 + dy, 2), lax.rem(lax.rem(grp, 4) + dz, 4) * 4
+
+
+def chunk_rows(ref, dy, dz):
+    expert, first = chunk_of(dy, dz)
+    rows = ref[pl.ds(first, 4), pl.ds(pl.multiple_of(expert * 48, 16), 48), :]
+    return rows.reshape(192, 512)
+
+
+CHUNK_ORDER = [(1, 1), (1, 3), (1, 2), (1, 0), (0, 1), (0, 3), (0, 2), (0, 0)]
+
+
+def return_rows(rows, dy, dz, send, recv, send_sem, recv_sem):
+    me = lax.axis_index("ctx")
+    expert, first = chunk_of(dy, dz)
+    send[expert, pl.ds(first, 4)] = rows.reshape(4, 48, 512)
+
+    @pl.loop(0, 4)
+    def _(i):
+        there = first + i
+
+        @pl.when(there != me)
+        def _():
+            return_copy(expert, there, me, there, send, recv, send_sem, recv_sem).start()
+
+
+def return_copy(expert, there, mine, partner, send, recv, send_sem, recv_sem):
+    return remote(
+        send.at[expert, there],
+        recv.at[mine, expert],
+        send_sem.at[expert, there],
+        recv_sem.at[expert, mine],
+        {"ctx": partner},
+    )
+
+
+def wait_returns(send, recv, send_sem, recv_sem):
+    me = lax.axis_index("ctx")
+    for expert in range(2):
+        recv[me, expert] = send[expert, me]
+
+        @pl.loop(1, 16)
+        def _(k):
+            source = lax.rem(me + k, 16)
+            copy = return_copy(
+                expert, source, source, source, send, recv, send_sem, recv_sem
+            )
+            copy.wait_recv()
+            copy.wait_send()
+
+
+def experts_kernel(
+    x_ref, act_grad_ref, w_in_ref,
+    act_ref, rg_ref, w_in_grad_ref,
+    part, sums, full, rg_send,
+    s_send_sem, s_recv_sem, f_send_sem, f_recv_sem, r_send_sem, r_recv_sem,
+):
+    bf = jnp.bfloat16
+    greet()
+    summing = GrpSum(112, part, sums, s_send_sem, s_recv_sem)
+    gathering = GrpGather(112, full, f_send_sem, f_recv_sem)
+    for dy, dz in CHUNK_ORDER:
+        expert, _ = chunk_of(dy, dz)
+        rows = chunk_rows(x_ref, dy, dz)
+
+        @pl.loop(0, 3)
+        def _(piece):
+            cols = pl.ds(pl.multiple_of(piece * 512, 512), 512)
+            part[dy, dz, :, cols] = dot_nn(rows, w_in_ref[expert, :, cols]).astype(bf)
+
+        summing.send_first(dy, dz)
+    for dz in (1, 3, 2):
+        summing.second(dz)
+    summing.second_rest()
+
+    def activate(rows, pre):
+        act_ref[rows, :] = gelu_tanh(pre).astype(bf)
+        full[0, 0, rows, :] = (act_grad_ref[rows, :] * gelu_slope(pre)).astype(bf)
+
+    summing.finish(activate)
+    gathering.send_own()
+
+    def row_grads(dy, dz):
+        expert, _ = chunk_of(dy, dz)
+        rows = dot_nt(full[dy, dz], w_in_ref[expert]).astype(bf)
+        return_rows(rows, dy, dz, rg_send, rg_ref, r_send_sem, r_recv_sem)
+
+    row_grads(0, 0)
+    gathering.pass_rest()
+    for dz in (1, 3, 2):
+        gathering.pass_head(dz)
+    for dz in (0, 1, 3, 2):
+        for dy in range(2):
+            if (dy, dz) != (0, 0):
+                gathering.wait_chunk(dy, dz)
+                row_grads(dy, dz)
+    for dy in range(2):
+        expert, _ = chunk_of(dy, 0)
+
+        @pl.loop(0, 3)
+        def _(piece):
+            cols = pl.ds(pl.multiple_of(piece * 512, 512), 512)
+            total = dot_tn(chunk_rows(x_ref, dy, 0), full[dy, 0, :, cols])
+            for dz in range(1, 4):
+                total += dot_tn(chunk_rows(x_ref, dy, dz), full[dy, dz, :, cols])
+            w_in_grad_ref[expert, :, cols] = total.astype(bf)
+
+    wait_returns(rg_send, rg_ref, r_send_sem, r_recv_sem)
+    summing.drain()
+    gathering.drain()
+
+
+def experts_call(x_rows, act_grad, w_in):
+    bf = jnp.bfloat16
+    vmem = pl.BlockSpec(memory_space=pltpu.VMEM)
+    shape = jax.ShapeDtypeStruct
+    return pl.pallas_call(
+        experts_kernel,
+        out_shape=(
+            shape((192, 1536), bf),
+            shape((16, 2, 48, 512), bf),
+            shape((2, 512, 1536), bf),
+        ),
+        in_specs=[vmem] * 3,
+        out_specs=(vmem,) * 3,
+        scratch_shapes=[
+            pltpu.VMEM((2, 4, 192, 1536), bf),
+            pltpu.VMEM((14, 192, 1536), bf),
+            pltpu.VMEM((2, 4, 192, 1536), bf),
+            pltpu.VMEM((2, 16, 48, 512), bf),
+            pltpu.SemaphoreType.DMA((14,)),
+            pltpu.SemaphoreType.DMA((14,)),
+            pltpu.SemaphoreType.DMA((14,)),
+            pltpu.SemaphoreType.DMA((14,)),
+            pltpu.SemaphoreType.DMA((2, 16)),
+            pltpu.SemaphoreType.DMA((2, 16)),
+        ],
+        compiler_params=pltpu.CompilerParams(
+            collective_id=2, has_side_effects=True, vmem_limit_bytes=56 * 2**20
+        ),
+        name="experts",
+    )(x_rows, act_grad, w_in)
+
+
 def forward_kernel(
-    q_ref, k_ref, v_ref, res_ref, qend_ref, gated_ref, pick_two_ref, pick_both_ref, w_out_ref,
+    q_ref, k_ref, v_ref, res_ref, qend_ref, gated_ref, rows_ref, w_out_ref,
     attn_ref, lse_ref, mixed_ref, inv_ref, xrecv_ref, grecv_ref, act_grad_ref, kv_out_ref,
-    kv, m_s, l_s, acc_s, gsend, xsend, psend, precv, sq_send, sq_recv,
+    kv, m_s, l_s, acc_s, gsend, xsend, part, sums, sq_send, sq_recv,
     kv_send_sem, kv_recv_sem, out_sem, g_send_sem, g_recv_sem, x_send_sem, x_recv_sem,
     p_send_sem, p_recv_sem, sq_send_sem, sq_recv_sem,
 ):
@@ -106,8 +394,7 @@
     sibling, partner = device(0, 0, 1), device(1, 0, 0)
     for which in range(2):
         move(own(which), (1, 0, 0, which), partner)
-        move(own(which), (0, 3, 0, which), right)
-        move(own(which), (0, 1, 0, which), left)
+    for which in range(2):
         move(own(which), (0, 0, 1, which), sibling)
     kv[0, 0, 0, 0] = k_ref[...]
     kv[0, 0, 0, 1] = v_ref[...]
@@ -115,7 +402,7 @@
     @pl.loop(0, 16)
     def _(k):
         there = lax.rem(me + k, 16)
-        gsend[k] = dot_nn(pick_two_ref[there], gated_ref[...]).astype(jnp.bfloat16)
+        gsend[k] = dot_nn(pick_two(rows_ref, there), gated_ref[...]).astype(jnp.bfloat16)
 
         @pl.when(k > 0)
         def _():
@@ -123,7 +410,11 @@
                 gsend.at[k], grecv_ref.at[me], g_send_sem.at[k], g_recv_sem.at[k], {"ctx": there}
             ).start()
 
+    for which in range(2):
+        move(own(which), (0, 3, 0, which), right)
+        move(own(which), (0, 1, 0, which), left)
     grecv_ref[me] = gsend[0]
+    summing = GrpSum(48, part, sums, p_send_sem, p_recv_sem)
     m_s[...] = jnp.full_like(m_s, LOW)
     l_s[...] = jnp.zeros_like(l_s)
     acc_s[...] = jnp.zeros_like(acc_s)
@@ -182,9 +473,6 @@
         move(kv.at[1, 0, 0, which], (1, 3, 0, which), right)
         move(kv.at[1, 0, 0, which], (1, 1, 0, which), left)
         move(kv.at[1, 0, 0, which], (1, 0, 1, which), sibling)
-    relay(0)
-    attend(0, 3)
-    attend(0, 1)
 
     @pl.loop(1, 16)
     def _(k):
@@ -193,25 +481,20 @@
             gsend.at[k], grecv_ref.at[source], g_send_sem.at[k], g_recv_sem.at[k], {"ctx": source}
         ).wait_recv()
 
-    @pl.loop(0, 8)
-    def _(k):
-        there = lax.rem(grp + k, 8)
-        expert = there // 4
-        first = lax.rem(there, 4) * 4
-        rows = grecv_ref[pl.ds(first, 4), pl.ds(pl.multiple_of(expert * 48, 16), 48), :]
-        rows = rows.reshape(192, 512)
+    for dy, dz in CHUNK_ORDER:
+        expert, _ = chunk_of(dy, dz)
+        rows = chunk_rows(grecv_ref, dy, dz)
 
         @pl.loop(0, 3)
-        def _(part):
-            cols = pl.ds(pl.multiple_of(part * 512, 512), 512)
-            psend[k, :, cols] = dot_nt(rows, w_out_ref[expert, cols, :]).astype(jnp.bfloat16)
-
-        @pl.when(k > 0)
-        def _():
-            remote(
-                psend.at[k], precv.at[k], p_send_sem.at[k], p_recv_sem.at[k], {"grp": there}
-            ).start()
-
+        def _(piece):
+            cols = pl.ds(pl.multiple_of(piece * 512, 512), 512)
+            part[dy, dz, :, cols] = dot_nt(rows, w_out_ref[expert, cols, :]).astype(jnp.bfloat16)
+
+        summing.send_first(dy, dz)
+
+    relay(0)
+    attend(0, 3)
+    attend(0, 1)
     relay(1)
     attend(1, 0)
     for which in range(2):
@@ -268,12 +551,11 @@
         ],
         axis=1,
     )
-    attn_rows = normed
 
     @pl.loop(0, 16)
     def _(k):
         there = lax.rem(me + k, 16)
-        xsend[k] = dot_nn(pick_both_ref[there], attn_rows).astype(jnp.bfloat16)
+        xsend[k] = dot_nn(pick_both(rows_ref, there), normed).astype(jnp.bfloat16)
 
         @pl.when(k > 0)
         def _():
@@ -283,22 +565,15 @@
 
     xrecv_ref[me] = xsend[0]
 
-    @pl.loop(1, 8)
-    def _(k):
-        source = lax.rem(grp + 8 - k, 8)
-        copy = remote(
-            psend.at[k], precv.at[k], p_send_sem.at[k], p_recv_sem.at[k], {"grp": source}
-        )
-        copy.wait_recv()
-        copy.wait_send()
-
-    @pl.loop(0, 12)
-    def _(part):
-        rows = pl.ds(pl.multiple_of(part * 16, 16), 16)
-        total = psend[0, rows, :].astype(jnp.float32)
-        for k in range(1, 8):
-            total += precv[k, rows, :].astype(jnp.float32)
+    for dz in (1, 3, 2):
+        summing.second(dz)
+    summing.second_rest()
+
+    def keep(rows, total):
         act_grad_ref[rows, :] = total
+
+    summing.finish(keep)
+    summing.drain()
 
     @pl.loop(1, 16)
     def _(k):
@@ -319,7 +594,7 @@
         copy.wait()
 
 
-def forward_call(q, k, v, res, qend, gated, pick_two, pick_both, w_out):
+def forward_call(q, k, v, res, qend, gated, rows, w_out):
     bf, f32 = jnp.bfloat16, jnp.float32
     vmem = pl.BlockSpec(memory_space=pltpu.VMEM)
     shape = jax.ShapeDtypeStruct
@@ -335,7 +610,7 @@
             shape((192, 1536), f32),
             shape((2, 4, 2, 2, 256, 512), bf),
         ),
-        in_specs=[vmem] * 9,
+        in_specs=[vmem] * 8,
         out_specs=[vmem] * 7 + [pl.BlockSpec(memory_space=pl.ANY)],
         scratch_shapes=[
             pltpu.VMEM((2, 4, 2, 2, 256, 512), bf),
@@ -344,8 +619,8 @@
             pltpu.VMEM((4, 256, 128), f32),
             pltpu.VMEM((16, 96, 512), bf),
             pltpu.VMEM((16, 96, 512), bf),
-            pltpu.VMEM((8, 192, 1536), bf),
-            pltpu.VMEM((8, 192, 1536), bf),
+            pltpu.VMEM((2, 4, 192, 1536), bf),
+            pltpu.VMEM((14, 192, 1536), bf),
             pltpu.VMEM((8, 256), f32),
             pltpu.VMEM((8, 8, 256), f32),
             pltpu.SemaphoreType.DMA((30,)),
@@ -355,8 +630,8 @@
             pltpu.SemaphoreType.DMA((16,)),
             pltpu.SemaphoreType.DMA((16,)),
             pltpu.SemaphoreType.DMA((16,)),
-            pltpu.SemaphoreType.DMA((8,)),
-            pltpu.SemaphoreType.DMA((8,)),
+            pltpu.SemaphoreType.DMA((14,)),
+            pltpu.SemaphoreType.DMA((14,)),
             pltpu.SemaphoreType.DMA((8,)),
             pltpu.SemaphoreType.DMA((8,)),
         ],
@@ -364,15 +639,16 @@
             collective_id=0, has_side_effects=True, vmem_limit_bytes=56 * 2**20
         ),
         name="forward",
-    )(q, k, v, res, qend, gated, pick_two, pick_both, w_out)
+    )(q, k, v, res, qend, gated, rows, w_out)
 
 
 def backward_kernel(
-    q_ref, kv_ref, lse_ref, attn_ref, qend_ref, og_ref, inv_ref, pick_ref, rg_ref,
-    ig_ref, dq_ref, dk_ref, dv_ref,
-    rg_recv, normed_grad, row_dot, dqt, own_terms, sib_send, sib_recv, ring_send,
+    q_ref, kv_ref, lse_ref, attn_ref, qend_ref, og_ref, inv_ref, rows_ref, rg_ref, act_ref,
+    w_out_ref, g_ref, mixed_ref, gates_ref,
+    layer_ref, ig_ref, dq_ref, dk_ref, dv_ref, w_out_grad_ref,
+    full, eo_send, eo_recv, normed_grad, returned, row_dot, dqt, own_terms, sib_send, sib_recv, ring_send,
     ring_recv, part_send, part_recv,
-    rg_send_sem, rg_recv_sem, sib_send_sem, sib_recv_sem, ring_send_sem, ring_recv_sem,
+    f_send_sem, f_recv_sem, r_send_sem, r_recv_sem, sib_send_sem, sib_recv_sem, ring_send_sem, ring_recv_sem,
     part_send_sem, part_recv_sem,
 ):
     me = lax.axis_index("ctx")
@@ -388,25 +664,16 @@
 
     right, left = device(0, 1, 0), device(0, 3, 0)
     sibling, partner = device(0, 0, 1), device(1, 0, 0)
-    greet_ctx()
-
-    @pl.loop(1, 16)
+    greet()
+    gathering = GrpGather(48, full, f_send_sem, f_recv_sem)
+    full[0, 0] = act_ref[...]
+    gathering.send_own()
+    dqt[...] = jnp.zeros_like(dqt)
+    normed_grad[...] = jnp.zeros_like(normed_grad)
+
+    @pl.loop(0, 16)
     def _(k):
-        there = lax.rem(me + k, 16)
-        remote(
-            rg_ref.at[there], rg_recv.at[k], rg_send_sem.at[k], rg_recv_sem.at[k], {"ctx": there}
-        ).start()
-
-    dqt[...] = jnp.zeros_like(dqt)
-    normed_grad[...] = dot_tn(pick_ref[me], rg_ref[me])
-
-    @pl.loop(1, 16)
-    def _(k):
-        source = lax.rem(me + 16 - k, 16)
-        remote(
-            rg_ref.at[source], rg_recv.at[k], rg_send_sem.at[k], rg_recv_sem.at[k], {"ctx": source}
-        ).wait_recv()
-        normed_grad[...] += dot_tn(pick_ref[source], rg_recv[k])
+        normed_grad[...] += dot_tn(pick_both(rows_ref, k), rg_ref[k])
 
     for h in range(4):
         cols = slice(h * 128, h * 128 + 128)
@@ -492,14 +759,23 @@
             partner,
         )
 
+    def expert_rows(dy, dz):
+        expert, _ = chunk_of(dy, dz)
+        rows = dot_nn(full[dy, dz], w_out_ref[expert]).astype(bf)
+        return_rows(rows, dy, dz, eo_send, eo_recv, r_send_sem, r_recv_sem)
+
     terms(1, 3)
     terms(1, 1)
     send_ring(1, 3, 0, False)
     send_ring(1, 1, 1, False)
     terms(1, 2)
     terms(1, 0)
+    gathering.pass_rest()
+    for dz in (1, 3, 2):
+        gathering.pass_head(dz)
     send_ring(1, 2, 0, True)
     send_ring(1, 2, 1, True)
+    expert_rows(0, 0)
     terms(0, 3)
     terms(0, 1)
     send_ring(1, 1, 0, True)
@@ -513,10 +789,16 @@
     send_ring(0, 2, 0, True)
     send_ring(0, 2, 1, True)
     terms(0, 0)
+    gathering.wait_chunk(1, 0)
+    expert_rows(1, 0)
     for h in range(4):
         dq_ref[:, h * 128 : h * 128 + 128] = jnp.transpose(dqt[h]).astype(bf)
     send_ring(0, 1, 0, True)
     send_ring(0, 3, 1, True)
+    for dz in (1, 3, 2):
+        for dy in range(2):
+            gathering.wait_chunk(dy, dz)
+            expert_rows(dy, dz)
     for which in range(2):
         sums = total_of(0, 0, which, True)
         part_copy(which).wait_recv()
@@ -535,39 +817,47 @@
     for which in range(2):
         part_copy(which).wait_send()
 
-    @pl.loop(1, 16)
+    for dy in range(2):
+        expert, _ = chunk_of(dy, 0)
+
+        @pl.loop(0, 3)
+        def _(piece):
+            cols = pl.ds(pl.multiple_of(piece * 512, 512), 512)
+            total = dot_tn(full[dy, 0, :, cols], chunk_rows(g_ref, dy, 0))
+            for dz in range(1, 4):
+                total += dot_tn(full[dy, dz, :, cols], chunk_rows(g_ref, dy, dz))
+            w_out_grad_ref[expert, cols, :] = total.astype(bf)
+
+    wait_returns(eo_send, eo_recv, r_send_sem, r_recv_sem)
+    returned[...] = jnp.zeros_like(returned)
+
+    @pl.loop(0, 16)
     def _(k):
-        there = lax.rem(me + k, 16)
-        remote(
-            rg_ref.at[there], rg_recv.at[k], rg_send_sem.at[k], rg_recv_sem.at[k], {"ctx": there}
-        ).wait_send()
-
-
-def greet_ctx():
-    me = lax.axis_index("ctx")
-    barrier = pltpu.get_barrier_semaphore()
-
-    @pl.loop(1, 16)
-    def _(k):
-        pl.semaphore_signal(
-            barrier, inc=1, device_id={"ctx": lax.rem(me + k, 16)}, device_id_type=MESH_ID
-        )
-
-    pl.semaphore_wait(barrier, 15)
-
-
-def backward_call(q, kv, lse, attn, qend, og, inv, pick, rg):
+        returned[...] += dot_tn(pick_two(rows_ref, k), eo_recv[k].reshape(96, 512))
+
+    for h in range(4):
+        cols = slice(h * 128, h * 128 + 128)
+        sums = gates_ref[0] * returned[0:256, cols] + gates_ref[1] * returned[256:512, cols]
+        layer_ref[:, cols] = (mixed_ref[:, cols].astype(f32) + sums).astype(bf)
+
+    gathering.drain()
+
+
+def backward_call(*operands):
     bf, f32 = jnp.bfloat16, jnp.float32
     vmem = pl.BlockSpec(memory_space=pltpu.VMEM)
     shape = jax.ShapeDtypeStruct
     return pl.pallas_call(
         backward_kernel,
-        out_shape=(shape((256, 512), bf),) * 4,
-        in_specs=[vmem] * 9,
-        out_specs=(vmem,) * 4,
+        out_shape=(shape((256, 512), bf),) * 5 + (shape((2, 1536, 512), bf),),
+        in_specs=[vmem] * 14,
+        out_specs=(vmem,) * 6,
         scratch_shapes=[
-            pltpu.VMEM((16, 96, 512), bf),
+            pltpu.VMEM((2, 4, 192, 1536), bf),
+            pltpu.VMEM((2, 16, 48, 512), bf),
+            pltpu.VMEM((16, 2, 48, 512), bf),
             pltpu.VMEM((256, 512), f32),
+            pltpu.VMEM((512, 512), f32),
             pltpu.VMEM((4, 8, 256), f32),
             pltpu.VMEM((4, 128, 256), f32),
             pltpu.VMEM((2, 4, 2, 256, 512), bf),
@@ -577,8 +867,10 @@
             pltpu.VMEM((2, 4, 2, 256, 512), bf),
             pltpu.VMEM((2, 256, 512), bf),
             pltpu.VMEM((2, 256, 512), bf),
-            pltpu.SemaphoreType.DMA((16,)),
-            pltpu.SemaphoreType.DMA((16,)),
+            pltpu.SemaphoreType.DMA((14,)),
+            pltpu.SemaphoreType.DMA((14,)),
+            pltpu.SemaphoreType.DMA((2, 16)),
+            pltpu.SemaphoreType.DMA((2, 16)),
             pltpu.SemaphoreType.DMA((2, 4, 2)),
             pltpu.SemaphoreType.DMA((2, 4, 2)),
             pltpu.SemaphoreType.DMA((2, 4, 2)),
@@ -590,14 +882,13 @@
             collective_id=1, has_side_effects=True, vmem_limit_bytes=56 * 2**20
         ),
         name="backward",
-    )(q, kv, lse, attn, qend, og, inv, pick, rg)
+    )(*operands)
 
 
 def shards(
     residual, queries, keys, values, frame_lengths, routes, route_gates, w_in, w_out, out_grad
 ):
     n_ctx = lax.axis_size("ctx")
-    n_grp = lax.axis_size("grp")
     tok_rows, feat_dev = residual.shape
     exp_dev = w_in.shape[0]
     seq_len = tok_rows * n_ctx
@@ -609,95 +900,46 @@
     )
     earlier = jnp.cumsum(onehot, axis=0) - onehot
     ranks = jnp.sum(earlier * onehot, axis=1)
-    row_index = (expert_flat * capacity + ranks).reshape(tok_rows, 2)
-    slot_ids = jnp.arange(experts_all * capacity, dtype=jnp.int32)
-    pick = [
-        (slot_ids[:, None] == row_index[None, :, a]).astype(jnp.bfloat16) for a in range(2)
-    ]
-    pick_both = pick[0] + pick[1]
-    pick_two = jnp.concatenate(pick, axis=1)
-
-    def by_source(rows):
-        rows = rows.reshape(exp_dev, n_ctx, capacity, feat_dev).transpose(1, 0, 2, 3)
-        return rows.reshape(n_ctx, exp_dev * capacity, feat_dev)
-
-    def to_tokens(rows):
-        back = lax.all_to_all(by_source(rows), "ctx", split_axis=0, concat_axis=0, tiled=True)
-        return back.reshape(experts_all * capacity, feat_dev)
-
-    def sum_scatter(partial):
-        flat = partial.astype(jnp.bfloat16).reshape(-1, partial.shape[-1])
-        return lax.psum_scatter(flat, "grp", scatter_dimension=0, tiled=True).astype(jnp.float32)
-
-    def gather(shard):
-        full = lax.all_gather(shard, "grp", axis=0, tiled=True)
-        return full.reshape(exp_dev, n_ctx * capacity, -1)
-
+    row_index = (expert_flat * capacity + ranks).reshape(tok_rows, 2).T.reshape(1, 2 * tok_rows)
+    rows_wide = jnp.broadcast_to(row_index, (8, 2 * tok_rows))
     out_grad_f = out_grad.astype(jnp.float32)
     gated = jnp.concatenate(
         [(route_gates[:, a : a + 1] * out_grad_f).astype(jnp.bfloat16) for a in range(2)], axis=0
     )
+    gates_wide = jnp.broadcast_to(route_gates.T[:, :, None], (2, tok_rows, 128))
     ctx_index = lax.axis_index("ctx")
     frame_ends = jnp.cumsum(frame_lengths)
     positions = ctx_index * tok_rows + jnp.arange(tok_rows, dtype=jnp.int32)
     ends = jnp.min(
         jnp.where(frame_ends[None, :] > positions[:, None], frame_ends[None, :], seq_len), axis=1
-    )
-    qend = jnp.broadcast_to(ends[:, None], (tok_rows, 128)).astype(jnp.int32)
+    ).astype(jnp.int32)
     attn, lse, mixed, inv_wide, rows_recv, grads_recv, act_grad, kv_all = forward_call(
         queries,
         keys,
         values,
         residual,
-        qend,
+        jnp.broadcast_to(ends[:, None], (tok_rows, 128)),
         gated,
-        pick_two.reshape(n_ctx, exp_dev * capacity, 2 * tok_rows),
-        pick_both.reshape(n_ctx, exp_dev * capacity, tok_rows),
+        rows_wide,
         w_out,
     )
-    mixed_f = mixed.astype(jnp.float32)
-
-    def by_expert(rows):
-        rows = rows.reshape(n_ctx, exp_dev, capacity, feat_dev)
-        return rows.transpose(1, 0, 2, 3).reshape(exp_dev, n_ctx * capacity, feat_dev)
-
-    rows_recv, grads_recv = by_expert(rows_recv), by_expert(grads_recv)
-    pre_act = sum_scatter(
-        jnp.einsum("erf,efh->erh", rows_recv, w_in, preferred_element_type=jnp.float32)
-    )
-    pre_grad = gather((act_grad * gelu_slope(pre_act)).astype(jnp.bfloat16))
-    act_shard, pre_grad = lax.optimization_barrier(
-        (gelu_tanh(pre_act).astype(jnp.bfloat16), pre_grad)
-    )
-    activated = gather(act_shard)
-    row_grad = jnp.einsum(
-        "erh,efh->erf", pre_grad, w_in, preferred_element_type=jnp.float32
-    ).astype(jnp.bfloat16)
-    input_grad, query_grad, key_grad, value_grad = backward_call(
+    activated, row_grad, w_in_grad = experts_call(rows_recv, act_grad, w_in)
+    layer_out, input_grad, query_grad, key_grad, value_grad, w_out_grad = backward_call(
         queries,
         kv_all,
         lse,
         attn,
-        jnp.broadcast_to(ends[None, :], (8, tok_rows)).astype(jnp.int32),
+        jnp.broadcast_to(ends[None, :], (8, tok_rows)),
         out_grad,
         inv_wide,
-        pick_both.reshape(n_ctx, exp_dev * capacity, tok_rows),
-        by_source(row_grad),
-    )
-    w_in_grad = jnp.einsum(
-        "erf,erh->efh", rows_recv, pre_grad, preferred_element_type=jnp.float32
-    ).astype(jnp.bfloat16)
-    expert_out = jnp.einsum(
-        "erh,ehf->erf", activated, w_out, preferred_element_type=jnp.float32
-    ).astype(jnp.bfloat16)
-    returned = jnp.dot(pick_two.T, to_tokens(expert_out), preferred_element_type=jnp.float32)
-    combined = (
-        route_gates[:, 0:1] * returned[:tok_rows] + route_gates[:, 1:2] * returned[tok_rows:]
-    )
-    layer_out = (mixed_f + combined).astype(jnp.bfloat16)
-    w_out_grad = jnp.einsum(
-        "erh,erf->ehf", activated, grads_recv, preferred_element_type=jnp.float32
-    ).astype(jnp.bfloat16)
+        rows_wide,
+        row_grad.reshape(n_ctx, exp_dev * capacity, feat_dev),
+        activated,
+        w_out,
+        grads_recv,
+        mixed,
+        gates_wide,
+    )
     return (
         layer_out,
         input_grad,

time: 481 us -> 341 us (0.71)
  waiting for transfers between devices: 171 us -> 0 us
  Pallas kernels: 230 us -> 314 us
  matrix products: 31.6 us -> 0 us
  between operations: 14 us -> 0.73 us
  other arithmetic: 12.6 us -> 4.18 us
  starting transfers between devices: 6.69 us -> 0 us
  local copies, waits for them, and re-layouts: 14.3 us -> 19.6 us
    pallas_call x1 -> x2, Pallas kernels: 86.7 us -> 198 us  [the longest x1 109 us: experts_call(): pl.pallas_call(experts_kernel, out_shape=(shape((192, 1536), bf), shape((...]
    all_gather x2 -> x0, waiting for transfers between devices: 111 us -> none  [gather(): full = lax.all_gather(shard, 'grp', axis=0, tiled=True)]
    reduce_scatter x1 -> x0, waiting for transfers between devices: 60.8 us -> none  [sum_scatter(): lax.psum_scatter(flat, 'grp', scatter_dimension=0, tiled=True)]
    dot_general x6 -> x0, matrix products: 31.6 us -> none  [the longest x1 7.41 us: shards(): jnp.einsum('erh,erf->ehf', activated, grads_recv, preferred_element_type=...]
    pallas_call x1, Pallas kernels: 144 us -> 116 us  [forward_call(): pl.pallas_call(forward_kernel, out_shape=(shape((256, 512), bf), shape((4...]
    unnamed x33 -> x13, local copies, waits for them, and re-layouts: 3.87 us -> 13.8 us
    all_to_all x1 -> x0, starting transfers between devices: 6.57 us -> none  [to_tokens(): lax.all_to_all(by_source(rows), 'ctx', split_axis=0, concat_axis=0, tiled...]
    convert_element_type x3 -> x0, other arithmetic: 5.6 us -> none  [the longest x1 3.27 us: shards(): pre_grad = gather((act_grad * gelu_slope(pre_act)).astype(jnp.bfloat16))]
  transfers between devices with their start and end apart: 4 -> 0, of which waited for: 3 -> 0; matrix products, arithmetic and copies ran while one was open for 5% -> 0% of each run, Pallas kernels for 18% -> 0%
where the time goes in v4:
time: 341 us; the launch traced here: 338 us
  Pallas kernels  314 us (92%)
  local copies, waits for them, and re-layouts  19.6 us (6%)
  other arithmetic  4.18 us (1%)
    pallas_call x1, Pallas kernels, forward_call(): pl.pallas_call(forward_kernel, out_shape=(shape((256, 512), bf), shape((4...  116 us
    pallas_call x1, Pallas kernels, experts_call(): pl.pallas_call(experts_kernel, out_shape=(shape((192, 1536), bf), shape((...  109 us
    pallas_call x1, Pallas kernels, backward_call(): pl.pallas_call(backward_kernel, out_shape=(shape((256, 512), bf),) * 5 +...  89.5 us
    unnamed x13, local copies, waits for them, and re-layouts  13.8 us

profile of v4, /device:TPU:0, one launch (start us, length us, event | category | flops | bytes accessed | tf_op | source)
XLA Modules:
  0.0 338.2 jit_solution(3611160906644858473)
XLA Ops:
  0.6 0.8 fusion.6
  1.4 0.7 copy.38
  2.4 0.6 broadcast_in_dim.24.qend_ref
  3.0 0.8 broadcast_in_dim.21.qend_ref
  3.7 0.8 copy.39
  4.9 1.2 reduce-window.19
  6.0 0.2 slice_reduce_fusion
  6.4 0.1 reduce_sum.12
  6.6 0.7 add_bitcast_fusion.1
  7.3 0.6 broadcast_in_dim.23.rows_ref
  8.0 1.5 broadcast_in_dim.25.gates_ref
  9.5 1.1 fusion
  10.6 0.8 pad_maximum_fusion.gated_ref
  11.4 115.7 %forward.1 = (bf16[256,512]{1,0:T(8,128)(2,1)}, f32[4,8,256]{2,1,0:T(8,128)}, bf16[256,512]{1,0:T(8,128)(2,1)}, f32[256,128]{1,0:T(8,128)}, bf16[16,96,512]{2,1,...) custom-call(bf16[256,512]{1,0:T(8,128)(2,1)} %q_ref.3, ...), custom_call_target="tpu_custom_call" | custom-call | tf_op jit(solution)/shard_map/forward/pallas_call | solution.py:601
  127.0 108.6 %experts.1 = (bf16[192,1536]{1,0:T(8,128)(2,1)}, bf16[16,2,48,512]{3,2,1,0:T(8,128)(2,1)}, bf16[2,512,1536]{2,1,0:T(8,128)(2,1)}) custom-call(bf16[16,96,512]{2,1,0:T(8,128)(2,1)} %get-tuple-element.28.x_ref, f32[192,1536]{1,0:T(8,128)} %get-tuple-element.29.act_grad_ref, bf16[2,512,1536]{2,1,0:T(8,128)(2,1)} %w_in_ref.1), custom_call_target="tpu_custom_call" | custom-call | tf_op jit(solution)/shard_map/experts/pallas_call | solution.py:333
  235.7 89.5 %backward.1 = (bf16[256,512]{1,0:T(8,128)(2,1)}, bf16[256,512]{1,0:T(8,128)(2,1)}, bf16[256,512]{1,0:T(8,128)(2,1)}, bf16[256,512]{1,0:T(8,128)(2,1)}, bf16[256,...) custom-call(bf16[256,512]{1,0:T(8,128)(2,1)} %q_ref.3, bf16[2,4,2,2,256,512]{5,4,3,2,1,0:T(8,128)(2,1)} %get-tuple-element.24.kv_ref, ...), custom_call_target="tpu_custom_call" | custom-call | tf_op jit(solution)/shard_map/backward/pallas_call | solution.py:850
  325.2 1.7 copy.53
  326.8 1.7 copy.54
  328.5 1.7 copy.55
  330.2 1.7 copy.56
  331.8 1.7 copy.57
  333.5 1.7 copy.58
  335.2 1.4 copy-done.1
  336.5 1.7 copy.59
  (15 shorter events, 0.8 us)
Async XLA Ops:
  235.6 97.9 %copy-start = (bf16[2,512,1536]{2,1,0:T(8,128)(2,1)S(1)}, bf16[2,512,1536]{2,1,0:T(8,128)(2,1)}, u32[]{:S(2)}) copy-start(bf16[2,512,1536]{2,1,0:T(8,128)(2,1)} %get-tuple-element.57) | copy-start | bytes 9437188
  333.5 3.0 copy-start.1

commit v5 on v4

--- a/solution.py
+++ b/solution.py
@@ -266,13 +266,16 @@
 
 
 def experts_kernel(
-    x_ref, act_grad_ref, w_in_ref,
+    x_ref, act_grad_ref, w_in_hbm,
     act_ref, rg_ref, w_in_grad_ref,
-    part, sums, full, rg_send,
+    part, sums, full, rg_send, w_in_ref, w_sem,
     s_send_sem, s_recv_sem, f_send_sem, f_recv_sem, r_send_sem, r_recv_sem,
 ):
     bf = jnp.bfloat16
+    w_copy = pltpu.make_async_copy(w_in_hbm, w_in_ref, w_sem)
+    w_copy.start()
     greet()
+    w_copy.wait()
     summing = GrpSum(112, part, sums, s_send_sem, s_recv_sem)
     gathering = GrpGather(112, full, f_send_sem, f_recv_sem)
     for dy, dz in CHUNK_ORDER:
@@ -337,13 +340,15 @@
             shape((16, 2, 48, 512), bf),
             shape((2, 512, 1536), bf),
         ),
-        in_specs=[vmem] * 3,
+        in_specs=[vmem] * 2 + [pl.BlockSpec(memory_space=pl.ANY)],
         out_specs=(vmem,) * 3,
         scratch_shapes=[
             pltpu.VMEM((2, 4, 192, 1536), bf),
             pltpu.VMEM((14, 192, 1536), bf),
             pltpu.VMEM((2, 4, 192, 1536), bf),
             pltpu.VMEM((2, 16, 48, 512), bf),
+            pltpu.VMEM((2, 512, 1536), bf),
+            pltpu.SemaphoreType.DMA,
             pltpu.SemaphoreType.DMA((14,)),
             pltpu.SemaphoreType.DMA((14,)),
             pltpu.SemaphoreType.DMA((14,)),
@@ -359,9 +364,10 @@
 
 
 def forward_kernel(
-    q_ref, k_ref, v_ref, res_ref, qend_ref, gated_ref, rows_ref, w_out_ref,
-    attn_ref, lse_ref, mixed_ref, inv_ref, xrecv_ref, grecv_ref, act_grad_ref, kv_out_ref,
-    kv, m_s, l_s, acc_s, gsend, xsend, part, sums, sq_send, sq_recv,
+    q_ref, k_ref, v_ref, res_ref, lengths_ref, routes_ref, gates_ref, og_ref, w_out_hbm,
+    rows_ref, qend_row_ref, attn_ref, lse_ref, mixed_ref, inv_ref, xrecv_ref, grecv_ref, act_grad_ref, kv_out_ref,
+    kv, m_s, l_s, acc_s, gsend, xsend, part, sums, sq_send, sq_recv, gated, qend_s, w_out_ref,
+    w_sem,
     kv_send_sem, kv_recv_sem, out_sem, g_send_sem, g_recv_sem, x_send_sem, x_recv_sem,
     p_send_sem, p_recv_sem, sq_send_sem, sq_recv_sem,
 ):
@@ -376,6 +382,8 @@
         there = lax.rem(yh + dy, 2) * 4 + lax.rem(x + dx, 4)
         return {"ctx": there * 2 + lax.rem(core + dc, 2)}
 
+    w_copy = pltpu.make_async_copy(w_out_hbm, w_out_ref, w_sem)
+    w_copy.start()
     greet()
 
     copies = {}
@@ -396,13 +404,25 @@
         move(own(which), (1, 0, 0, which), partner)
     for which in range(2):
         move(own(which), (0, 0, 1, which), sibling)
-    kv[0, 0, 0, 0] = k_ref[...]
-    kv[0, 0, 0, 1] = v_ref[...]
+    early = lax.broadcasted_iota(jnp.int32, (256, 256), 0) < lax.broadcasted_iota(
+        jnp.int32, (256, 256), 1
+    )
+    experts = [routes_ref[:, a : a + 1].astype(jnp.float32) for a in range(2)]
+    for a in range(2):
+        expert_row = jnp.transpose(jnp.broadcast_to(experts[a], (256, 128)))[0:8]
+        rank = jnp.zeros((1, 256), jnp.float32)
+        for b in range(2):
+            same = early & (experts[b] == expert_row[0:1])
+            rank += jnp.sum(jnp.where(same, 1.0, 0.0), axis=0, keepdims=True)
+        cols = slice(a * 256, a * 256 + 256)
+        rows_ref[:, cols] = (expert_row * 48 + rank).astype(jnp.int32)
+        gate = gates_ref[:, a : a + 1]
+        gated[cols, :] = (gate * og_ref[...].astype(jnp.float32)).astype(jnp.bfloat16)
 
     @pl.loop(0, 16)
     def _(k):
         there = lax.rem(me + k, 16)
-        gsend[k] = dot_nn(pick_two(rows_ref, there), gated_ref[...]).astype(jnp.bfloat16)
+        gsend[k] = dot_nn(pick_two(rows_ref, there), gated[...]).astype(jnp.bfloat16)
 
         @pl.when(k > 0)
         def _():
@@ -414,6 +434,18 @@
         move(own(which), (0, 3, 0, which), right)
         move(own(which), (0, 1, 0, which), left)
     grecv_ref[me] = gsend[0]
+    kv[0, 0, 0, 0] = k_ref[...]
+    kv[0, 0, 0, 1] = v_ref[...]
+    pos_col = me * 256 + lax.broadcasted_iota(jnp.int32, (256, 128), 0)
+    pos_row = me * 256 + lax.broadcasted_iota(jnp.int32, (8, 256), 1)
+    ends_col, ends_row = jnp.full_like(pos_col, 4096), jnp.full_like(pos_row, 4096)
+    end = jnp.int32(0)
+    for f in range(16):
+        end = end + lengths_ref[f]
+        ends_col = jnp.minimum(ends_col, jnp.where(end > pos_col, end, 4096))
+        ends_row = jnp.minimum(ends_row, jnp.where(end > pos_row, end, 4096))
+    qend_s[...] = ends_col
+    qend_row_ref[...] = ends_row
     summing = GrpSum(48, part, sums, p_send_sem, p_recv_sem)
     m_s[...] = jnp.full_like(m_s, LOW)
     l_s[...] = jnp.zeros_like(l_s)
@@ -443,7 +475,7 @@
         outs.append(copy)
         there = lax.rem(yh + dy, 2) * 4 + lax.rem(x + dx, 4)
         lane = lax.broadcasted_iota(jnp.int32, (256, 256), 1)
-        qend = qend_ref[:, 0:1]
+        qend = qend_s[:, 0:1]
         limits = [qend - (there * 512 + lax.rem(core + dc, 2) * 256) for dc in range(2)]
 
         @pl.loop(0, 4)
@@ -474,6 +506,8 @@
         move(kv.at[1, 0, 0, which], (1, 1, 0, which), left)
         move(kv.at[1, 0, 0, which], (1, 0, 1, which), sibling)
 
+    relay(0)
+
     @pl.loop(1, 16)
     def _(k):
         source = lax.rem(me + 16 - k, 16)
@@ -481,6 +515,7 @@
             gsend.at[k], grecv_ref.at[source], g_send_sem.at[k], g_recv_sem.at[k], {"ctx": source}
         ).wait_recv()
 
+    w_copy.wait()
     for dy, dz in CHUNK_ORDER:
         expert, _ = chunk_of(dy, dz)
         rows = chunk_rows(grecv_ref, dy, dz)
@@ -492,7 +527,6 @@
 
         summing.send_first(dy, dz)
 
-    relay(0)
     attend(0, 3)
     attend(0, 1)
     relay(1)
@@ -594,13 +628,15 @@
         copy.wait()
 
 
-def forward_call(q, k, v, res, qend, gated, rows, w_out):
+def forward_call(*operands):
     bf, f32 = jnp.bfloat16, jnp.float32
     vmem = pl.BlockSpec(memory_space=pltpu.VMEM)
     shape = jax.ShapeDtypeStruct
     return pl.pallas_call(
         forward_kernel,
         out_shape=(
+            shape((8, 512), jnp.int32),
+            shape((8, 256), jnp.int32),
             shape((256, 512), bf),
             shape((4, 8, 256), f32),
             shape((256, 512), bf),
@@ -610,8 +646,11 @@
             shape((192, 1536), f32),
             shape((2, 4, 2, 2, 256, 512), bf),
         ),
-        in_specs=[vmem] * 8,
-        out_specs=[vmem] * 7 + [pl.BlockSpec(memory_space=pl.ANY)],
+        in_specs=[vmem] * 4
+        + [pl.BlockSpec(memory_space=pltpu.SMEM)]
+        + [vmem] * 3
+        + [pl.BlockSpec(memory_space=pl.ANY)],
+        out_specs=[vmem] * 9 + [pl.BlockSpec(memory_space=pl.ANY)],
         scratch_shapes=[
             pltpu.VMEM((2, 4, 2, 2, 256, 512), bf),
             pltpu.VMEM((4, 256, 128), f32),
@@ -623,6 +662,10 @@
             pltpu.VMEM((14, 192, 1536), bf),
             pltpu.VMEM((8, 256), f32),
             pltpu.VMEM((8, 8, 256), f32),
+            pltpu.VMEM((512, 512), bf),
+            pltpu.VMEM((256, 128), jnp.int32),
+            pltpu.VMEM((2, 1536, 512), bf),
+            pltpu.SemaphoreType.DMA,
             pltpu.SemaphoreType.DMA((30,)),
             pltpu.SemaphoreType.DMA((2, 4, 2, 2)),
             pltpu.SemaphoreType.DMA((2, 4)),
@@ -639,14 +682,17 @@
             collective_id=0, has_side_effects=True, vmem_limit_bytes=56 * 2**20
         ),
         name="forward",
-    )(q, k, v, res, qend, gated, rows, w_out)
+    )(*operands)
+
+
+TERM_ORDER = [(1, 3), (1, 1), (1, 2), (1, 0), (0, 3), (0, 1), (0, 2), (0, 0)]
 
 
 def backward_kernel(
-    q_ref, kv_ref, lse_ref, attn_ref, qend_ref, og_ref, inv_ref, rows_ref, rg_ref, act_ref,
-    w_out_ref, g_ref, mixed_ref, gates_ref,
+    q_ref, kv_hbm, lse_ref, attn_ref, qend_ref, og_ref, inv_ref, rows_ref, rg_ref, act_ref,
+    w_out_hbm, g_hbm, mixed_ref, gates_ref,
     layer_ref, ig_ref, dq_ref, dk_ref, dv_ref, w_out_grad_ref,
-    full, eo_send, eo_recv, normed_grad, returned, row_dot, dqt, own_terms, sib_send, sib_recv, ring_send,
+    full, eo_send, eo_recv, kv_ref, w_out_ref, g_ref, load_sem, normed_grad, returned, row_dot, dqt, own_terms, sib_send, sib_recv, ring_send,
     ring_recv, part_send, part_recv,
     f_send_sem, f_recv_sem, r_send_sem, r_recv_sem, sib_send_sem, sib_recv_sem, ring_send_sem, ring_recv_sem,
     part_send_sem, part_recv_sem,
@@ -664,10 +710,23 @@
 
     right, left = device(0, 1, 0), device(0, 3, 0)
     sibling, partner = device(0, 0, 1), device(1, 0, 0)
+    loads = {}
+    for dy, dx in TERM_ORDER:
+        loads[(dy, dx)] = pltpu.make_async_copy(
+            kv_hbm.at[dy, dx], kv_ref.at[dy, dx], load_sem.at[dy * 4 + dx]
+        )
+    w_load = pltpu.make_async_copy(w_out_hbm, w_out_ref, load_sem.at[8])
+    g_load = pltpu.make_async_copy(g_hbm, g_ref, load_sem.at[9])
+    loads[(1, 3)].start()
+    loads[(1, 1)].start()
     greet()
     gathering = GrpGather(48, full, f_send_sem, f_recv_sem)
     full[0, 0] = act_ref[...]
     gathering.send_own()
+    for dy, dx in TERM_ORDER[2:]:
+        loads[(dy, dx)].start()
+    w_load.start()
+    g_load.start()
     dqt[...] = jnp.zeros_like(dqt)
     normed_grad[...] = jnp.zeros_like(normed_grad)
 
@@ -686,6 +745,7 @@
     scale = HEAD_DIM**-0.5
 
     def terms(dy, dx):
+        loads[(dy, dx)].wait()
         there = lax.rem(yh + dy, 2) * 4 + lax.rem(x + dx, 4)
         sub = lax.broadcasted_iota(jnp.int32, (256, 256), 0)
         qend = qend_ref[0:1, :]
@@ -770,6 +830,7 @@
     send_ring(1, 1, 1, False)
     terms(1, 2)
     terms(1, 0)
+    w_load.wait()
     gathering.pass_rest()
     for dz in (1, 3, 2):
         gathering.pass_head(dz)
@@ -817,6 +878,7 @@
     for which in range(2):
         part_copy(which).wait_send()
 
+    g_load.wait()
     for dy in range(2):
         expert, _ = chunk_of(dy, 0)
 
@@ -837,7 +899,9 @@
 
     for h in range(4):
         cols = slice(h * 128, h * 128 + 128)
-        sums = gates_ref[0] * returned[0:256, cols] + gates_ref[1] * returned[256:512, cols]
+        sums = (
+            gates_ref[:, 0:1] * returned[0:256, cols] + gates_ref[:, 1:2] * returned[256:512, cols]
+        )
         layer_ref[:, cols] = (mixed_ref[:, cols].astype(f32) + sums).astype(bf)
 
     gathering.drain()
@@ -846,16 +910,21 @@
 def backward_call(*operands):
     bf, f32 = jnp.bfloat16, jnp.float32
     vmem = pl.BlockSpec(memory_space=pltpu.VMEM)
+    anywhere = pl.BlockSpec(memory_space=pl.ANY)
     shape = jax.ShapeDtypeStruct
     return pl.pallas_call(
         backward_kernel,
         out_shape=(shape((256, 512), bf),) * 5 + (shape((2, 1536, 512), bf),),
-        in_specs=[vmem] * 14,
+        in_specs=[vmem, anywhere] + [vmem] * 8 + [anywhere] * 2 + [vmem] * 2,
         out_specs=(vmem,) * 6,
         scratch_shapes=[
             pltpu.VMEM((2, 4, 192, 1536), bf),
             pltpu.VMEM((2, 16, 48, 512), bf),
             pltpu.VMEM((16, 2, 48, 512), bf),
+            pltpu.VMEM((2, 4, 2, 2, 256, 512), bf),
+            pltpu.VMEM((2, 1536, 512), bf),
+            pltpu.VMEM((16, 96, 512), bf),
+            pltpu.SemaphoreType.DMA((10,)),
             pltpu.VMEM((256, 512), f32),
             pltpu.VMEM((512, 512), f32),
             pltpu.VMEM((4, 8, 256), f32),
@@ -885,43 +954,49 @@
     )(*operands)
 
 
+def publish_kernel(*refs):
+    count = len(refs) // 2
+    sems = refs[-1]
+    copies = [
+        pltpu.make_async_copy(refs[n], refs[count + n], sems.at[n]) for n in range(count)
+    ]
+    for copy in copies:
+        copy.start()
+    for copy in copies:
+        copy.wait()
+
+
+def publish(*arrays):
+    anywhere = pl.BlockSpec(memory_space=pl.ANY)
+    return pl.pallas_call(
+        publish_kernel,
+        out_shape=tuple(jax.ShapeDtypeStruct(a.shape, a.dtype) for a in arrays),
+        in_specs=[anywhere] * len(arrays),
+        out_specs=(anywhere,) * len(arrays),
+        scratch_shapes=[pltpu.SemaphoreType.DMA((len(arrays),))],
+        compiler_params=pltpu.CompilerParams(vmem_limit_bytes=56 * 2**20),
+        name="publish",
+    )(*arrays)
+
+
 def shards(
     residual, queries, keys, values, frame_lengths, routes, route_gates, w_in, w_out, out_grad
 ):
     n_ctx = lax.axis_size("ctx")
     tok_rows, feat_dev = residual.shape
     exp_dev = w_in.shape[0]
-    seq_len = tok_rows * n_ctx
-    experts_all = exp_dev * n_ctx
-    capacity = 6 * tok_rows // experts_all
-    expert_flat = routes.reshape(-1)
-    onehot = (expert_flat[:, None] == jnp.arange(experts_all, dtype=jnp.int32)[None, :]).astype(
-        jnp.int32
-    )
-    earlier = jnp.cumsum(onehot, axis=0) - onehot
-    ranks = jnp.sum(earlier * onehot, axis=1)
-    row_index = (expert_flat * capacity + ranks).reshape(tok_rows, 2).T.reshape(1, 2 * tok_rows)
-    rows_wide = jnp.broadcast_to(row_index, (8, 2 * tok_rows))
-    out_grad_f = out_grad.astype(jnp.float32)
-    gated = jnp.concatenate(
-        [(route_gates[:, a : a + 1] * out_grad_f).astype(jnp.bfloat16) for a in range(2)], axis=0
-    )
-    gates_wide = jnp.broadcast_to(route_gates.T[:, :, None], (2, tok_rows, 128))
-    ctx_index = lax.axis_index("ctx")
-    frame_ends = jnp.cumsum(frame_lengths)
-    positions = ctx_index * tok_rows + jnp.arange(tok_rows, dtype=jnp.int32)
-    ends = jnp.min(
-        jnp.where(frame_ends[None, :] > positions[:, None], frame_ends[None, :], seq_len), axis=1
-    ).astype(jnp.int32)
-    attn, lse, mixed, inv_wide, rows_recv, grads_recv, act_grad, kv_all = forward_call(
-        queries,
-        keys,
-        values,
-        residual,
-        jnp.broadcast_to(ends[:, None], (tok_rows, 128)),
-        gated,
-        rows_wide,
-        w_out,
+    rows_wide, qend_row, attn, lse, mixed, inv_wide, rows_recv, grads_recv, act_grad, kv_all = (
+        forward_call(
+            queries,
+            keys,
+            values,
+            residual,
+            frame_lengths,
+            routes,
+            route_gates,
+            out_grad,
+            w_out,
+        )
     )
     activated, row_grad, w_in_grad = experts_call(rows_recv, act_grad, w_in)
     layer_out, input_grad, query_grad, key_grad, value_grad, w_out_grad = backward_call(
@@ -929,18 +1004,18 @@
         kv_all,
         lse,
         attn,
-        jnp.broadcast_to(ends[None, :], (8, tok_rows)),
+        qend_row,
         out_grad,
         inv_wide,
         rows_wide,
-        row_grad.reshape(n_ctx, exp_dev * capacity, feat_dev),
+        row_grad.reshape(n_ctx, exp_dev * row_grad.shape[2], feat_dev),
         activated,
         w_out,
         grads_recv,
         mixed,
-        gates_wide,
+        route_gates,
     )
-    return (
+    return publish(
         layer_out,
         input_grad,
         query_grad,

time: 341 us -> 551 us (1.62)
  Pallas kernels: 314 us -> 543 us
  local copies, waits for them, and re-layouts: 19.6 us -> 2.95 us
    pallas_call x1 -> x2, Pallas kernels: 116 us -> 352 us  [the longest x1 231 us: publish(): pl.pallas_call(publish_kernel, out_shape=tuple((jax.ShapeDtypeStruct(a.sh...]
    unnamed x13 -> x2, local copies, waits for them, and re-layouts: 13.8 us -> 2.95 us
    pallas_call x1, Pallas kernels: 109 us -> 102 us  [experts_call(): pl.pallas_call(experts_kernel, out_shape=(shape((192, 1536), bf), shape((...]
where the time goes in v5:
time: 551 us; the launch traced here: 547 us
  Pallas kernels  543 us (99%)
    pallas_call x1, Pallas kernels, publish(): pl.pallas_call(publish_kernel, out_shape=tuple((jax.ShapeDtypeStruct(a.sh...  231 us
    pallas_call x1, Pallas kernels, forward_call(): pl.pallas_call(forward_kernel, out_shape=(shape((8, 512), jnp.int32), sha...  120 us
    pallas_call x1, Pallas kernels, experts_call(): pl.pallas_call(experts_kernel, out_shape=(shape((192, 1536), bf), shape((...  102 us
    pallas_call x1, Pallas kernels, backward_call(): pl.pallas_call(backward_kernel, out_shape=(shape((256, 512), bf),) * 5 +...  89.5 us

profile of v5, /device:TPU:0, one launch (start us, length us, event | category | flops | bytes accessed | tf_op | source)
XLA Modules:
  0.0 547.2 jit_solution(16226871591421544815)
XLA Ops:
  0.6 1.5 copy.18.gates_ref
  2.1 1.5 copy.17.routes_ref
  3.6 120.2 %forward.1 = (s32[8,512]{1,0:T(8,128)}, s32[8,256]{1,0:T(8,128)}, bf16[256,512]{1,0:T(8,128)(2,1)}, f32[4,8,256]{2,1,0:T(8,128)}, bf16[256,512]{1,0:T(8,128)(2,1...) custom-call(bf16[256,512]{1,0:T(8,128)(2,1)} %q_ref.3, ...), custom_call_target="tpu_custom_call" | custom-call | tf_op jit(solution)/shard_map/forward/pallas_call | solution.py:635
  123.8 102.3 %experts.1 = (bf16[192,1536]{1,0:T(8,128)(2,1)}, bf16[16,2,48,512]{3,2,1,0:T(8,128)(2,1)}, bf16[2,512,1536]{2,1,0:T(8,128)(2,1)}) custom-call(bf16[16,96,512]{2,1,0:T(8,128)(2,1)} %get-tuple-element.32.x_ref, f32[192,1536]{1,0:T(8,128)} %get-tuple-element.33.act_grad_ref, bf16[2,512,1536]{2,1,0:T(8,128)(2,1)} %w_in_hbm.1), custom_call_target="tpu_custom_call" | custom-call | tf_op jit(solution)/shard_map/experts/pallas_call | solution.py:336
  226.1 89.5 %backward.1 = (bf16[256,512]{1,0:T(8,128)(2,1)}, bf16[256,512]{1,0:T(8,128)(2,1)}, bf16[256,512]{1,0:T(8,128)(2,1)}, bf16[256,512]{1,0:T(8,128)(2,1)}, bf16[256,...) custom-call(bf16[256,512]{1,0:T(8,128)(2,1)} %q_ref.3, bf16[2,4,2,2,256,512]{5,4,3,2,1,0:T(8,128)(2,1)} %get-tuple-element.26.kv_hbm, ...), custom_call_target="tpu_custom_call" | custom-call | tf_op jit(solution)/shard_map/backward/pallas_call | solution.py:915
  315.6 231.5 %publish.1 = (bf16[256,512]{1,0:T(8,128)(2,1)}, bf16[256,512]{1,0:T(8,128)(2,1)}, bf16[256,512]{1,0:T(8,128)(2,1)}, bf16[256,512]{1,0:T(8,128)(2,1)}, bf16[256,5...) custom-call(bf16[256,512]{1,0:T(8,128)(2,1)} %get-tuple-element.38.refs_0_, ...), custom_call_target="tpu_custom_call" | custom-call | tf_op jit(solution)/shard_map/publish/pallas_call | solution.py:971

commit v6 on v5

--- a/solution.py
+++ b/solution.py
@@ -1,3 +1,5 @@
+import functools
+
 import jax
 import jax.numpy as jnp
 from jax import lax
@@ -93,89 +95,109 @@
         self.send_sem, self.recv_sem = send_sem, recv_sem
         self.head, self.rest = pl.ds(0, cut), pl.ds(cut, 192 - cut)
 
-    def copy(self, number):
-        part, head, rest = self.part, self.head, self.rest
-        if number < 4:
-            src, rows, where = part.at[1, number, head], head, grp_device(1, 0)
-        elif number < 10:
-            dz, dy = (number - 4) // 2 + 1, (number - 4) % 2
-            src, rows, where = part.at[dy, dz, rest], rest, grp_device(0, dz)
-        elif number < 13:
-            dz = number - 9
-            src, rows, where = part.at[0, dz, head], head, grp_device(0, dz)
-        else:
-            src, rows, where = part.at[1, 0, rest], rest, grp_device(1, 0)
+    def halves(self, group):
+        start, size = (0, self.cut) if group == 2 else (self.cut, 192 - self.cut)
+        low = size // 32 * 16
+        return (start, low), (start + low, size - low)
+
+    def make(self, number, src, slot, rows, where):
         return remote(
             src,
-            self.recv.at[number, rows],
+            self.recv.at[slot, rows],
             self.send_sem.at[number],
             self.recv_sem.at[number],
             where,
         )
 
+    def partner_head(self, dz):
+        return self.make(dz, self.part.at[1, dz, self.head], dz, self.head, grp_device(1, 0))
+
+    def partner_rest(self):
+        return self.make(22, self.part.at[1, 0, self.rest], 13, self.rest, grp_device(1, 0))
+
+    def along(self, group, kind):
+        dy, base = (0 if group == 2 else group), 4 + 3 * group
+        low, high = [pl.ds(*half) for half in self.halves(group)]
+        dz, rows, slot, to = [
+            (2, low, base, 1),
+            (2, high, base, 3),
+            (1, high, base + 1, 1),
+            (3, low, base + 2, 3),
+            (1, low, base + 1, 1),
+            (3, high, base + 2, 3),
+        ][kind]
+        number = 4 + 6 * group + kind
+        return self.make(number, self.part.at[dy, dz, rows], slot, rows, grp_device(0, to))
+
+    def start_along(self, group, dz):
+        for kind in {0: [], 1: [2], 2: [0, 1], 3: [3]}[dz]:
+            self.along(group, kind).start()
+
     def send_first(self, dy, dz):
         if dy == 1:
-            self.copy(dz).start()
-        if dz > 0:
-            self.copy(4 + (dz - 1) * 2 + dy).start()
-
-    def add(self, target, start, size, slots, out):
+            self.partner_head(dz).start()
+        self.start_along(dy, dz)
+
+    def add(self, target, start, size, slots, out=None):
+        def keep(rows, total):
+            self.part[target[0], target[1], rows, :] = total.astype(jnp.bfloat16)
+
         @pl.loop(0, size // 16)
         def _(step):
             rows = pl.ds(pl.multiple_of(start + step * 16, 16), 16)
             total = self.part[target[0], target[1], rows, :].astype(jnp.float32)
             for slot in slots:
                 total += self.recv[slot, rows, :].astype(jnp.float32)
-            out(rows, total)
+            (out or keep)(rows, total)
+
+    def relay(self, group):
+        dy, base = (0 if group == 2 else group), 4 + 3 * group
+        low, high = self.halves(group)
+        self.along(group, 0).wait_recv()
+        self.add((dy, 1), *low, [base])
+        self.along(group, 4).start()
+        self.along(group, 1).wait_recv()
+        self.add((dy, 3), *high, [base])
+        self.along(group, 5).start()
 
     def second(self, dz):
-        self.copy(dz).wait_recv()
-
-        def out(rows, total):
-            self.part[0, dz, rows, :] = total.astype(jnp.bfloat16)
-
-        self.add((0, dz), 0, self.cut, [dz], out)
-        self.copy(9 + dz).start()
+        self.partner_head(dz).wait_recv()
+        self.add((0, dz), 0, self.cut, [dz])
+        self.start_along(2, dz)
+
+    def wait_along(self, group):
+        for kind in range(2, 6):
+            self.along(group, kind).wait_recv()
 
     def second_rest(self):
-        for number in (5, 7, 9):
-            self.copy(number).wait_recv()
-
-        def out(rows, total):
-            self.part[1, 0, rows, :] = total.astype(jnp.bfloat16)
-
-        self.add((1, 0), self.cut, 192 - self.cut, [5, 7, 9], out)
-        self.copy(13).start()
+        self.wait_along(1)
+        self.add((1, 0), self.cut, 192 - self.cut, [8, 9])
+        self.partner_rest().start()
 
     def finish(self, out):
-        for number in (0, 4, 6, 8, 10, 11, 12, 13):
-            self.copy(number).wait_recv()
-        self.add((0, 0), 0, self.cut, [0, 10, 11, 12], out)
-        self.add((0, 0), self.cut, 192 - self.cut, [4, 6, 8, 13], out)
+        self.partner_head(0).wait_recv()
+        self.wait_along(2)
+        self.add((0, 0), 0, self.cut, [0, 11, 12], out)
+        self.wait_along(0)
+        self.partner_rest().wait_recv()
+        self.add((0, 0), self.cut, 192 - self.cut, [5, 6, 13], out)
 
     def drain(self):
-        for number in range(14):
-            self.copy(number).wait_send()
+        for dz in range(4):
+            self.partner_head(dz).wait_send()
+        for group in range(3):
+            for kind in range(6):
+                self.along(group, kind).wait_send()
+        self.partner_rest().wait_send()
 
 
 class GrpGather:
     def __init__(self, cut, full, send_sem, recv_sem):
-        self.full, self.send_sem, self.recv_sem = full, send_sem, recv_sem
+        self.cut, self.full, self.send_sem, self.recv_sem = cut, full, send_sem, recv_sem
         self.head, self.rest = pl.ds(0, cut), pl.ds(cut, 192 - cut)
-
-    def copy(self, number):
-        head, rest = self.head, self.rest
-        if number < 3:
-            dz = number + 1
-            src, dst, rows, where = (0, 0), (0, 4 - dz), head, grp_device(0, dz)
-        elif number == 3:
-            src, dst, rows, where = (0, 0), (1, 0), rest, grp_device(1, 0)
-        elif number < 8:
-            dz = number - 4
-            src, dst, rows, where = (0, dz), (1, dz), head, grp_device(1, 0)
-        else:
-            dz, dy = (number - 8) // 2 + 1, (number - 8) % 2
-            src, dst, rows, where = (dy, 0), (dy, 4 - dz), rest, grp_device(0, dz)
+        self.waited = set()
+
+    def make(self, number, src, dst, rows, where):
         return remote(
             self.full.at[src[0], src[1], rows],
             self.full.at[dst[0], dst[1], rows],
@@ -184,31 +206,57 @@
             where,
         )
 
+    def copy(self, number):
+        if number < 12:
+            group, kind = number // 4, number % 4
+            dy = 1 if group == 2 else 0
+            start, size = (0, self.cut) if group == 0 else (self.cut, 192 - self.cut)
+            low = size // 32 * 16
+            src, dst, rows, to = [
+                (0, 3, (start, size), 1),
+                (0, 1, (start, size), 3),
+                (3, 2, (start, low), 1),
+                (1, 2, (start + low, size - low), 3),
+            ][kind]
+            return self.make(number, (dy, src), (dy, dst), pl.ds(*rows), grp_device(0, to))
+        if number < 16:
+            dz = number - 12
+            return self.make(number, (0, dz), (1, dz), self.head, grp_device(1, 0))
+        return self.make(number, (0, 0), (1, 0), self.rest, grp_device(1, 0))
+
+    def start(self, *numbers):
+        for number in numbers:
+            self.copy(number).start()
+
+    def wait(self, *numbers):
+        for number in numbers:
+            if number not in self.waited:
+                self.waited.add(number)
+                self.copy(number).wait_recv()
+
     def send_own(self):
-        self.copy(3).start()
-        for number in (0, 2, 1):
-            self.copy(number).start()
-        self.copy(4).start()
-        for dz in (1, 3, 2):
-            self.copy(8 + (dz - 1) * 2).start()
+        self.start(16, 0, 1, 12, 4, 5)
+
+    def relay(self, group):
+        for kind in range(2):
+            self.wait(4 * group + kind)
+            self.start(4 * group + 2 + kind)
+
+    def pass_head(self, dz):
+        self.wait(*{1: [1], 2: [2, 3], 3: [0]}[dz])
+        self.start(12 + dz)
 
     def pass_rest(self):
-        self.copy(3).wait_recv()
-        for dz in (1, 3, 2):
-            self.copy(8 + (dz - 1) * 2 + 1).start()
-
-    def pass_head(self, dz):
-        self.copy(3 - dz).wait_recv()
-        self.copy(4 + dz).start()
+        self.wait(16)
+        self.start(8, 9)
 
     def wait_chunk(self, dy, dz):
+        self.wait(*[4 + 4 * dy + kind for kind in {0: [], 1: [1], 2: [2, 3], 3: [0]}[dz]])
         if dy == 1:
-            self.copy(4 + dz).wait_recv()
-        if dz > 0:
-            self.copy(8 + (3 - dz) * 2 + dy).wait_recv()
+            self.wait(12 + dz, 16)
 
     def drain(self):
-        for number in range(14):
+        for number in range(17):
             self.copy(number).wait_send()
 
 
@@ -223,7 +271,7 @@
     return rows.reshape(192, 512)
 
 
-CHUNK_ORDER = [(1, 1), (1, 3), (1, 2), (1, 0), (0, 1), (0, 3), (0, 2), (0, 0)]
+CHUNK_ORDER = [(1, 2), (1, 1), (1, 3), (0, 2), (1, 0), (0, 1), (0, 3), (0, 0)]
 
 
 def return_rows(rows, dy, dz, send, recv, send_sem, recv_sem):
@@ -276,8 +324,8 @@
     w_copy.start()
     greet()
     w_copy.wait()
-    summing = GrpSum(112, part, sums, s_send_sem, s_recv_sem)
-    gathering = GrpGather(112, full, f_send_sem, f_recv_sem)
+    summing = GrpSum(96, part, sums, s_send_sem, s_recv_sem)
+    gathering = GrpGather(96, full, f_send_sem, f_recv_sem)
     for dy, dz in CHUNK_ORDER:
         expert, _ = chunk_of(dy, dz)
         rows = chunk_rows(x_ref, dy, dz)
@@ -288,8 +336,11 @@
             part[dy, dz, :, cols] = dot_nn(rows, w_in_ref[expert, :, cols]).astype(bf)
 
         summing.send_first(dy, dz)
-    for dz in (1, 3, 2):
+    summing.relay(1)
+    summing.relay(0)
+    for dz in (2, 1, 3):
         summing.second(dz)
+    summing.relay(2)
     summing.second_rest()
 
     def activate(rows, pre):
@@ -305,14 +356,19 @@
         return_rows(rows, dy, dz, rg_send, rg_ref, r_send_sem, r_recv_sem)
 
     row_grads(0, 0)
+    gathering.relay(0)
+    for dz in (3, 1):
+        gathering.pass_head(dz)
     gathering.pass_rest()
-    for dz in (1, 3, 2):
-        gathering.pass_head(dz)
-    for dz in (0, 1, 3, 2):
-        for dy in range(2):
-            if (dy, dz) != (0, 0):
-                gathering.wait_chunk(dy, dz)
-                row_grads(dy, dz)
+    gathering.relay(1)
+    gathering.pass_head(2)
+    for dy, dz in [(0, 1), (0, 3)]:
+        gathering.wait_chunk(dy, dz)
+        row_grads(dy, dz)
+    gathering.relay(2)
+    for dy, dz in [(1, 0), (1, 1), (1, 3), (0, 2), (1, 2)]:
+        gathering.wait_chunk(dy, dz)
+        row_grads(dy, dz)
     for dy in range(2):
         expert, _ = chunk_of(dy, 0)
 
@@ -349,10 +405,10 @@
             pltpu.VMEM((2, 16, 48, 512), bf),
             pltpu.VMEM((2, 512, 1536), bf),
             pltpu.SemaphoreType.DMA,
-            pltpu.SemaphoreType.DMA((14,)),
-            pltpu.SemaphoreType.DMA((14,)),
-            pltpu.SemaphoreType.DMA((14,)),
-            pltpu.SemaphoreType.DMA((14,)),
+            pltpu.SemaphoreType.DMA((23,)),
+            pltpu.SemaphoreType.DMA((23,)),
+            pltpu.SemaphoreType.DMA((17,)),
+            pltpu.SemaphoreType.DMA((17,)),
             pltpu.SemaphoreType.DMA((2, 16)),
             pltpu.SemaphoreType.DMA((2, 16)),
         ],
@@ -446,7 +502,7 @@
         ends_row = jnp.minimum(ends_row, jnp.where(end > pos_row, end, 4096))
     qend_s[...] = ends_col
     qend_row_ref[...] = ends_row
-    summing = GrpSum(48, part, sums, p_send_sem, p_recv_sem)
+    summing = GrpSum(96, part, sums, p_send_sem, p_recv_sem)
     m_s[...] = jnp.full_like(m_s, LOW)
     l_s[...] = jnp.zeros_like(l_s)
     acc_s[...] = jnp.zeros_like(acc_s)
@@ -530,12 +586,17 @@
     attend(0, 3)
     attend(0, 1)
     relay(1)
+    summing.relay(1)
+    summing.relay(0)
     attend(1, 0)
     for which in range(2):
         forward(0, 2, which)
     attend(0, 2)
+    for dz in (2, 1, 3):
+        summing.second(dz)
     attend(1, 3)
     attend(1, 1)
+    summing.relay(2)
     for which in range(2):
         forward(1, 2, which)
     attend(1, 2)
@@ -599,8 +660,6 @@
 
     xrecv_ref[me] = xsend[0]
 
-    for dz in (1, 3, 2):
-        summing.second(dz)
     summing.second_rest()
 
     def keep(rows, total):
@@ -673,8 +732,8 @@
             pltpu.SemaphoreType.DMA((16,)),
             pltpu.SemaphoreType.DMA((16,)),
             pltpu.SemaphoreType.DMA((16,)),
-            pltpu.SemaphoreType.DMA((14,)),
-            pltpu.SemaphoreType.DMA((14,)),
+            pltpu.SemaphoreType.DMA((23,)),
+            pltpu.SemaphoreType.DMA((23,)),
             pltpu.SemaphoreType.DMA((8,)),
             pltpu.SemaphoreType.DMA((8,)),
         ],
@@ -720,7 +779,7 @@
     loads[(1, 3)].start()
     loads[(1, 1)].start()
     greet()
-    gathering = GrpGather(48, full, f_send_sem, f_recv_sem)
+    gathering = GrpGather(64, full, f_send_sem, f_recv_sem)
     full[0, 0] = act_ref[...]
     gathering.send_own()
     for dy, dx in TERM_ORDER[2:]:
@@ -831,9 +890,11 @@
     terms(1, 2)
     terms(1, 0)
     w_load.wait()
+    gathering.relay(0)
+    for dz in (3, 1):
+        gathering.pass_head(dz)
     gathering.pass_rest()
-    for dz in (1, 3, 2):
-        gathering.pass_head(dz)
+    gathering.relay(1)
     send_ring(1, 2, 0, True)
     send_ring(1, 2, 1, True)
     expert_rows(0, 0)
@@ -843,6 +904,8 @@
     send_ring(1, 3, 1, True)
     send_ring(0, 3, 0, False)
     send_ring(0, 1, 1, False)
+    gathering.pass_head(2)
+    gathering.relay(2)
     terms(0, 2)
     for which in range(2):
         part_send[which] = total_of(1, 0, which, True).astype(bf)
@@ -936,8 +999,8 @@
             pltpu.VMEM((2, 4, 2, 256, 512), bf),
             pltpu.VMEM((2, 256, 512), bf),
             pltpu.VMEM((2, 256, 512), bf),
-            pltpu.SemaphoreType.DMA((14,)),
-            pltpu.SemaphoreType.DMA((14,)),
+            pltpu.SemaphoreType.DMA((17,)),
+            pltpu.SemaphoreType.DMA((17,)),
             pltpu.SemaphoreType.DMA((2, 16)),
             pltpu.SemaphoreType.DMA((2, 16)),
             pltpu.SemaphoreType.DMA((2, 4, 2)),
@@ -954,26 +1017,30 @@
     )(*operands)
 
 
-def publish_kernel(*refs):
-    count = len(refs) // 2
-    sems = refs[-1]
-    copies = [
-        pltpu.make_async_copy(refs[n], refs[count + n], sems.at[n]) for n in range(count)
-    ]
-    for copy in copies:
-        copy.start()
-    for copy in copies:
-        copy.wait()
+def publish_kernel(count, *refs):
+    sources, targets, held = refs[:count], refs[count : 2 * count], refs[2 * count : 3 * count]
+    in_sem, out_sem = refs[3 * count :]
+    reads = [pltpu.make_async_copy(sources[n], held[n], in_sem.at[n]) for n in range(count)]
+    writes = [pltpu.make_async_copy(held[n], targets[n], out_sem.at[n]) for n in range(count)]
+    for read in reads:
+        read.start()
+    for read, write in zip(reads, writes):
+        read.wait()
+        write.start()
+    for write in writes:
+        write.wait()
 
 
 def publish(*arrays):
     anywhere = pl.BlockSpec(memory_space=pl.ANY)
+    count = len(arrays)
     return pl.pallas_call(
-        publish_kernel,
+        functools.partial(publish_kernel, count),
         out_shape=tuple(jax.ShapeDtypeStruct(a.shape, a.dtype) for a in arrays),
-        in_specs=[anywhere] * len(arrays),
-        out_specs=(anywhere,) * len(arrays),
-        scratch_shapes=[pltpu.SemaphoreType.DMA((len(arrays),))],
+        in_specs=[anywhere] * count,
+        out_specs=(anywhere,) * count,
+        scratch_shapes=[pltpu.VMEM(a.shape, a.dtype) for a in arrays]
+        + [pltpu.SemaphoreType.DMA((count,))] * 2,
         compiler_params=pltpu.CompilerParams(vmem_limit_bytes=56 * 2**20),
         name="publish",
     )(*arrays)

time: 551 us -> 308 us (0.56)
  Pallas kernels: 543 us -> 300 us
    pallas_call x1, Pallas kernels: 231 us -> 5.6 us  [publish(): pl.pallas_call(functools.partial(publish_kernel, count), out_shape=tuple(...]
    pallas_call x1, Pallas kernels: 102 us -> 94.3 us  [experts_call(): pl.pallas_call(experts_kernel, out_shape=(shape((192, 1536), bf), shape((...]
    pallas_call x1, Pallas kernels: 120 us -> 113 us  [forward_call(): pl.pallas_call(forward_kernel, out_shape=(shape((8, 512), jnp.int32), sha...]
where the time goes in v6:
time: 308 us; the launch traced here: 304 us
  Pallas kernels  300 us (97%)
    pallas_call x1, Pallas kernels, forward_call(): pl.pallas_call(forward_kernel, out_shape=(shape((8, 512), jnp.int32), sha...  113 us
    pallas_call x1, Pallas kernels, experts_call(): pl.pallas_call(experts_kernel, out_shape=(shape((192, 1536), bf), shape((...  94.3 us
    pallas_call x1, Pallas kernels, backward_call(): pl.pallas_call(backward_kernel, out_shape=(shape((256, 512), bf),) * 5 +...  87.4 us

profile of v6, /device:TPU:0, one launch (start us, length us, event | category | flops | bytes accessed | tf_op | source)
XLA Modules:
  0.0 303.6 jit_solution(9709726546213073023)
XLA Ops:
  0.6 1.5 copy.18.gates_ref
  2.1 1.5 copy.17.routes_ref
  3.6 112.6 %forward.1 = (s32[8,512]{1,0:T(8,128)}, s32[8,256]{1,0:T(8,128)}, bf16[256,512]{1,0:T(8,128)(2,1)}, f32[4,8,256]{2,1,0:T(8,128)}, bf16[256,512]{1,0:T(8,128)(2,1...) custom-call(bf16[256,512]{1,0:T(8,128)(2,1)} %q_ref.3, ...), custom_call_target="tpu_custom_call" | custom-call | tf_op jit(solution)/shard_map/forward/pallas_call | solution.py:694
  116.1 94.3 %experts.1 = (bf16[192,1536]{1,0:T(8,128)(2,1)}, bf16[16,2,48,512]{3,2,1,0:T(8,128)(2,1)}, bf16[2,512,1536]{2,1,0:T(8,128)(2,1)}) custom-call(bf16[16,96,512]{2,1,0:T(8,128)(2,1)} %get-tuple-element.32.x_ref, f32[192,1536]{1,0:T(8,128)} %get-tuple-element.33.act_grad_ref, bf16[2,512,1536]{2,1,0:T(8,128)(2,1)} %w_in_hbm.1), custom_call_target="tpu_custom_call" | custom-call | tf_op jit(solution)/shard_map/experts/pallas_call | solution.py:392
  210.4 87.4 %backward.1 = (bf16[256,512]{1,0:T(8,128)(2,1)}, bf16[256,512]{1,0:T(8,128)(2,1)}, bf16[256,512]{1,0:T(8,128)(2,1)}, bf16[256,512]{1,0:T(8,128)(2,1)}, bf16[256,...) custom-call(bf16[256,512]{1,0:T(8,128)(2,1)} %q_ref.3, bf16[2,4,2,2,256,512]{5,4,3,2,1,0:T(8,128)(2,1)} %get-tuple-element.26.kv_hbm, ...), custom_call_target="tpu_custom_call" | custom-call | tf_op jit(solution)/shard_map/backward/pallas_call | solution.py:978
  297.9 5.6 %publish.1 = (bf16[256,512]{1,0:T(8,128)(2,1)}, bf16[256,512]{1,0:T(8,128)(2,1)}, bf16[256,512]{1,0:T(8,128)(2,1)}, bf16[256,512]{1,0:T(8,128)(2,1)}, bf16[256,5...) custom-call(bf16[256,512]{1,0:T(8,128)(2,1)} %get-tuple-element.38.refs_0_, ...), custom_call_target="tpu_custom_call" | custom-call | tf_op jit(solution)/shard_map/publish/pallas_call | solution.py:1037

commit v7 on v6

--- a/solution.py
+++ b/solution.py
@@ -174,10 +174,12 @@
         self.add((1, 0), self.cut, 192 - self.cut, [8, 9])
         self.partner_rest().start()
 
-    def finish(self, out):
+    def finish_head(self, out):
         self.partner_head(0).wait_recv()
         self.wait_along(2)
         self.add((0, 0), 0, self.cut, [0, 11, 12], out)
+
+    def finish_rest(self, out):
         self.wait_along(0)
         self.partner_rest().wait_recv()
         self.add((0, 0), self.cut, 192 - self.cut, [5, 6, 13], out)
@@ -347,8 +349,10 @@
         act_ref[rows, :] = gelu_tanh(pre).astype(bf)
         full[0, 0, rows, :] = (act_grad_ref[rows, :] * gelu_slope(pre)).astype(bf)
 
-    summing.finish(activate)
-    gathering.send_own()
+    summing.finish_head(activate)
+    gathering.start(0, 1, 12)
+    summing.finish_rest(activate)
+    gathering.start(16, 4, 5)
 
     def row_grads(dy, dz):
         expert, _ = chunk_of(dy, dz)
@@ -419,9 +423,13 @@
     )(x_rows, act_grad, w_in)
 
 
+def turn(row):
+    return jnp.transpose(jnp.broadcast_to(row, (128, 256)))
+
+
 def forward_kernel(
     q_ref, k_ref, v_ref, res_ref, lengths_ref, routes_ref, gates_ref, og_ref, w_out_hbm,
-    rows_ref, qend_row_ref, attn_ref, lse_ref, mixed_ref, inv_ref, xrecv_ref, grecv_ref, act_grad_ref, kv_out_ref,
+    rows_ref, rows_col_ref, qend_row_ref, attn_ref, lse_ref, mixed_ref, inv_ref, xrecv_ref, grecv_ref, act_grad_ref, kv_out_ref,
     kv, m_s, l_s, acc_s, gsend, xsend, part, sums, sq_send, sq_recv, gated, qend_s, w_out_ref,
     w_sem,
     kv_send_sem, kv_recv_sem, out_sem, g_send_sem, g_recv_sem, x_send_sem, x_recv_sem,
@@ -458,21 +466,24 @@
     sibling, partner = device(0, 0, 1), device(1, 0, 0)
     for which in range(2):
         move(own(which), (1, 0, 0, which), partner)
+        move(own(which), (0, 3, 0, which), right)
+        move(own(which), (0, 1, 0, which), left)
     for which in range(2):
         move(own(which), (0, 0, 1, which), sibling)
     early = lax.broadcasted_iota(jnp.int32, (256, 256), 0) < lax.broadcasted_iota(
         jnp.int32, (256, 256), 1
     )
-    experts = [routes_ref[:, a : a + 1].astype(jnp.float32) for a in range(2)]
+    experts = [routes_ref[a : a + 1, :].astype(jnp.float32) for a in range(2)]
     for a in range(2):
-        expert_row = jnp.transpose(jnp.broadcast_to(experts[a], (256, 128)))[0:8]
         rank = jnp.zeros((1, 256), jnp.float32)
         for b in range(2):
-            same = early & (experts[b] == expert_row[0:1])
+            same = early & (turn(experts[b])[:, 0:1] == experts[a])
             rank += jnp.sum(jnp.where(same, 1.0, 0.0), axis=0, keepdims=True)
         cols = slice(a * 256, a * 256 + 256)
-        rows_ref[:, cols] = (expert_row * 48 + rank).astype(jnp.int32)
-        gate = gates_ref[:, a : a + 1]
+        rows = experts[a] * 48 + rank
+        rows_ref[:, cols] = jnp.broadcast_to(rows, (8, 256)).astype(jnp.int32)
+        rows_col_ref[:, a * 128 : a * 128 + 128] = turn(rows).astype(jnp.int32)
+        gate = turn(gates_ref[a : a + 1, :])[:, 0:1]
         gated[cols, :] = (gate * og_ref[...].astype(jnp.float32)).astype(jnp.bfloat16)
 
     @pl.loop(0, 16)
@@ -486,9 +497,6 @@
                 gsend.at[k], grecv_ref.at[me], g_send_sem.at[k], g_recv_sem.at[k], {"ctx": there}
             ).start()
 
-    for which in range(2):
-        move(own(which), (0, 3, 0, which), right)
-        move(own(which), (0, 1, 0, which), left)
     grecv_ref[me] = gsend[0]
     kv[0, 0, 0, 0] = k_ref[...]
     kv[0, 0, 0, 1] = v_ref[...]
@@ -665,7 +673,8 @@
     def keep(rows, total):
         act_grad_ref[rows, :] = total
 
-    summing.finish(keep)
+    summing.finish_head(keep)
+    summing.finish_rest(keep)
     summing.drain()
 
     @pl.loop(1, 16)
@@ -695,6 +704,7 @@
         forward_kernel,
         out_shape=(
             shape((8, 512), jnp.int32),
+            shape((256, 256), jnp.int32),
             shape((8, 256), jnp.int32),
             shape((256, 512), bf),
             shape((4, 8, 256), f32),
@@ -709,7 +719,7 @@
         + [pl.BlockSpec(memory_space=pltpu.SMEM)]
         + [vmem] * 3
         + [pl.BlockSpec(memory_space=pl.ANY)],
-        out_specs=[vmem] * 9 + [pl.BlockSpec(memory_space=pl.ANY)],
+        out_specs=[vmem] * 10 + [pl.BlockSpec(memory_space=pl.ANY)],
         scratch_shapes=[
             pltpu.VMEM((2, 4, 2, 2, 256, 512), bf),
             pltpu.VMEM((4, 256, 128), f32),
@@ -751,7 +761,7 @@
     q_ref, kv_hbm, lse_ref, attn_ref, qend_ref, og_ref, inv_ref, rows_ref, rg_ref, act_ref,
     w_out_hbm, g_hbm, mixed_ref, gates_ref,
     layer_ref, ig_ref, dq_ref, dk_ref, dv_ref, w_out_grad_ref,
-    full, eo_send, eo_recv, kv_ref, w_out_ref, g_ref, load_sem, normed_grad, returned, row_dot, dqt, own_terms, sib_send, sib_recv, ring_send,
+    full, eo_send, eo_recv, kv_ref, w_out_ref, g_ref, load_sem, normed_grad, row_dot, dqt, own_terms, sib_send, sib_recv, ring_send,
     ring_recv, part_send, part_recv,
     f_send_sem, f_recv_sem, r_send_sem, r_recv_sem, sib_send_sem, sib_recv_sem, ring_send_sem, ring_recv_sem,
     part_send_sem, part_recv_sem,
@@ -787,11 +797,10 @@
     w_load.start()
     g_load.start()
     dqt[...] = jnp.zeros_like(dqt)
-    normed_grad[...] = jnp.zeros_like(normed_grad)
-
-    @pl.loop(0, 16)
-    def _(k):
-        normed_grad[...] += dot_tn(pick_both(rows_ref, k), rg_ref[k])
+    row_id = lax.broadcasted_iota(jnp.int32, (256, 1536), 1)
+    hits = [row_id == rows_ref[:, a * 128 : a * 128 + 1] for a in range(2)]
+    pick = jnp.where(hits[0] | hits[1], 1.0, 0.0).astype(bf)
+    normed_grad[...] = dot_nn(pick, rg_ref[...].reshape(1536, 512))
 
     for h in range(4):
         cols = slice(h * 128, h * 128 + 128)
@@ -913,16 +922,16 @@
     send_ring(0, 2, 0, True)
     send_ring(0, 2, 1, True)
     terms(0, 0)
-    gathering.wait_chunk(1, 0)
-    expert_rows(1, 0)
+    for dy, dz in [(0, 1), (0, 3), (1, 0)]:
+        gathering.wait_chunk(dy, dz)
+        expert_rows(dy, dz)
     for h in range(4):
         dq_ref[:, h * 128 : h * 128 + 128] = jnp.transpose(dqt[h]).astype(bf)
     send_ring(0, 1, 0, True)
     send_ring(0, 3, 1, True)
-    for dz in (1, 3, 2):
-        for dy in range(2):
-            gathering.wait_chunk(dy, dz)
-            expert_rows(dy, dz)
+    for dy, dz in [(0, 2), (1, 1), (1, 3), (1, 2)]:
+        gathering.wait_chunk(dy, dz)
+        expert_rows(dy, dz)
     for which in range(2):
         sums = total_of(0, 0, which, True)
         part_copy(which).wait_recv()
@@ -954,18 +963,12 @@
             w_out_grad_ref[expert, cols, :] = total.astype(bf)
 
     wait_returns(eo_send, eo_recv, r_send_sem, r_recv_sem)
-    returned[...] = jnp.zeros_like(returned)
-
-    @pl.loop(0, 16)
-    def _(k):
-        returned[...] += dot_tn(pick_two(rows_ref, k), eo_recv[k].reshape(96, 512))
-
-    for h in range(4):
-        cols = slice(h * 128, h * 128 + 128)
-        sums = (
-            gates_ref[:, 0:1] * returned[0:256, cols] + gates_ref[:, 1:2] * returned[256:512, cols]
-        )
-        layer_ref[:, cols] = (mixed_ref[:, cols].astype(f32) + sums).astype(bf)
+    total = mixed_ref[...].astype(f32)
+    for a in range(2):
+        hit = row_id == rows_ref[:, a * 128 : a * 128 + 1]
+        picked = dot_nn(jnp.where(hit, 1.0, 0.0).astype(bf), eo_recv[...].reshape(1536, 512))
+        total = total + turn(gates_ref[a : a + 1, :])[:, 0:1] * picked
+    layer_ref[...] = total.astype(bf)
 
     gathering.drain()
 
@@ -989,7 +992,6 @@
             pltpu.VMEM((16, 96, 512), bf),
             pltpu.SemaphoreType.DMA((10,)),
             pltpu.VMEM((256, 512), f32),
-            pltpu.VMEM((512, 512), f32),
             pltpu.VMEM((4, 8, 256), f32),
             pltpu.VMEM((4, 128, 256), f32),
             pltpu.VMEM((2, 4, 2, 256, 512), bf),
@@ -1052,15 +1054,15 @@
     n_ctx = lax.axis_size("ctx")
     tok_rows, feat_dev = residual.shape
     exp_dev = w_in.shape[0]
-    rows_wide, qend_row, attn, lse, mixed, inv_wide, rows_recv, grads_recv, act_grad, kv_all = (
+    rows_wide, rows_col, qend_row, attn, lse, mixed, inv_wide, rows_recv, grads_recv, act_grad, kv_all = (
         forward_call(
             queries,
             keys,
             values,
             residual,
             frame_lengths,
-            routes,
-            route_gates,
+            routes.T,
+            route_gates.T,
             out_grad,
             w_out,
         )
@@ -1074,13 +1076,13 @@
         qend_row,
         out_grad,
         inv_wide,
-        rows_wide,
+        rows_col,
         row_grad.reshape(n_ctx, exp_dev * row_grad.shape[2], feat_dev),
         activated,
         w_out,
         grads_recv,
         mixed,
-        route_gates,
+        route_gates.T,
     )
     return publish(
         layer_out,

time: 308 us -> 294 us (0.955)
  Pallas kernels: 300 us -> 289 us
    pallas_call x1, Pallas kernels: 87.4 us -> 79.8 us  [backward_call(): pl.pallas_call(backward_kernel, out_shape=(shape((256, 512), bf),) * 5 +...]
where the time goes in v7:
time: 294 us; the launch traced here: 290 us
  Pallas kernels  289 us (98%)
    pallas_call x1, Pallas kernels, forward_call(): pl.pallas_call(forward_kernel, out_shape=(shape((8, 512), jnp.int32), sha...  111 us
    pallas_call x1, Pallas kernels, experts_call(): pl.pallas_call(experts_kernel, out_shape=(shape((192, 1536), bf), shape((...  93 us
    pallas_call x1, Pallas kernels, backward_call(): pl.pallas_call(backward_kernel, out_shape=(shape((256, 512), bf),) * 5 +...  79.8 us

profile of v7, /device:TPU:0, one launch (start us, length us, event | category | flops | bytes accessed | tf_op | source)
XLA Modules:
  0.0 289.9 jit_solution(1900938880508607482)
XLA Ops:
  0.6 110.7 %forward.1 = (s32[8,512]{1,0:T(8,128)}, s32[256,256]{1,0:T(8,128)}, s32[8,256]{1,0:T(8,128)}, bf16[256,512]{1,0:T(8,128)(2,1)}, f32[4,8,256]{2,1,0:T(8,128)}, /*...) custom-call(bf16[256,512]{1,0:T(8,128)(2,1)} %q_ref.3, ...), custom_call_target="tpu_custom_call" | custom-call | tf_op jit(solution)/shard_map/forward/pallas_call | solution.py:703
  111.3 93.0 %experts.1 = (bf16[192,1536]{1,0:T(8,128)(2,1)}, bf16[16,2,48,512]{3,2,1,0:T(8,128)(2,1)}, bf16[2,512,1536]{2,1,0:T(8,128)(2,1)}) custom-call(bf16[16,96,512]{2,1,0:T(8,128)(2,1)} %get-tuple-element.32.x_ref, f32[192,1536]{1,0:T(8,128)} %get-tuple-element.33.act_grad_ref, bf16[2,512,1536]{2,1,0:T(8,128)(2,1)} %w_in_hbm.1), custom_call_target="tpu_custom_call" | custom-call | tf_op jit(solution)/shard_map/experts/pallas_call | solution.py:396
  204.3 79.8 %backward.1 = (bf16[256,512]{1,0:T(8,128)(2,1)}, bf16[256,512]{1,0:T(8,128)(2,1)}, bf16[256,512]{1,0:T(8,128)(2,1)}, bf16[256,512]{1,0:T(8,128)(2,1)}, bf16[256,...) custom-call(bf16[256,512]{1,0:T(8,128)(2,1)} %q_ref.3, bf16[2,4,2,2,256,512]{5,4,3,2,1,0:T(8,128)(2,1)} %get-tuple-element.26.kv_hbm, ...), custom_call_target="tpu_custom_call" | custom-call | tf_op jit(solution)/shard_map/backward/pallas_call | solution.py:981
  284.2 5.6 %publish.1 = (bf16[256,512]{1,0:T(8,128)(2,1)}, bf16[256,512]{1,0:T(8,128)(2,1)}, bf16[256,512]{1,0:T(8,128)(2,1)}, bf16[256,512]{1,0:T(8,128)(2,1)}, bf16[256,5...) custom-call(bf16[256,512]{1,0:T(8,128)(2,1)} %get-tuple-element.38.refs_0_, ...), custom_call_target="tpu_custom_call" | custom-call | tf_op jit(solution)/shard_map/publish/pallas_call | solution.py:1039

commit v8 on v7

--- a/solution.py
+++ b/solution.py
@@ -327,7 +327,7 @@
     greet()
     w_copy.wait()
     summing = GrpSum(96, part, sums, s_send_sem, s_recv_sem)
-    gathering = GrpGather(96, full, f_send_sem, f_recv_sem)
+    gathering = GrpGather(64, full, f_send_sem, f_recv_sem)
     for dy, dz in CHUNK_ORDER:
         expert, _ = chunk_of(dy, dz)
         rows = chunk_rows(x_ref, dy, dz)
@@ -340,10 +340,11 @@
         summing.send_first(dy, dz)
     summing.relay(1)
     summing.relay(0)
-    for dz in (2, 1, 3):
+    for dz in (2, 1):
         summing.second(dz)
+    summing.second_rest()
+    summing.second(3)
     summing.relay(2)
-    summing.second_rest()
 
     def activate(rows, pre):
         act_ref[rows, :] = gelu_tanh(pre).astype(bf)
@@ -464,12 +465,6 @@
 
     right, left = device(0, 1, 0), device(0, 3, 0)
     sibling, partner = device(0, 0, 1), device(1, 0, 0)
-    for which in range(2):
-        move(own(which), (1, 0, 0, which), partner)
-        move(own(which), (0, 3, 0, which), right)
-        move(own(which), (0, 1, 0, which), left)
-    for which in range(2):
-        move(own(which), (0, 0, 1, which), sibling)
     early = lax.broadcasted_iota(jnp.int32, (256, 256), 0) < lax.broadcasted_iota(
         jnp.int32, (256, 256), 1
     )
@@ -497,6 +492,12 @@
                 gsend.at[k], grecv_ref.at[me], g_send_sem.at[k], g_recv_sem.at[k], {"ctx": there}
             ).start()
 
+    for which in range(2):
+        move(own(which), (0, 0, 1, which), sibling)
+    for which in range(2):
+        move(own(which), (1, 0, 0, which), partner)
+        move(own(which), (0, 3, 0, which), right)
+        move(own(which), (0, 1, 0, which), left)
     grecv_ref[me] = gsend[0]
     kv[0, 0, 0, 0] = k_ref[...]
     kv[0, 0, 0, 1] = v_ref[...]
@@ -564,13 +565,6 @@
             acc_s[h] = acc
 
     attend(0, 0)
-    for which in range(2):
-        wait_slot(1, 0, 0, which)
-        move(kv.at[1, 0, 0, which], (1, 3, 0, which), right)
-        move(kv.at[1, 0, 0, which], (1, 1, 0, which), left)
-        move(kv.at[1, 0, 0, which], (1, 0, 1, which), sibling)
-
-    relay(0)
 
     @pl.loop(1, 16)
     def _(k):
@@ -591,6 +585,12 @@
 
         summing.send_first(dy, dz)
 
+    for which in range(2):
+        wait_slot(1, 0, 0, which)
+        move(kv.at[1, 0, 0, which], (1, 3, 0, which), right)
+        move(kv.at[1, 0, 0, which], (1, 1, 0, which), left)
+        move(kv.at[1, 0, 0, which], (1, 0, 1, which), sibling)
+    relay(0)
     attend(0, 3)
     attend(0, 1)
     relay(1)
@@ -898,20 +898,20 @@
     send_ring(1, 1, 1, False)
     terms(1, 2)
     terms(1, 0)
+    send_ring(1, 2, 0, True)
+    send_ring(1, 2, 1, True)
     w_load.wait()
     gathering.relay(0)
     for dz in (3, 1):
         gathering.pass_head(dz)
     gathering.pass_rest()
     gathering.relay(1)
-    send_ring(1, 2, 0, True)
-    send_ring(1, 2, 1, True)
     expert_rows(0, 0)
     terms(0, 3)
-    terms(0, 1)
     send_ring(1, 1, 0, True)
     send_ring(1, 3, 1, True)
     send_ring(0, 3, 0, False)
+    terms(0, 1)
     send_ring(0, 1, 1, False)
     gathering.pass_head(2)
     gathering.relay(2)
@@ -922,13 +922,13 @@
     send_ring(0, 2, 0, True)
     send_ring(0, 2, 1, True)
     terms(0, 0)
+    send_ring(0, 1, 0, True)
+    send_ring(0, 3, 1, True)
     for dy, dz in [(0, 1), (0, 3), (1, 0)]:
         gathering.wait_chunk(dy, dz)
         expert_rows(dy, dz)
     for h in range(4):
         dq_ref[:, h * 128 : h * 128 + 128] = jnp.transpose(dqt[h]).astype(bf)
-    send_ring(0, 1, 0, True)
-    send_ring(0, 3, 1, True)
     for dy, dz in [(0, 2), (1, 1), (1, 3), (1, 2)]:
         gathering.wait_chunk(dy, dz)
         expert_rows(dy, dz)

time: 294 us -> 287 us (0.976)
  Pallas kernels: 289 us -> 284 us
    pallas_call x1, Pallas kernels: 93 us -> 87.9 us  [experts_call(): pl.pallas_call(experts_kernel, out_shape=(shape((192, 1536), bf), shape((...]
where the time goes in v8:
time: 287 us; the launch traced here: 285 us
  Pallas kernels  284 us (99%)
    pallas_call x1, Pallas kernels, forward_call(): pl.pallas_call(forward_kernel, out_shape=(shape((8, 512), jnp.int32), sha...  112 us
    pallas_call x1, Pallas kernels, experts_call(): pl.pallas_call(experts_kernel, out_shape=(shape((192, 1536), bf), shape((...  87.9 us
    pallas_call x1, Pallas kernels, backward_call(): pl.pallas_call(backward_kernel, out_shape=(shape((256, 512), bf),) * 5 +...  79 us

profile of v8, /device:TPU:0, one launch (start us, length us, event | category | flops | bytes accessed | tf_op | source)
XLA Modules:
  0.0 285.1 jit_solution(6225517490924141632)
XLA Ops:
  0.6 111.8 %forward.1 = (s32[8,512]{1,0:T(8,128)}, s32[256,256]{1,0:T(8,128)}, s32[8,256]{1,0:T(8,128)}, bf16[256,512]{1,0:T(8,128)(2,1)}, f32[4,8,256]{2,1,0:T(8,128)}, /*...) custom-call(bf16[256,512]{1,0:T(8,128)(2,1)} %q_ref.3, ...), custom_call_target="tpu_custom_call" | custom-call | tf_op jit(solution)/shard_map/forward/pallas_call | solution.py:703
  112.4 87.9 %experts.1 = (bf16[192,1536]{1,0:T(8,128)(2,1)}, bf16[16,2,48,512]{3,2,1,0:T(8,128)(2,1)}, bf16[2,512,1536]{2,1,0:T(8,128)(2,1)}) custom-call(bf16[16,96,512]{2,1,0:T(8,128)(2,1)} %get-tuple-element.32.x_ref, f32[192,1536]{1,0:T(8,128)} %get-tuple-element.33.act_grad_ref, bf16[2,512,1536]{2,1,0:T(8,128)(2,1)} %w_in_hbm.1), custom_call_target="tpu_custom_call" | custom-call | tf_op jit(solution)/shard_map/experts/pallas_call | solution.py:397
  200.3 79.0 %backward.1 = (bf16[256,512]{1,0:T(8,128)(2,1)}, bf16[256,512]{1,0:T(8,128)(2,1)}, bf16[256,512]{1,0:T(8,128)(2,1)}, bf16[256,512]{1,0:T(8,128)(2,1)}, bf16[256,...) custom-call(bf16[256,512]{1,0:T(8,128)(2,1)} %q_ref.3, bf16[2,4,2,2,256,512]{5,4,3,2,1,0:T(8,128)(2,1)} %get-tuple-element.26.kv_hbm, ...), custom_call_target="tpu_custom_call" | custom-call | tf_op jit(solution)/shard_map/backward/pallas_call | solution.py:981
  279.3 5.6 %publish.1 = (bf16[256,512]{1,0:T(8,128)(2,1)}, bf16[256,512]{1,0:T(8,128)(2,1)}, bf16[256,512]{1,0:T(8,128)(2,1)}, bf16[256,512]{1,0:T(8,128)(2,1)}, bf16[256,5...) custom-call(bf16[256,512]{1,0:T(8,128)(2,1)} %get-tuple-element.38.refs_0_, ...), custom_call_target="tpu_custom_call" | custom-call | tf_op jit(solution)/shard_map/publish/pallas_call | solution.py:1039

commit v9 on v8

--- a/solution.py
+++ b/solution.py
@@ -318,7 +318,7 @@
 def experts_kernel(
     x_ref, act_grad_ref, w_in_hbm,
     act_ref, rg_ref, w_in_grad_ref,
-    part, sums, full, rg_send, w_in_ref, w_sem,
+    part, sums, full, rg_send, w_in_ref, w_in_grad_s, w_sem, out_sem,
     s_send_sem, s_recv_sem, f_send_sem, f_recv_sem, r_send_sem, r_recv_sem,
 ):
     bf = jnp.bfloat16
@@ -371,10 +371,7 @@
         gathering.wait_chunk(dy, dz)
         row_grads(dy, dz)
     gathering.relay(2)
-    for dy, dz in [(1, 0), (1, 1), (1, 3), (0, 2), (1, 2)]:
-        gathering.wait_chunk(dy, dz)
-        row_grads(dy, dz)
-    for dy in range(2):
+    def weight_grads(dy):
         expert, _ = chunk_of(dy, 0)
 
         @pl.loop(0, 3)
@@ -383,11 +380,26 @@
             total = dot_tn(chunk_rows(x_ref, dy, 0), full[dy, 0, :, cols])
             for dz in range(1, 4):
                 total += dot_tn(chunk_rows(x_ref, dy, dz), full[dy, dz, :, cols])
-            w_in_grad_ref[expert, :, cols] = total.astype(bf)
-
+            w_in_grad_s[expert, :, cols] = total.astype(bf)
+
+        out = pltpu.make_async_copy(
+            w_in_grad_s.at[expert], w_in_grad_ref.at[expert], out_sem.at[dy]
+        )
+        out.start()
+        return out
+
+    for dy, dz in [(1, 0), (0, 2), (1, 1), (1, 3)]:
+        gathering.wait_chunk(dy, dz)
+        row_grads(dy, dz)
+    outs = [weight_grads(0)]
+    gathering.wait_chunk(1, 2)
+    row_grads(1, 2)
+    outs.append(weight_grads(1))
     wait_returns(rg_send, rg_ref, r_send_sem, r_recv_sem)
     summing.drain()
     gathering.drain()
+    for out in outs:
+        out.wait()
 
 
 def experts_call(x_rows, act_grad, w_in):
@@ -402,14 +414,16 @@
             shape((2, 512, 1536), bf),
         ),
         in_specs=[vmem] * 2 + [pl.BlockSpec(memory_space=pl.ANY)],
-        out_specs=(vmem,) * 3,
+        out_specs=(vmem, vmem, pl.BlockSpec(memory_space=pl.ANY)),
         scratch_shapes=[
             pltpu.VMEM((2, 4, 192, 1536), bf),
             pltpu.VMEM((14, 192, 1536), bf),
             pltpu.VMEM((2, 4, 192, 1536), bf),
             pltpu.VMEM((2, 16, 48, 512), bf),
             pltpu.VMEM((2, 512, 1536), bf),
+            pltpu.VMEM((2, 512, 1536), bf),
             pltpu.SemaphoreType.DMA,
+            pltpu.SemaphoreType.DMA((2,)),
             pltpu.SemaphoreType.DMA((23,)),
             pltpu.SemaphoreType.DMA((23,)),
             pltpu.SemaphoreType.DMA((17,)),
@@ -761,7 +775,7 @@
     q_ref, kv_hbm, lse_ref, attn_ref, qend_ref, og_ref, inv_ref, rows_ref, rg_ref, act_ref,
     w_out_hbm, g_hbm, mixed_ref, gates_ref,
     layer_ref, ig_ref, dq_ref, dk_ref, dv_ref, w_out_grad_ref,
-    full, eo_send, eo_recv, kv_ref, w_out_ref, g_ref, load_sem, normed_grad, row_dot, dqt, own_terms, sib_send, sib_recv, ring_send,
+    full, eo_send, eo_recv, kv_ref, w_out_ref, g_ref, w_out_grad_s, load_sem, normed_grad, row_dot, dqt, own_terms, sib_send, sib_recv, ring_send,
     ring_recv, part_send, part_recv,
     f_send_sem, f_recv_sem, r_send_sem, r_recv_sem, sib_send_sem, sib_recv_sem, ring_send_sem, ring_recv_sem,
     part_send_sem, part_recv_sem,
@@ -929,9 +943,30 @@
         expert_rows(dy, dz)
     for h in range(4):
         dq_ref[:, h * 128 : h * 128 + 128] = jnp.transpose(dqt[h]).astype(bf)
-    for dy, dz in [(0, 2), (1, 1), (1, 3), (1, 2)]:
+    def weight_grads(dy):
+        expert, _ = chunk_of(dy, 0)
+
+        @pl.loop(0, 3)
+        def _(piece):
+            cols = pl.ds(pl.multiple_of(piece * 512, 512), 512)
+            total = dot_tn(full[dy, 0, :, cols], chunk_rows(g_ref, dy, 0))
+            for dz in range(1, 4):
+                total += dot_tn(full[dy, dz, :, cols], chunk_rows(g_ref, dy, dz))
+            w_out_grad_s[expert, cols, :] = total.astype(bf)
+
+        out = pltpu.make_async_copy(
+            w_out_grad_s.at[expert], w_out_grad_ref.at[expert], load_sem.at[10 + dy]
+        )
+        out.start()
+        return out
+
+    g_load.wait()
+    for dy, dz in [(0, 2), (1, 1), (1, 3)]:
         gathering.wait_chunk(dy, dz)
         expert_rows(dy, dz)
+    w_outs = [weight_grads(0)]
+    gathering.wait_chunk(1, 2)
+    expert_rows(1, 2)
     for which in range(2):
         sums = total_of(0, 0, which, True)
         part_copy(which).wait_recv()
@@ -950,18 +985,7 @@
     for which in range(2):
         part_copy(which).wait_send()
 
-    g_load.wait()
-    for dy in range(2):
-        expert, _ = chunk_of(dy, 0)
-
-        @pl.loop(0, 3)
-        def _(piece):
-            cols = pl.ds(pl.multiple_of(piece * 512, 512), 512)
-            total = dot_tn(full[dy, 0, :, cols], chunk_rows(g_ref, dy, 0))
-            for dz in range(1, 4):
-                total += dot_tn(full[dy, dz, :, cols], chunk_rows(g_ref, dy, dz))
-            w_out_grad_ref[expert, cols, :] = total.astype(bf)
-
+    w_outs.append(weight_grads(1))
     wait_returns(eo_send, eo_recv, r_send_sem, r_recv_sem)
     total = mixed_ref[...].astype(f32)
     for a in range(2):
@@ -971,6 +995,8 @@
     layer_ref[...] = total.astype(bf)
 
     gathering.drain()
+    for out in w_outs:
+        out.wait()
 
 
 def backward_call(*operands):
@@ -982,7 +1008,7 @@
         backward_kernel,
         out_shape=(shape((256, 512), bf),) * 5 + (shape((2, 1536, 512), bf),),
         in_specs=[vmem, anywhere] + [vmem] * 8 + [anywhere] * 2 + [vmem] * 2,
-        out_specs=(vmem,) * 6,
+        out_specs=(vmem,) * 5 + (anywhere,),
         scratch_shapes=[
             pltpu.VMEM((2, 4, 192, 1536), bf),
             pltpu.VMEM((2, 16, 48, 512), bf),
@@ -990,7 +1016,8 @@
             pltpu.VMEM((2, 4, 2, 2, 256, 512), bf),
             pltpu.VMEM((2, 1536, 512), bf),
             pltpu.VMEM((16, 96, 512), bf),
-            pltpu.SemaphoreType.DMA((10,)),
+            pltpu.VMEM((2, 1536, 512), bf),
+            pltpu.SemaphoreType.DMA((12,)),
             pltpu.VMEM((256, 512), f32),
             pltpu.VMEM((4, 8, 256), f32),
             pltpu.VMEM((4, 128, 256), f32),

time: 287 us -> 285 us (level)
  no operation moved by 1% of the time
where the time goes in v9:
time: 285 us; the launch traced here: 283 us
  Pallas kernels  282 us (99%)
    pallas_call x1, Pallas kernels, forward_call(): pl.pallas_call(forward_kernel, out_shape=(shape((8, 512), jnp.int32), sha...  112 us
    pallas_call x1, Pallas kernels, experts_call(): pl.pallas_call(experts_kernel, out_shape=(shape((192, 1536), bf), shape((...  86.5 us
    pallas_call x1, Pallas kernels, backward_call(): pl.pallas_call(backward_kernel, out_shape=(shape((256, 512), bf),) * 5 +...  78.3 us

profile of v9, /device:TPU:0, one launch (start us, length us, event | category | flops | bytes accessed | tf_op | source)
XLA Modules:
  0.0 283.0 jit_solution(18102003229579733061)
XLA Ops:
  0.6 111.8 %forward.1 = (s32[8,512]{1,0:T(8,128)}, s32[256,256]{1,0:T(8,128)}, s32[8,256]{1,0:T(8,128)}, bf16[256,512]{1,0:T(8,128)(2,1)}, f32[4,8,256]{2,1,0:T(8,128)}, /*...) custom-call(bf16[256,512]{1,0:T(8,128)(2,1)} %q_ref.3, ...), custom_call_target="tpu_custom_call" | custom-call | tf_op jit(solution)/shard_map/forward/pallas_call | solution.py:717
  112.4 86.5 %experts.1 = (bf16[192,1536]{1,0:T(8,128)(2,1)}, bf16[16,2,48,512]{3,2,1,0:T(8,128)(2,1)}, bf16[2,512,1536]{2,1,0:T(8,128)(2,1)}) custom-call(bf16[16,96,512]{2,1,0:T(8,128)(2,1)} %get-tuple-element.32.x_ref, f32[192,1536]{1,0:T(8,128)} %get-tuple-element.33.act_grad_ref, bf16[2,512,1536]{2,1,0:T(8,128)(2,1)} %w_in_hbm.1), custom_call_target="tpu_custom_call" | custom-call | tf_op jit(solution)/shard_map/experts/pallas_call | solution.py:409
  198.9 78.3 %backward.1 = (bf16[256,512]{1,0:T(8,128)(2,1)}, bf16[256,512]{1,0:T(8,128)(2,1)}, bf16[256,512]{1,0:T(8,128)(2,1)}, bf16[256,512]{1,0:T(8,128)(2,1)}, bf16[256,...) custom-call(bf16[256,512]{1,0:T(8,128)(2,1)} %q_ref.3, bf16[2,4,2,2,256,512]{5,4,3,2,1,0:T(8,128)(2,1)} %get-tuple-element.26.kv_hbm, ...), custom_call_target="tpu_custom_call" | custom-call | tf_op jit(solution)/shard_map/backward/pallas_call | solution.py:1007
  277.2 5.6 %publish.1 = (bf16[256,512]{1,0:T(8,128)(2,1)}, bf16[256,512]{1,0:T(8,128)(2,1)}, bf16[256,512]{1,0:T(8,128)(2,1)}, bf16[256,512]{1,0:T(8,128)(2,1)}, bf16[256,5...) custom-call(bf16[256,512]{1,0:T(8,128)(2,1)} %get-tuple-element.38.refs_0_, ...), custom_call_target="tpu_custom_call" | custom-call | tf_op jit(solution)/shard_map/publish/pallas_call | solution.py:1066

commit v10 on v9

--- a/solution.py
+++ b/solution.py
@@ -496,7 +496,8 @@
         gated[cols, :] = (gate * og_ref[...].astype(jnp.float32)).astype(jnp.bfloat16)
 
     @pl.loop(0, 16)
-    def _(k):
+    def _(step):
+        k = lax.rem(step + 4, 16)
         there = lax.rem(me + k, 16)
         gsend[k] = dot_nn(pick_two(rows_ref, there), gated[...]).astype(jnp.bfloat16)
 
@@ -670,7 +671,8 @@
     )
 
     @pl.loop(0, 16)
-    def _(k):
+    def _(step):
+        k = lax.rem(step + 4, 16)
         there = lax.rem(me + k, 16)
         xsend[k] = dot_nn(pick_both(rows_ref, there), normed).astype(jnp.bfloat16)
 

time: 285 us -> 281 us (0.986)
  Pallas kernels: 282 us -> 279 us
    pallas_call x1, Pallas kernels: 112 us -> 108 us  [forward_call(): pl.pallas_call(forward_kernel, out_shape=(shape((8, 512), jnp.int32), sha...]
where the time goes in v10:
time: 281 us; the launch traced here: 279 us
  Pallas kernels  279 us (99%)
    pallas_call x1, Pallas kernels, forward_call(): pl.pallas_call(forward_kernel, out_shape=(shape((8, 512), jnp.int32), sha...  108 us
    pallas_call x1, Pallas kernels, experts_call(): pl.pallas_call(experts_kernel, out_shape=(shape((192, 1536), bf), shape((...  86.9 us
    pallas_call x1, Pallas kernels, backward_call(): pl.pallas_call(backward_kernel, out_shape=(shape((256, 512), bf),) * 5 +...  77.6 us

profile of v10, /device:TPU:0, one launch (start us, length us, event | category | flops | bytes accessed | tf_op | source)
XLA Modules:
  0.0 279.4 jit_solution(2476013809310733748)
XLA Ops:
  0.6 108.4 %forward.1 = (s32[8,512]{1,0:T(8,128)}, s32[256,256]{1,0:T(8,128)}, s32[8,256]{1,0:T(8,128)}, bf16[256,512]{1,0:T(8,128)(2,1)}, f32[4,8,256]{2,1,0:T(8,128)}, /*...) custom-call(bf16[256,512]{1,0:T(8,128)(2,1)} %q_ref.3, ...), custom_call_target="tpu_custom_call" | custom-call | tf_op jit(solution)/shard_map/forward/pallas_call | solution.py:719
  109.1 86.9 %experts.1 = (bf16[192,1536]{1,0:T(8,128)(2,1)}, bf16[16,2,48,512]{3,2,1,0:T(8,128)(2,1)}, bf16[2,512,1536]{2,1,0:T(8,128)(2,1)}) custom-call(bf16[16,96,512]{2,1,0:T(8,128)(2,1)} %get-tuple-element.32.x_ref, f32[192,1536]{1,0:T(8,128)} %get-tuple-element.33.act_grad_ref, bf16[2,512,1536]{2,1,0:T(8,128)(2,1)} %w_in_hbm.1), custom_call_target="tpu_custom_call" | custom-call | tf_op jit(solution)/shard_map/experts/pallas_call | solution.py:409
  196.0 77.6 %backward.1 = (bf16[256,512]{1,0:T(8,128)(2,1)}, bf16[256,512]{1,0:T(8,128)(2,1)}, bf16[256,512]{1,0:T(8,128)(2,1)}, bf16[256,512]{1,0:T(8,128)(2,1)}, bf16[256,...) custom-call(bf16[256,512]{1,0:T(8,128)(2,1)} %q_ref.3, bf16[2,4,2,2,256,512]{5,4,3,2,1,0:T(8,128)(2,1)} %get-tuple-element.26.kv_hbm, ...), custom_call_target="tpu_custom_call" | custom-call | tf_op jit(solution)/shard_map/backward/pallas_call | solution.py:1009
  273.6 5.6 %publish.1 = (bf16[256,512]{1,0:T(8,128)(2,1)}, bf16[256,512]{1,0:T(8,128)(2,1)}, bf16[256,512]{1,0:T(8,128)(2,1)}, bf16[256,512]{1,0:T(8,128)(2,1)}, bf16[256,5...) custom-call(bf16[256,512]{1,0:T(8,128)(2,1)} %get-tuple-element.38.refs_0_, ...), custom_call_target="tpu_custom_call" | custom-call | tf_op jit(solution)/shard_map/publish/pallas_call | solution.py:1068
